TPU v7x, 32 devices: a whole 2x2x4 slice. The times are simulated.
32 devices in a mesh: fsdp: 16 (over z, x, core), seq: 2 (over y).
Axes of the slice: x: 2, y: 2, z: 4, core: 2. Of those that a mesh axis runs over, the one named last changes fastest.
Arguments:
- tokens: bfloat16 [4096, 1024], P(('fsdp', 'seq')), may hold values from -6 to 6
- norm_gain: bfloat16 [1024], P(('fsdp', 'seq')), may hold values from 0.5 to 2
- w_query: bfloat16 [1024, 2048], P(('fsdp', 'seq')), may hold values from -0.1875 to 0.1875
- key_projection_weight: bfloat16 [1024, 1024], P(('fsdp', 'seq')), may hold values from -0.1875 to 0.1875
- value_projection_weight: bfloat16 [1024, 1024], P(('fsdp', 'seq')), may hold values from -0.1875 to 0.1875
- w_output: bfloat16 [2048, 1024], P(('fsdp', 'seq')), may hold values from -1 to 1
- query_gain: bfloat16 [128], P(('fsdp', 'seq')), may hold values from 0.5 to 1.5
- key_gain: bfloat16 [128], P(('fsdp', 'seq')), may hold values from 0.5 to 1.5
- mlp_gain: bfloat16 [1024], P(('fsdp', 'seq')), may hold values from 0.5 to 2
- w_gate: bfloat16 [1024, 3072], P(('fsdp', 'seq')), may hold values from -0.1875 to 0.1875
- w_up: bfloat16 [1024, 3072], P(('fsdp', 'seq')), may hold values from -0.1875 to 0.1875
- w_down: bfloat16 [3072, 1024], P(('fsdp', 'seq')), may hold values from -0.21875 to 0.21875
- lengths: int32 [16, 4], P('fsdp'), may hold values from 1 to 192, 256 in all within a row
- seq_order: int32 [16, 4], P('fsdp'), may hold values from 0 to 3, each once within a row
- cotangent: bfloat16 [4096, 1024], P(('fsdp', 'seq')), may hold values from -6 to 6
Outputs:
- result: bfloat16 [4096, 1024], P(('fsdp', 'seq'))
- grad_tokens: float32 [4096, 1024], P(('fsdp', 'seq'))
- grad_norm_gain: float32 [1024], P(('fsdp', 'seq'))
- grad_w_query: float32 [1024, 2048], P(('fsdp', 'seq'))
- grad_w_key: float32 [1024, 1024], P(('fsdp', 'seq'))
- grad_w_value: float32 [1024, 1024], P(('fsdp', 'seq'))
- grad_w_output: float32 [2048, 1024], P(('fsdp', 'seq'))
- grad_query_gain: float32 [128], P(('fsdp', 'seq'))
- key_gain_gradient: float32 [128], P(('fsdp', 'seq'))
- grad_mlp_gain: float32 [1024], P(('fsdp', 'seq'))
- grad_w_gate: float32 [1024, 3072], P(('fsdp', 'seq'))
- grad_w_up: float32 [1024, 3072], P(('fsdp', 'seq'))
- grad_w_down: float32 [3072, 1024], P(('fsdp', 'seq'))
Inputs may be any that keep to these rules, and one draw needn't show every extreme that they name: In each row the 4 lengths sum to 256, and the longest is exactly 192. Each row is a permutation of the 4 sequences of its group: seq_order[f, k] is the sequence placed k-th.
All inputs are finite; a program needn't handle non-finite values.
Results may differ from a plain program's by a relative error of at most 0.015.
Values may be sent and summed in bfloat16 or wider, within the bound.
No kernel may reach another device: no remote copies, remote signals or barrier semaphores. Data moves between devices by JAX's collectives and lax.ppermute only.
A program may use at most 192 MiB of HBM per device.

v0:
```python
import jax
import jax.numpy as jnp
from jax import lax
from jax.sharding import PartitionSpec as P

QUERY_HEADS = 16
KEY_VALUE_HEADS = 8
HEAD_SIZE = 128


EPS = 1e-06
THETA = 1000000.0


def from_behind(block, axis, distance):
    devices = range(lax.axis_size(axis))
    route = [(i - distance, i) for i in devices if i - distance in devices]
    return lax.ppermute(block, axis, route)


def rms_norm(values, gain_vec):
    return values * lax.rsqrt(jnp.mean(values * values, axis=-1, keepdims=True) + EPS) * gain_vec


def rotate(values, positions):
    half_width = values.shape[-1] // 2
    frequency = jnp.power(
        THETA, -jnp.arange(half_width, dtype=jnp.float32) * (2.0 / values.shape[-1])
    )
    angles = positions.astype(jnp.float32)[:, None] * frequency[None, :]
    cosine = jnp.cos(angles)[:, None, :]
    sine_part = jnp.sin(angles)[:, None, :]
    first_half = values[..., :half_width]
    second_half = values[..., half_width:]
    return jnp.concatenate(
        [
            first_half * cosine - second_half * sine_part,
            second_half * cosine + first_half * sine_part,
        ],
        axis=-1,
    )


def seq_bounds(lengths, seq_order):
    seq_count = lengths.shape[-1]
    picked = seq_order[..., :, None] == jnp.arange(seq_count, dtype=jnp.int32)
    packed = jnp.sum(jnp.where(picked, lengths[..., None, :], 0), axis=-1)
    seq_ends = jnp.cumsum(packed, axis=-1)
    return (seq_ends - packed, seq_ends)


def row_starts(row_ids, seq_starts, seq_ends):
    inside = (seq_starts[None, :] <= row_ids[:, None]) & (row_ids[:, None] < seq_ends[None, :])
    return jnp.sum(jnp.where(inside, seq_starts[None, :], 0), axis=1)


def gated_unit(gate_pre, upward):
    return gate_pre / (1.0 + jnp.exp(-gate_pre)) * upward


def local(
    tokens,
    norm_gain,
    w_query,
    key_projection_weight,
    value_projection_weight,
    w_output,
    query_gain,
    key_gain,
    mlp_gain,
    w_gate,
    w_up,
    w_down,
    lengths,
    seq_order,
    cotangent,
):
    current_rows = tokens.shape[0]
    sequence_groups = QUERY_HEADS // KEY_VALUE_HEADS
    score_scale = HEAD_SIZE ** (-0.5)
    device_seq = lax.axis_index("seq")
    seq_starts, seq_ends = seq_bounds(lengths[0], seq_order[0])
    row_ids = device_seq * current_rows + jnp.arange(current_rows, dtype=jnp.int32)
    first_rows = row_starts(row_ids, seq_starts, seq_ends)
    positions = row_ids - first_rows
    span_length = 2 * current_rows
    col_ids = (device_seq - 1) * current_rows + jnp.arange(span_length, dtype=jnp.int32)
    allowed = (col_ids[None, :] <= row_ids[:, None]) & (col_ids[None, :] >= first_rows[:, None])
    inputs = tokens.astype(jnp.float32)
    gain_first, query_full, key_full, value_full, output_full, query_norm, key_norm = (
        lax.all_gather(norm_gain, ("fsdp", "seq"), axis=0, tiled=True),
        lax.all_gather(w_query, ("fsdp", "seq"), axis=0, tiled=True),
        lax.all_gather(key_projection_weight, ("fsdp", "seq"), axis=0, tiled=True),
        lax.all_gather(value_projection_weight, ("fsdp", "seq"), axis=0, tiled=True),
        lax.all_gather(w_output, ("fsdp", "seq"), axis=0, tiled=True),
        lax.all_gather(query_gain, ("fsdp", "seq"), axis=0, tiled=True),
        lax.all_gather(key_gain, ("fsdp", "seq"), axis=0, tiled=True),
    )
    normalized_input = rms_norm(inputs, gain_first).astype(jnp.bfloat16)
    query_raw = jnp.dot(normalized_input, query_full, preferred_element_type=jnp.float32).reshape(
        current_rows, QUERY_HEADS, HEAD_SIZE
    )
    unnormed_key = jnp.dot(normalized_input, key_full, preferred_element_type=jnp.float32).reshape(
        current_rows, KEY_VALUE_HEADS, HEAD_SIZE
    )
    lower_value = jnp.dot(normalized_input, value_full, preferred_element_type=jnp.float32).astype(
        jnp.bfloat16
    )
    lower_query = rotate(rms_norm(query_raw, query_norm), positions).astype(jnp.bfloat16)
    key_low = (
        rotate(rms_norm(unnormed_key, key_norm), positions)
        .astype(jnp.bfloat16)
        .reshape(current_rows, KEY_VALUE_HEADS * HEAD_SIZE)
    )
    earlier_key, earlier_value = from_behind((key_low, lower_value), "seq", 1)
    key_span_rows = jnp.concatenate([earlier_key, key_low], axis=0)
    value_span_rows = jnp.concatenate([earlier_value, lower_value], axis=0)
    key_head_rows = key_span_rows.reshape(span_length, KEY_VALUE_HEADS, HEAD_SIZE).transpose(
        1, 0, 2
    )
    value_head_rows = value_span_rows.reshape(span_length, KEY_VALUE_HEADS, HEAD_SIZE).transpose(
        1, 0, 2
    )
    query_head_rows = lower_query.reshape(
        current_rows, KEY_VALUE_HEADS, sequence_groups, HEAD_SIZE
    ).transpose(1, 2, 0, 3)

    def scores_of(query_portion, key_part):
        scores = (
            jnp.einsum("gqd,kd->gqk", query_portion, key_part, preferred_element_type=jnp.float32)
            * score_scale
        )
        return jnp.where(allowed[None], scores, -1e30)

    def head_forward(operands):
        query_portion, key_part, value_part = operands
        scores = scores_of(query_portion, key_part)
        row_max = jnp.max(scores, axis=-1, keepdims=True)
        exp_scores = jnp.exp(scores - row_max)
        row_total = jnp.sum(exp_scores, axis=-1, keepdims=True)
        attn_probs = (exp_scores / row_total).astype(jnp.bfloat16)
        head_mix = jnp.einsum(
            "gqk,kd->gqd", attn_probs, value_part, preferred_element_type=jnp.float32
        )
        return (head_mix, row_max + jnp.log(row_total))

    head_out, log_total = lax.map(head_forward, (query_head_rows, key_head_rows, value_head_rows))
    attn_low = (
        head_out.transpose(2, 0, 1, 3)
        .reshape(current_rows, QUERY_HEADS * HEAD_SIZE)
        .astype(jnp.bfloat16)
    )
    hidden = inputs + jnp.dot(attn_low, output_full, preferred_element_type=jnp.float32)
    gain_second, gate_full, up_full, down_full = (
        lax.all_gather(mlp_gain, ("fsdp", "seq"), axis=0, tiled=True),
        lax.all_gather(w_gate, ("fsdp", "seq"), axis=0, tiled=True),
        lax.all_gather(w_up, ("fsdp", "seq"), axis=0, tiled=True),
        lax.all_gather(w_down, ("fsdp", "seq"), axis=0, tiled=True),
    )
    normed_mid = rms_norm(hidden, gain_second).astype(jnp.bfloat16)
    gate_pre = jnp.dot(normed_mid, gate_full, preferred_element_type=jnp.float32)
    upward = jnp.dot(normed_mid, up_full, preferred_element_type=jnp.float32)
    mixed_low = gated_unit(gate_pre, upward).astype(jnp.bfloat16)
    result = (hidden + jnp.dot(mixed_low, down_full, preferred_element_type=jnp.float32)).astype(
        jnp.bfloat16
    )
    grad_out = cotangent.astype(jnp.float32)
    gain_second, gate_full, up_full, down_full = (
        lax.all_gather(mlp_gain, ("fsdp", "seq"), axis=0, tiled=True),
        lax.all_gather(w_gate, ("fsdp", "seq"), axis=0, tiled=True),
        lax.all_gather(w_up, ("fsdp", "seq"), axis=0, tiled=True),
        lax.all_gather(w_down, ("fsdp", "seq"), axis=0, tiled=True),
    )
    grad_down_w = jnp.dot(mixed_low.T, cotangent, preferred_element_type=jnp.float32)
    grad_mixed = jnp.dot(cotangent, down_full.T, preferred_element_type=jnp.float32)
    unused_unit, unit_pull = jax.vjp(gated_unit, gate_pre, upward)
    grad_gate, grad_upward = unit_pull(grad_mixed)
    gate_grad_low = grad_gate.astype(jnp.bfloat16)
    up_grad_low = grad_upward.astype(jnp.bfloat16)
    grad_gate_w = jnp.dot(normed_mid.T, gate_grad_low, preferred_element_type=jnp.float32)
    grad_up_w = jnp.dot(normed_mid.T, up_grad_low, preferred_element_type=jnp.float32)
    grad_normed_mid = jnp.dot(
        gate_grad_low, gate_full.T, preferred_element_type=jnp.float32
    ) + jnp.dot(up_grad_low, up_full.T, preferred_element_type=jnp.float32)
    unused_mid, mid_pull = jax.vjp(rms_norm, hidden, gain_second.astype(jnp.float32))
    grad_hidden, grad_gain_second = mid_pull(grad_normed_mid)
    grad_hidden = grad_out + grad_hidden
    mlp_sums = (
        lax.psum_scatter(grad_gain_second, ("fsdp", "seq"), scatter_dimension=0, tiled=True),
        lax.psum_scatter(grad_gate_w, ("fsdp", "seq"), scatter_dimension=0, tiled=True),
        lax.psum_scatter(grad_up_w, ("fsdp", "seq"), scatter_dimension=0, tiled=True),
        lax.psum_scatter(grad_down_w, ("fsdp", "seq"), scatter_dimension=0, tiled=True),
    )
    gain_first, query_full, key_full, value_full, output_full, query_norm, key_norm = (
        lax.all_gather(norm_gain, ("fsdp", "seq"), axis=0, tiled=True),
        lax.all_gather(w_query, ("fsdp", "seq"), axis=0, tiled=True),
        lax.all_gather(key_projection_weight, ("fsdp", "seq"), axis=0, tiled=True),
        lax.all_gather(value_projection_weight, ("fsdp", "seq"), axis=0, tiled=True),
        lax.all_gather(w_output, ("fsdp", "seq"), axis=0, tiled=True),
        lax.all_gather(query_gain, ("fsdp", "seq"), axis=0, tiled=True),
        lax.all_gather(key_gain, ("fsdp", "seq"), axis=0, tiled=True),
    )
    grad_attn_out = grad_hidden.astype(jnp.bfloat16)
    grad_output_w = jnp.dot(attn_low.T, grad_attn_out, preferred_element_type=jnp.float32)
    attention_gradient = jnp.dot(
        grad_attn_out, output_full.T, preferred_element_type=jnp.float32
    ).astype(jnp.bfloat16)
    head_gradients = attention_gradient.reshape(
        current_rows, KEY_VALUE_HEADS, sequence_groups, HEAD_SIZE
    ).transpose(1, 2, 0, 3)

    def head_backward(operands):
        query_portion, key_part, value_part, grad_part, log_part = operands
        attn_probs = jnp.exp(scores_of(query_portion, key_part) - log_part)
        grad_probs = jnp.einsum(
            "gqd,kd->gqk", grad_part, value_part, preferred_element_type=jnp.float32
        )
        row_dot = jnp.sum(attn_probs * grad_probs, axis=-1, keepdims=True)
        grad_scores = (attn_probs * (grad_probs - row_dot)).astype(jnp.bfloat16)
        grad_query = (
            jnp.einsum("gqk,kd->gqd", grad_scores, key_part, preferred_element_type=jnp.float32)
            * score_scale
        )
        grad_key = (
            jnp.einsum(
                "gqk,gqd->kd", grad_scores, query_portion, preferred_element_type=jnp.float32
            )
            * score_scale
        )
        grad_value = jnp.einsum(
            "gqk,gqd->kd",
            attn_probs.astype(jnp.bfloat16),
            grad_part,
            preferred_element_type=jnp.float32,
        )
        return (grad_query, grad_key, grad_value)

    grad_query_h, key_head_gradient, value_head_gradient = lax.map(
        head_backward, (query_head_rows, key_head_rows, value_head_rows, head_gradients, log_total)
    )
    key_block_list = key_head_gradient.transpose(1, 0, 2).reshape(
        2, current_rows, KEY_VALUE_HEADS * HEAD_SIZE
    )
    value_block_list = value_head_gradient.transpose(1, 0, 2).reshape(
        2, current_rows, KEY_VALUE_HEADS * HEAD_SIZE
    )
    back_key, back_value = (
        from_behind(key_block_list[0].astype(jnp.bfloat16), "seq", -1).astype(jnp.float32),
        from_behind(value_block_list[0].astype(jnp.bfloat16), "seq", -1).astype(jnp.float32),
    )
    own_key_gradient = key_block_list[1] + back_key
    grad_value_own = value_block_list[1] + back_value

    def head_path(raw_heads, gain_vec):
        return rotate(rms_norm(raw_heads, gain_vec), positions)

    grad_query_rot = grad_query_h.transpose(2, 0, 1, 3).reshape(
        current_rows, QUERY_HEADS, HEAD_SIZE
    )
    unused_query, query_pull = jax.vjp(head_path, query_raw, query_norm.astype(jnp.float32))
    grad_query_raw, grad_query_gain = query_pull(grad_query_rot)
    unused_key, key_pullback = jax.vjp(head_path, unnormed_key, key_norm.astype(jnp.float32))
    raw_key_gradient, key_gain_gradient = key_pullback(
        own_key_gradient.reshape(current_rows, KEY_VALUE_HEADS, HEAD_SIZE)
    )
    query_grad_low = grad_query_raw.reshape(current_rows, QUERY_HEADS * HEAD_SIZE).astype(
        jnp.bfloat16
    )
    lower_key_gradient = raw_key_gradient.reshape(current_rows, KEY_VALUE_HEADS * HEAD_SIZE).astype(
        jnp.bfloat16
    )
    value_grad_low = grad_value_own.astype(jnp.bfloat16)
    grad_query_w = jnp.dot(normalized_input.T, query_grad_low, preferred_element_type=jnp.float32)
    grad_key_w = jnp.dot(normalized_input.T, lower_key_gradient, preferred_element_type=jnp.float32)
    grad_value_w = jnp.dot(normalized_input.T, value_grad_low, preferred_element_type=jnp.float32)
    grad_normed_in = (
        jnp.dot(query_grad_low, query_full.T, preferred_element_type=jnp.float32)
        + jnp.dot(lower_key_gradient, key_full.T, preferred_element_type=jnp.float32)
        + jnp.dot(value_grad_low, value_full.T, preferred_element_type=jnp.float32)
    )
    unused_first, first_pull = jax.vjp(rms_norm, inputs, gain_first.astype(jnp.float32))
    grad_inputs, grad_gain_first = first_pull(grad_normed_in)
    grad_tokens = grad_hidden + grad_inputs
    attn_sums = (
        lax.psum_scatter(grad_gain_first, ("fsdp", "seq"), scatter_dimension=0, tiled=True),
        lax.psum_scatter(grad_query_w, ("fsdp", "seq"), scatter_dimension=0, tiled=True),
        lax.psum_scatter(grad_key_w, ("fsdp", "seq"), scatter_dimension=0, tiled=True),
        lax.psum_scatter(grad_value_w, ("fsdp", "seq"), scatter_dimension=0, tiled=True),
        lax.psum_scatter(grad_output_w, ("fsdp", "seq"), scatter_dimension=0, tiled=True),
        lax.psum_scatter(grad_query_gain, ("fsdp", "seq"), scatter_dimension=0, tiled=True),
        lax.psum_scatter(key_gain_gradient, ("fsdp", "seq"), scatter_dimension=0, tiled=True),
    )
    return (result, grad_tokens) + tuple(attn_sums) + tuple(mlp_sums)


def solution(mesh):
    placed = (
        P(("fsdp", "seq"), None),
        P(("fsdp", "seq")),
        P(("fsdp", "seq"), None),
        P(("fsdp", "seq"), None),
        P(("fsdp", "seq"), None),
        P(("fsdp", "seq"), None),
        P(("fsdp", "seq")),
        P(("fsdp", "seq")),
        P(("fsdp", "seq")),
        P(("fsdp", "seq"), None),
        P(("fsdp", "seq"), None),
        P(("fsdp", "seq"), None),
        P("fsdp", None),
        P("fsdp", None),
        P(("fsdp", "seq"), None),
    )
    return jax.shard_map(
        local,
        mesh=mesh,
        in_specs=placed,
        out_specs=(
            P(("fsdp", "seq"), None),
            P(("fsdp", "seq"), None),
            P(("fsdp", "seq")),
            P(("fsdp", "seq"), None),
            P(("fsdp", "seq"), None),
            P(("fsdp", "seq"), None),
            P(("fsdp", "seq"), None),
            P(("fsdp", "seq")),
            P(("fsdp", "seq")),
            P(("fsdp", "seq")),
            P(("fsdp", "seq"), None),
            P(("fsdp", "seq"), None),
            P(("fsdp", "seq"), None),
        ),
        check_vma=False,
    )
```

profile of v0, /device:TPU:2, one launch (start us, length us, event | category | flops | bytes accessed | tf_op | source)
XLA Modules:
  0.0 1721.8 jit_solution(9926414602563906702)
XLA Ops:
  15.4 41.5 %all-reduce.13 = (bf16[128]{0:T(256)(128)(2,1)S(1)}, bf16[1024]{0:T(1024)(128)(2,1)S(1)}, bf16[128]{0:T(256)(128)(2,1)S(1)}, bf16[1024]{0:T(1024)(128)(2,1)S(1)}) all-reduce(bf16[128]{0:T(256)(128)(2,1)S(1)} %dynamic-update-slice.1, bf16[1024]{0:T(1024)(128)(2,1)S(1)} %dynamic-update-slice, ...), channel_id=1, replica_groups=mesh['fsdp'=16,'seq'=2] {'fsdp','seq'}, use_global_device_ids=true, to_apply=%add.5 | all-reduce | flops 2304 | bytes 9216
  61.7 7.1 all-gather.10.cloned.1.call-done
  75.0 52.3 %all-gather.12.cloned.1.call-done = bf16[1024,1024]{1,0:T(8,128)(2,1)} async-done(((bf16[32,1024]{1,0:T(8,128)(2,1)}), bf16[1024,1024]{1,0:T(8,128)(2,1)}) %all-gather.12.cloned.1.call-update) | async-done | bytes 2097168 | tf_op jit(solution)/shard_map/all_gather | solution.py:94
  133.4 4.5 collective-permute-done.1
  138.1 53.0 %all-gather.8.cloned.1.call-done = bf16[1024,2048]{1,0:T(8,128)(2,1)} async-done(((bf16[32,2048]{1,0:T(8,128)(2,1)}), bf16[1024,2048]{1,0:T(8,128)(2,1)}) %all-gather.8.cloned.1.call-update) | async-done | bytes 4194320 | tf_op jit(solution)/shard_map/all_gather | solution.py:92
  197.0 24.2 %while.28 = (s32[]{:T(128)}, bf16[8,2,128,128]{2,3,1,0:T(8,128)(2,1)S(1)}, f32[8,2,128,1]{2,1,3,0:T(2,128)}, bf16[8,2,128,128]{3,2,1,0:T(8,128)(2,1)}, bf16[8,25...) while((s32[]{:T(128)}, ...), condition=%wide.region_9.10_spmd.clone, body=%wide.region_6.9_spmd.clone.sunk | while | flops 34176768 | bytes 1192549 | solution.py:147
  221.2 33.2 %all-gather.14.cloned.1.call-done = bf16[2048,1024]{1,0:T(8,128)(2,1)} async-done(((bf16[64,1024]{1,0:T(8,128)(2,1)}), bf16[2048,1024]{1,0:T(8,128)(2,1)}) %all-gather.14.cloned.1.call-update) | async-done | bytes 4194320 | tf_op jit(solution)/shard_map/all_gather | solution.py:95
  257.6 67.9 %all-gather.16.cloned.1.call-done = bf16[1024,3072]{1,0:T(8,128)(2,1)} async-done(((bf16[32,3072]{1,0:T(8,128)(2,1)}), bf16[1024,3072]{1,0:T(8,128)(2,1)}) %all-gather.16.cloned.1.call-update) | async-done | bytes 6291472 | tf_op jit(solution)/shard_map/all_gather | solution.py:156
  325.5 4.9 fusion.81
  330.4 65.8 %all-gather.18.cloned.1.call-done = bf16[1024,3072]{1,0:T(8,128)(2,1)} async-done(((bf16[32,3072]{1,0:T(8,128)(2,1)}), bf16[1024,3072]{1,0:T(8,128)(2,1)}) %all-gather.18.cloned.1.call-update) | async-done | bytes 6291472 | tf_op jit(solution)/shard_map/all_gather | solution.py:157
  396.3 5.0 fusion.82
  401.2 66.0 %all-gather.20.cloned.1.call-done = bf16[3072,1024]{1,0:T(8,128)(2,1)} async-done(((bf16[96,1024]{1,0:T(8,128)(2,1)}), bf16[3072,1024]{1,0:T(8,128)(2,1)}) %all-gather.20.cloned.1.call-update) | async-done | bytes 6291472 | tf_op jit(solution)/shard_map/all_gather | solution.py:158
  467.2 7.3 multiply_convert_fusion.1
  474.5 5.6 fusion.83
  487.8 72.4 %while.29 = (s32[]{:T(128)}, f32[8,2,128,128]{3,2,1,0:T(8,128)}, f32[8,256,128]{1,2,0:T(8,128)}, f32[8,256,128]{1,2,0:T(8,128)}, bf16[8,2,128,128]{3,2,1,0:T(8,1...) while((s32[]{:T(128)}, f32[8,2,128,128]{3,2,1,0:T(8,128)}, ...), condition=%wide.region_14.15_spmd.clone, body=%wide.region_12.14_spmd.clone.sunk | while | flops 84639488 | bytes 3420289 | solution.py:238
  563.7 8.0 collective-permute-done.3
  572.4 3.5 fusion.71
  579.8 13.3 collective-permute-done.2
  605.3 4.6 fusion.58
  611.0 6.3 fusion.85
  618.4 6.3 fusion.86
  625.8 4.5 fusion.64
  631.5 6.4 fusion.87
  638.0 4.6 fusion.47
  648.5 41.1 %all-reduce.12 = (f32[1024]{0:T(1024)S(1)}, f32[128]{0:T(128)S(1)}, f32[128]{0:T(128)S(1)}, f32[1024]{0:T(1024)S(1)}) all-reduce(f32[1024]{0:T(1024)S(1)} %get-tuple-element.294, f32[128]{0:T(128)S(1)} %copy-done.48, f32[128]{0:T(128)S(1)} %copy-done.47, f32[1024]{0:T(1024)S(1)} %copy-done.42), channel_id=2, replica_groups=mesh['fsdp'=16,'seq'=2] {'fsdp','seq'}, use_global_device_ids=true, to_apply=%region_19.20.clone | all-reduce | flops 2304 | bytes 18432
  693.9 17.3 %reduce-scatter.12.cloned.1.call-done = f32[32,1024]{1,0:T(8,128)} async-done(((f32[1024,1024]{1,0:T(8,128)}), f32[32,1024]{1,0:T(8,128)}) %reduce-scatter.12.cloned.1.call-update) | async-done | bytes 131088 | tf_op jit(solution)/shard_map/reduce_scatter | solution.py:288
  711.2 142.8 %reduce-scatter.10.cloned.1.call-done = f32[32,1024]{1,0:T(8,128)} async-done(((f32[1024,1024]{1,0:T(8,128)}), f32[32,1024]{1,0:T(8,128)}) %reduce-scatter.10.cloned.1.call-update) | async-done | bytes 131088 | tf_op jit(solution)/shard_map/reduce_scatter | solution.py:287
  854.0 189.1 %reduce-scatter.8.cloned.1.call-done = f32[32,2048]{1,0:T(8,128)} async-done(((f32[1024,2048]{1,0:T(8,128)}), f32[32,2048]{1,0:T(8,128)}) %reduce-scatter.8.cloned.1.call-update) | async-done | bytes 262160 | tf_op jit(solution)/shard_map/reduce_scatter | solution.py:286
  1043.2 162.5 %reduce-scatter.16.cloned.1.call-done = f32[32,3072]{1,0:T(8,128)} async-done(((f32[1024,3072]{1,0:T(8,128)}), f32[32,3072]{1,0:T(8,128)}) %reduce-scatter.16.cloned.1.call-update) | async-done | bytes 393232 | tf_op jit(solution)/shard_map/reduce_scatter | solution.py:190
  1205.6 162.3 %reduce-scatter.18.cloned.1.call-done = f32[32,3072]{1,0:T(8,128)} async-done(((f32[1024,3072]{1,0:T(8,128)}), f32[32,3072]{1,0:T(8,128)}) %reduce-scatter.18.cloned.1.call-update) | async-done | bytes 393232 | tf_op jit(solution)/shard_map/reduce_scatter | solution.py:191
  1368.0 185.1 %reduce-scatter.14.cloned.1.call-done = f32[64,1024]{1,0:T(8,128)} async-done(((f32[2048,1024]{1,0:T(8,128)}), f32[64,1024]{1,0:T(8,128)}) %reduce-scatter.14.cloned.1.call-update) | async-done | bytes 262160 | tf_op jit(solution)/shard_map/reduce_scatter | solution.py:289
  1553.0 162.2 %reduce-scatter.20.cloned.1.call-done = f32[96,1024]{1,0:T(8,128)} async-done(((f32[3072,1024]{1,0:T(8,128)}), f32[96,1024]{1,0:T(8,128)}) %reduce-scatter.20.cloned.1.call-update) | async-done | bytes 393232 | tf_op jit(solution)/shard_map/reduce_scatter | solution.py:192
  (345 shorter events, 172.5 us)
Async XLA Ops:
  7.2 61.7 %all-gather.10.cloned.1.call-start = ((), (), s32[]{:S(2)}) async-start(), calls=%async_computation.8 | async-start | bytes 2162688 | tf_op jit(solution)/shard_map/all_gather | solution.py:93
  7.9 119.4 %all-gather.12.cloned.1.call-start = ((), (), s32[]{:S(2)}) async-start(), calls=%async_computation.9 | async-start | bytes 2162688 | tf_op jit(solution)/shard_map/all_gather | solution.py:94
  8.7 182.4 %all-gather.8.cloned.1.call-start = ((), (), s32[]{:S(2)}) async-start(), calls=%async_computation.7 | async-start | bytes 4325376 | tf_op jit(solution)/shard_map/all_gather | solution.py:92
  9.4 245.1 %all-gather.14.cloned.1.call-start = ((), (), s32[]{:S(2)}) async-start(), calls=%async_computation.10 | async-start | bytes 4325376 | tf_op jit(solution)/shard_map/all_gather | solution.py:95
  10.0 315.5 %all-gather.16.cloned.1.call-start = ((), (), s32[]{:S(2)}) async-start(), calls=%async_computation.11 | async-start | bytes 6488064 | tf_op jit(solution)/shard_map/all_gather | solution.py:156
  10.6 385.7 %all-gather.18.cloned.1.call-start = ((), (), s32[]{:S(2)}) async-start(), calls=%async_computation.12 | async-start | bytes 6488064 | tf_op jit(solution)/shard_map/all_gather | solution.py:157
  11.1 456.1 %all-gather.20.cloned.1.call-start = ((), (), s32[]{:S(2)}) async-start(), calls=%async_computation.13 | async-start | bytes 6488064 | tf_op jit(solution)/shard_map/all_gather | solution.py:158
  11.9 699.3 %reduce-scatter.12.cloned.1.call-start = ((), (), s32[]{:S(2)}) async-start(), calls=%async_computation.16 | async-start | bytes 4325376 | tf_op jit(solution)/shard_map/reduce_scatter | solution.py:288
  56.8 70.5 %copy-start.1 = (bf16[128,1024]{1,0:T(8,128)(2,1)S(1)}, bf16[128,1024]{1,0:T(8,128)(2,1)}, u32[]{:S(2)}) copy-start(bf16[128,1024]{1,0:T(8,128)(2,1)} %param.19) | copy-start | bytes 786436
  58.0 133.0 %copy-start.37 = (f32[128]{0:T(128)}, f32[128]{0:T(128)S(1)}, u32[]{:S(2)}) copy-start(f32[128]{0:T(128)S(1)} %fusion.69) | copy-start | bytes 1540
  58.0 71.4 %copy-start.43 = (f32[128]{0:T(128)}, f32[128]{0:T(128)S(1)}, u32[]{:S(2)}) copy-start(f32[128]{0:T(128)S(1)} %convert_element_type.121) | copy-start | bytes 1540
  61.7 70.3 %copy-start.29 = (f32[128,64]{0,1:T(8,128)}, f32[128,64]{0,1:T(8,128)S(1)}, u32[]{:S(2)}) copy-start(f32[128,64]{0,1:T(8,128)S(1)} %get-tuple-element.363) | copy-start | bytes 98308
  61.7 70.4 %copy-start.31 = (f32[128,64]{0,1:T(8,128)}, f32[128,64]{0,1:T(8,128)S(1)}, u32[]{:S(2)}) copy-start(f32[128,64]{0,1:T(8,128)S(1)} %get-tuple-element.364) | copy-start | bytes 98308
  71.6 66.5 %copy-start.6 = (f32[128,8,128]{0,2,1:T(8,128)}, f32[128,8,128]{0,2,1:T(8,128)S(1)}, u32[]{:S(2)}) copy-start(f32[128,8,128]{0,2,1:T(8,128)S(1)} %copy.151) | copy-start | bytes 1572868
  71.7 66.4 %copy-start.40 = (f32[128,8]{0,1:T(8,128)}, f32[128,8]{0,1:T(8,128)S(1)}, u32[]{:S(2)}) copy-start(f32[128,8]{0,1:T(8,128)S(1)} %copy.150) | copy-start | bytes 12292
  72.5 59.8 %collective-permute-start = (bf16[128,1024]{0,1:T(8,128)(2,1)S(1)}, bf16[128,1024]{0,1:T(8,128)(2,1)S(1)}, u32[]{:S(2)}, u32[]{:S(2)}) collective-permute-start(bf16[128,1024]{0,1:T(8,128)(2,1)S(1)} %bitcast.208), channel_id=1, source_target_pairs={{0,1},{2,3},{4,5},{6,7},{8,9},{10,11},{12,13},{14,15},{16,17},{18,... | collective-permute-start | bytes 786440 | tf_op jit(solution)/shard_map/ppermute | solution.py:18
  129.4 8.5 collective-permute-start.1
  132.1 63.0 %copy-start.25 = (f32[128,64]{1,0:T(8,128)}, f32[128,64]{1,0:T(8,128)S(1)}, u32[]{:S(2)}) copy-start(f32[128,64]{1,0:T(8,128)S(1)} %copy.146) | copy-start | bytes 98308
  132.2 62.9 %copy-start.27 = (f32[128,64]{1,0:T(8,128)}, f32[128,64]{1,0:T(8,128)S(1)}, u32[]{:S(2)}) copy-start(f32[128,64]{1,0:T(8,128)S(1)} %copy.147) | copy-start | bytes 98308
  132.3 62.4 %copy-start.45 = (f32[128]{0:T(128)}, f32[128]{0:T(128)S(1)}, u32[]{:S(2)}) copy-start(f32[128]{0:T(128)S(1)} %convert_element_type.119) | copy-start | bytes 1540
  132.3 125.2 %copy-start.35 = (f32[1024]{0:T(1024)}, f32[1024]{0:T(1024)S(1)}, u32[]{:S(2)}) copy-start(f32[1024]{0:T(1024)S(1)} %convert_element_type.128) | copy-start | bytes 12292
  221.2 109.2 %copy-start.12 = (bf16[8,2,128,128]{2,3,1,0:T(8,128)(2,1)}, bf16[8,2,128,128]{2,3,1,0:T(8,128)(2,1)S(1)}, u32[]{:S(2)}) copy-start(bf16[8,2,128,128]{2,3,1,0:T(8,128)(2,1)S(1)} %get-tuple-element.105) | copy-start | bytes 1572868
  330.4 136.8 %copy-start.21 = (bf16[128,1024]{1,0:T(8,128)(2,1)S(1)}, bf16[128,1024]{1,0:T(8,128)(2,1)}, u32[]{:S(2)}) copy-start(bf16[128,1024]{1,0:T(8,128)(2,1)} %param.33) | copy-start | bytes 786436
  561.3 10.4 collective-permute-start.3
  576.0 278.0 %reduce-scatter.10.cloned.1.call-start = ((), (), s32[]{:S(2)}) async-start(), calls=%async_computation.15 | async-start | bytes 4325376 | tf_op jit(solution)/shard_map/reduce_scatter | solution.py:287
  577.2 15.9 collective-permute-start.2
  597.0 446.2 %reduce-scatter.8.cloned.1.call-start = ((), (), s32[]{:S(2)}) async-start(), calls=%async_computation.14 | async-start | bytes 8650752 | tf_op jit(solution)/shard_map/reduce_scatter | solution.py:286
  609.9 595.8 %reduce-scatter.16.cloned.1.call-start = ((), (), s32[]{:S(2)}) async-start(), calls=%async_computation.18 | async-start | bytes 12976128 | tf_op jit(solution)/shard_map/reduce_scatter | solution.py:190
  617.3 750.6 %reduce-scatter.18.cloned.1.call-start = ((), (), s32[]{:S(2)}) async-start(), calls=%async_computation.19 | async-start | bytes 12976128 | tf_op jit(solution)/shard_map/reduce_scatter | solution.py:191
  624.8 928.2 %reduce-scatter.14.cloned.1.call-start = ((), (), s32[]{:S(2)}) async-start(), calls=%async_computation.17 | async-start | bytes 8650752 | tf_op jit(solution)/shard_map/reduce_scatter | solution.py:289
  630.4 1084.9 %reduce-scatter.20.cloned.1.call-start = ((), (), s32[]{:S(2)}) async-start(), calls=%async_computation.20 | async-start | bytes 12976128 | tf_op jit(solution)/shard_map/reduce_scatter | solution.py:192
  645.3 46.6 %copy-start.50 = (f32[128]{0:T(128)S(1)}, f32[128]{0:T(128)}, u32[]{:S(2)}) copy-start(f32[128]{0:T(128)} %copy-done.49) | copy-start | bytes 1540
  (37 other events, 268.0 us)
Sparse Core Ops, SparseCore 0:
  11.1 57.7 all-gather.9
  72.0 55.3 all-gather.11
  130.2 60.7 all-gather.7
  193.8 60.6 all-gather.13
  257.2 68.2 all-gather.15
  328.2 67.9 all-gather.17
  399.2 67.9 all-gather.19
  576.1 135.0 reduce-scatter.11
  714.1 139.9 reduce-scatter.9
  856.8 186.3 reduce-scatter.7
  1049.8 155.8 reduce-scatter.15
  1213.1 154.7 reduce-scatter.17
  1370.8 182.1 reduce-scatter.13
  1559.5 155.7 reduce-scatter.19
where the time goes:
time: 1730 us; the launch traced here: 1720 us
  waiting for transfers between devices  1400 us (81%)
  matrix products  147 us (8%)
  blocking collectives  82.5 us (5%)
  other arithmetic  35.5 us (2%)
  local copies, waits for them, and re-layouts  35.5 us (2%)
    reduce_scatter x1, waiting for transfers between devices, local(): lax.psum_scatter(grad_query_w, ('fsdp', 'seq'), scatter_dimension=0, tile...  189 us
    reduce_scatter x1, waiting for transfers between devices, local(): lax.psum_scatter(grad_output_w, ('fsdp', 'seq'), scatter_dimension=0, til...  185 us
    reduce_scatter x1, waiting for transfers between devices, local(): lax.psum_scatter(grad_gate_w, ('fsdp', 'seq'), scatter_dimension=0, tiled...  162 us
    reduce_scatter x1, waiting for transfers between devices, local(): lax.psum_scatter(grad_up_w, ('fsdp', 'seq'), scatter_dimension=0, tiled=T...  162 us
    reduce_scatter x1, waiting for transfers between devices, local(): lax.psum_scatter(grad_down_w, ('fsdp', 'seq'), scatter_dimension=0, tiled...  162 us
    reduce_scatter x1, waiting for transfers between devices, local(): lax.psum_scatter(grad_key_w, ('fsdp', 'seq'), scatter_dimension=0, tiled=...  143 us
    unnamed x2, blocking collectives  82.5 us
    all_gather x1, waiting for transfers between devices, local(): lax.all_gather(w_gate, ('fsdp', 'seq'), axis=0, tiled=True)  67.9 us
  transfers between devices with their start and end apart: 18, of which 17 were waited for; matrix products, arithmetic and copies ran while one was open for 7% of the time, Pallas kernels for 0%

commit v1 on v0

v1 whole, which is shorter than its diff:
```python
import jax
import jax.numpy as jnp
import numpy as np
from jax import lax
from jax.sharding import Mesh, PartitionSpec as P

QUERY_HEADS = 16
KEY_VALUE_HEADS = 8
HEAD_SIZE = 128
GROUP = QUERY_HEADS // KEY_VALUE_HEADS

EPS = 1e-06
THETA = 1000000.0
SCALE = HEAD_SIZE ** (-0.5)

ALL = ("data", "x", "core", "seq")
BF = jnp.bfloat16
F32 = jnp.float32
SWAP = [(0, 1), (1, 0)]


def mm(a, b):
    return jnp.dot(a, b, preferred_element_type=F32)


def mm_nt(a, b):
    return lax.dot_general(a, b, (((1,), (1,)), ((), ())), preferred_element_type=F32)


def mm_tn(a, b):
    return lax.dot_general(a, b, (((0,), (0,)), ((), ())), preferred_element_type=F32)


def flip(value, axis):
    return lax.ppermute(value, axis, SWAP)


def after(value, *others):
    return lax.optimization_barrier((value,) + others)[0]


def gather_plane(block):
    from_d = lax.ppermute(block, ("x", "seq"), [(i, i ^ 3) for i in range(4)])
    near = jnp.stack([block, flip(block, "seq"), flip(block, "x"), from_d])
    return jnp.concatenate([near, flip(near, "core")], axis=0)


def scatter_plane(parts):
    total = parts[:4] + flip(parts[4:].astype(BF), "core").astype(F32)
    low = total[1:].astype(BF)
    from_d = lax.ppermute(low[2], ("x", "seq"), [(i, i ^ 3) for i in range(4)])
    from_y = flip(low[0], "seq")
    from_x = flip(low[1], "x")
    return total[0] + from_y.astype(F32) + from_x.astype(F32) + from_d.astype(F32)


def to_all(payload):
    return lax.all_to_all(payload, ALL, split_axis=0, concat_axis=0, tiled=True)


def row_routes(count, shift):
    return [
        (count * j + (d + shift) % count, d * 8 + j) for d in range(count) for j in range(8)
    ]


def gather_rows(block, count, mine):
    parts = [lax.ppermute(block, ALL, row_routes(count, s)) for s in range(count)]
    both = jnp.stack(parts + parts)
    start = (count - mine) % count
    turned = lax.dynamic_slice_in_dim(both, start, count, 0)
    return turned.reshape(count * block.shape[0], block.shape[1])


def scatter_rows(grad, count, mine):
    parts = grad.reshape(count, grad.shape[0] // count, grad.shape[1])
    both = jnp.concatenate([parts, parts], axis=0)
    turned = lax.dynamic_slice_in_dim(both, mine, count, 0)
    total = 0.0
    for s in range(count):
        back = [(b, a) for a, b in row_routes(count, s)]
        total = total + lax.ppermute(turned[s], ALL, back).astype(F32)
    return total


def col_payload(weights, extra=None):
    rows = weights[0].shape[0]
    pieces = []
    for weight in weights:
        per = weight.shape[1] // (8 * 128)
        cut = weight.reshape(rows, 8, per, 128).transpose(1, 2, 0, 3)
        pieces.append(cut.reshape(8, per * rows, 128))
    if extra is not None:
        pieces.append(jnp.broadcast_to(extra[None], (8,) + extra.shape))
    return jnp.concatenate(pieces, axis=1)


def send_cols(weights, count, extra=None):
    payload = col_payload(weights, extra)
    payload = jnp.broadcast_to(payload[None], (count,) + payload.shape)
    return to_all(payload.reshape((count * 8,) + payload.shape[2:]))


def cols_of(received, rows, blocks):
    devices = received.shape[0]
    return jnp.concatenate(
        [
            received[:, c * rows : (c + 1) * rows].reshape(devices * rows, 128)
            for c in range(blocks)
        ],
        axis=1,
    )


def grad_payload(grad, devices, extra=None):
    rows = grad.shape[0] // devices
    blocks = grad.shape[1] // 128
    cut = [grad[:, c * 128 : (c + 1) * 128].reshape(devices, rows, 128) for c in range(blocks)]
    if extra is not None:
        cut.append(jnp.broadcast_to(extra[None], (devices,) + extra.shape))
    return jnp.concatenate(cut, axis=1)


def grad_cols(total, rows, first, per):
    part = total[:, first * rows : (first + per) * rows].reshape(8, per, rows, 128)
    return part.transpose(2, 0, 1, 3).reshape(rows, 8 * per * 128)


def inv_rms(values):
    return lax.rsqrt(jnp.mean(values * values, axis=-1, keepdims=True) + EPS)


def turn(values, cosine, sine):
    half = values.shape[-1] // 2
    a, b = values[..., :half], values[..., half:]
    return jnp.concatenate([a * cosine - b * sine, b * cosine + a * sine], axis=-1)


def head_path(raw, gain, cosine, sine):
    return turn(raw * inv_rms(raw) * gain, cosine, sine).astype(BF)


def head_pull(grad, raw, gain, cosine, sine):
    back = turn(grad, cosine, -sine)
    r = inv_rms(raw)
    u = back * gain
    grad_gain = jnp.sum(back * raw * r, axis=(0, 1))
    return r * u - raw * (r * r * r) * jnp.mean(u * raw, axis=-1, keepdims=True), grad_gain


def seq_bounds(lengths, seq_order):
    seq_count = lengths.shape[-1]
    picked = seq_order[..., :, None] == jnp.arange(seq_count, dtype=jnp.int32)
    packed = jnp.sum(jnp.where(picked, lengths[..., None, :], 0), axis=-1)
    seq_ends = jnp.cumsum(packed, axis=-1)
    return (seq_ends - packed, seq_ends)


def local(
    tokens,
    norm_gain,
    w_query,
    w_key,
    w_value,
    w_output,
    query_gain,
    key_gain,
    mlp_gain,
    w_gate,
    w_up,
    w_down,
    lengths,
    seq_order,
    cotangent,
):
    rows, width = tokens.shape
    count = lax.axis_size("data")
    devices = count * 8
    mine = lax.axis_index("data")
    in_seq = lax.axis_index("seq")
    w_rows = w_query.shape[0]
    gains = query_gain.shape[0]
    n_seq = lengths.shape[1]

    extra = jnp.stack([query_gain, key_gain]).reshape(1, 2 * gains)
    extra = jnp.concatenate([extra, norm_gain[None], mlp_gain[None]], axis=1)
    n_extra = extra.shape[1]
    extra = jnp.pad(extra, ((0, 7), (0, 128 - n_extra)))
    got_qkv = send_cols([w_query, w_key, w_value], count, extra)
    qkv_full = cols_of(got_qkv, w_rows, 4)
    got_gains = got_qkv[:, 4 * w_rows, :n_extra].astype(F32)
    query_norm = got_gains[:, :gains].reshape(-1)
    key_norm = got_gains[:, gains : 2 * gains].reshape(-1)
    gain_in = got_gains[:, 2 * gains : 2 * gains + w_rows].reshape(-1)
    gain_mid = got_gains[:, 2 * gains + w_rows :].reshape(-1)
    got_gu = send_cols([after(w_gate, got_qkv), w_up], count)
    gu_full = cols_of(got_gu, w_rows, got_gu.shape[1] // w_rows)

    marks = jnp.concatenate([lengths, seq_order], axis=1).astype(BF)
    marks = jnp.pad(marks, ((0, 7), (0, width - 2 * n_seq)))
    got_tokens = gather_plane(jnp.concatenate([tokens, marks], axis=0))
    plane_rows = 8 * rows
    inputs = got_tokens[:, :rows].reshape(plane_rows, width).astype(F32)
    marks = got_tokens[0::2, rows, : 2 * n_seq].astype(jnp.int32)
    starts, ends = seq_bounds(marks[:, :n_seq], marks[:, n_seq:])
    row_ids = jnp.arange(rows, dtype=jnp.int32)
    row_ids = jnp.concatenate([in_seq * rows + row_ids, (1 - in_seq) * rows + row_ids])
    inside = (starts[:, None, :] <= row_ids[None, :, None]) & (
        row_ids[None, :, None] < ends[:, None, :]
    )
    first_rows = jnp.sum(jnp.where(inside, starts[:, None, :], 0), axis=2)
    allowed = (row_ids[None, None, :] <= row_ids[None, :, None]) & (
        row_ids[None, None, :] >= first_rows[:, :, None]
    )
    positions = (row_ids[None, :] - first_rows).reshape(plane_rows)
    half = HEAD_SIZE // 2
    frequency = jnp.power(THETA, -jnp.arange(half, dtype=F32) * (2.0 / HEAD_SIZE))
    angles = positions.astype(F32)[:, None] * frequency[None, :]
    cosine = jnp.cos(angles)[:, None, :]
    sine = jnp.sin(angles)[:, None, :]

    out_full = gather_rows(after(w_output, got_tokens), count, mine)
    cot_all = gather_plane(after(cotangent, got_tokens)).reshape(plane_rows, width)
    down_full = gather_rows(after(w_down, out_full), count, mine)
    ff = down_full.shape[0]
    normed_in = (inputs * inv_rms(inputs) * gain_in).astype(BF)
    qkv = mm(normed_in, qkv_full)
    query_raw = qkv[:, : GROUP * HEAD_SIZE].reshape(plane_rows, GROUP, HEAD_SIZE)
    key_raw = qkv[:, GROUP * HEAD_SIZE : -HEAD_SIZE].reshape(plane_rows, 1, HEAD_SIZE)
    span = 2 * rows
    query_low = head_path(query_raw, query_norm, cosine, sine).reshape(4, span, GROUP, HEAD_SIZE)
    key_low = head_path(key_raw, key_norm, cosine, sine).reshape(4, span, HEAD_SIZE)
    value_low = qkv[:, -HEAD_SIZE:].astype(BF).reshape(4, span, HEAD_SIZE)
    scores = jnp.einsum("bqhd,bkd->bhqk", query_low, key_low, preferred_element_type=F32) * SCALE
    scores = jnp.where(allowed[:, None], scores, -1e30)
    exp_scores = jnp.exp(scores - jnp.max(scores, axis=-1, keepdims=True))
    probs = exp_scores / jnp.sum(exp_scores, axis=-1, keepdims=True)
    probs_low = probs.astype(BF)
    attn_low = (
        jnp.einsum("bhqk,bkd->bqhd", probs_low, value_low, preferred_element_type=F32)
        .astype(BF)
        .reshape(plane_rows, GROUP * HEAD_SIZE)
    )
    out_parts = mm(attn_low, out_full).reshape(8, rows, width)
    hidden = tokens.astype(F32) + scatter_plane(out_parts)

    r_mid = inv_rms(hidden)
    normed_mid = gather_plane((hidden * r_mid * gain_mid).astype(BF)).reshape(plane_rows, width)
    gate_up = mm(normed_mid, gu_full)
    gate_pre, upward = gate_up[:, :ff], gate_up[:, ff:]
    sigma = 1.0 / (1.0 + jnp.exp(-gate_pre))
    silu = gate_pre * sigma
    mixed_low = (silu * upward).astype(BF)
    grad_mixed = mm_nt(cot_all, down_full)
    grad_gate = grad_mixed * upward * sigma * (1.0 + gate_pre * (1.0 - sigma))
    grad_up = grad_mixed * silu
    grad_gu = jnp.concatenate([grad_gate.astype(BF), grad_up.astype(BF)], axis=1)
    u_mid = gain_mid * scatter_plane(mm_nt(grad_gu, gu_full).reshape(8, rows, width))
    cot = cotangent.astype(F32)
    grad_hidden = (
        cot
        + r_mid * u_mid
        - hidden * (r_mid * r_mid * r_mid) * jnp.mean(u_mid * hidden, axis=-1, keepdims=True)
    )
    grad_out_all = gather_plane(grad_hidden.astype(BF)).reshape(plane_rows, width)

    result_parts = mm(mixed_low, down_full).reshape(8, rows, width)
    result = (hidden + scatter_plane(result_parts)).astype(BF)
    got_down = scatter_rows(mm_tn(mixed_low, cot_all).astype(BF), count, mine)
    got_ggu = to_all(grad_payload(mm_tn(normed_mid, grad_gu).astype(BF), devices))

    got_out = scatter_rows(mm_tn(attn_low, grad_out_all).astype(BF), count, mine)
    grad_attn = mm_nt(grad_out_all, out_full).astype(BF).reshape(4, span, GROUP, HEAD_SIZE)
    grad_probs = jnp.einsum("bqhd,bkd->bhqk", grad_attn, value_low, preferred_element_type=F32)
    row_dot = jnp.sum(probs * grad_probs, axis=-1, keepdims=True)
    grad_scores = (probs * (grad_probs - row_dot)).astype(BF)
    grad_query = (
        jnp.einsum("bhqk,bkd->bqhd", grad_scores, key_low, preferred_element_type=F32) * SCALE
    )
    grad_key = (
        jnp.einsum("bhqk,bqhd->bkd", grad_scores, query_low, preferred_element_type=F32) * SCALE
    )
    grad_value = jnp.einsum("bhqk,bqhd->bkd", probs_low, grad_attn, preferred_element_type=F32)
    grad_query_raw, query_gain_part = head_pull(
        grad_query.reshape(plane_rows, GROUP, HEAD_SIZE), query_raw, query_norm, cosine, sine
    )
    grad_key_raw, key_gain_part = head_pull(
        grad_key.reshape(plane_rows, 1, HEAD_SIZE), key_raw, key_norm, cosine, sine
    )
    grad_qkv = jnp.concatenate(
        [
            grad_query_raw.reshape(plane_rows, GROUP * HEAD_SIZE),
            grad_key_raw.reshape(plane_rows, HEAD_SIZE),
            grad_value.reshape(plane_rows, HEAD_SIZE),
        ],
        axis=1,
    ).astype(BF)
    gain_parts = jnp.stack([query_gain_part, key_gain_part])
    gain_high = gain_parts.astype(BF)
    gain_low = (gain_parts - gain_high.astype(F32)).astype(BF)
    gain_rows = jnp.pad(jnp.concatenate([gain_high, gain_low]), ((0, 4), (0, 0)))
    got_gqkv = to_all(
        grad_payload(mm_tn(normed_in, grad_qkv).astype(BF), devices, gain_rows)
    )
    u_in = gain_in * scatter_plane(mm_nt(grad_qkv, qkv_full).reshape(8, rows, width))
    x = tokens.astype(F32)
    r_in = inv_rms(x)
    grad_tokens = (
        grad_hidden
        + r_in * u_in
        - x * (r_in * r_in * r_in) * jnp.mean(u_in * x, axis=-1, keepdims=True)
    )

    def owned(got):
        return jnp.sum(got.reshape((count, 8) + got.shape[1:]).astype(F32), axis=0)

    def of_weight(total, first, weight):
        per = weight.shape[1] // (8 * 128)
        plain = grad_cols(total, w_rows, first, per)
        return plain, jnp.sum(plain * weight.astype(F32), axis=1)

    total_qkv = owned(got_gqkv)
    grad_w_query, gain_q = of_weight(total_qkv, 0, w_query)
    grad_w_key, gain_k = of_weight(total_qkv, 2, w_key)
    grad_w_value, gain_v = of_weight(total_qkv, 3, w_value)
    total_gu = owned(got_ggu)
    grad_w_gate, gain_g = of_weight(total_gu, 0, w_gate)
    grad_w_up, gain_u = of_weight(total_gu, ff // 128, w_up)
    gain_sums = jnp.sum(total_qkv[:, 4 * w_rows :], axis=0)
    me = lax.axis_index(ALL)
    gain_sums = gain_sums[0:2] + gain_sums[2:4]
    gain_mine = lax.dynamic_slice_in_dim(gain_sums, me * gains, gains, 1)
    return (
        result,
        grad_tokens,
        (gain_q + gain_k + gain_v) / norm_gain.astype(F32),
        grad_w_query,
        grad_w_key,
        grad_w_value,
        got_out,
        gain_mine[0],
        gain_mine[1],
        (gain_g + gain_u) / mlp_gain.astype(F32),
        grad_w_gate,
        grad_w_up,
        got_down,
    )


def solution(mesh):
    fsdp, seq = mesh.shape["fsdp"], mesh.shape["seq"]
    fine = Mesh(np.asarray(mesh.devices).reshape(fsdp // 4, 2, 2, seq), ALL)
    matrix, vector, group = P(ALL, None), P(ALL), P(ALL[:3], None)
    placed = (
        matrix, vector, matrix, matrix, matrix, matrix, vector, vector, vector,
        matrix, matrix, matrix, group, group, matrix,
    )
    outs = (
        matrix, matrix, vector, matrix, matrix, matrix, matrix, vector, vector, vector,
        matrix, matrix, matrix,
    )
    return jax.shard_map(local, mesh=fine, in_specs=placed, out_specs=outs, check_vma=False)
```

time: 1730 us -> 385 us (0.22)
  the two profiles are of different devices: /device:TPU:2 before, /device:TPU:0 now
where the time goes in v1:
time: 385 us; the launch traced here: 379 us
  starting transfers between devices  132 us (34%)
  local copies, waits for them, and re-layouts  93.4 us (24%)
  waiting for transfers between devices  71.5 us (19%)
  other arithmetic  48.5 us (13%)
  matrix products  31.2 us (8%)
    ppermute x24, waiting for transfers between devices, flip(): return lax.ppermute(value, axis, SWAP)  59.3 us
    unnamed x152, local copies, waits for them, and re-layouts  43.5 us
    ppermute x24, starting transfers between devices, flip(): return lax.ppermute(value, axis, SWAP)  35.9 us
    all_to_all x4, starting transfers between devices, to_all(): return lax.all_to_all(payload, ALL, split_axis=0, concat_axis=0, tiled=True)  32.6 us
    ppermute x8, starting transfers between devices, scatter_rows(): total = total + lax.ppermute(turned[s], ALL, back).astype(F32)  29.3 us
    ppermute x8, starting transfers between devices, gather_rows(): lax.ppermute(block, ALL, row_routes(count, s))  20.1 us
    ppermute x4, starting transfers between devices, gather_plane(): from_d = lax.ppermute(block, ('x', 'seq'), [(i, i ^ 3) for i in range(4)])  9.66 us
    another operation x9, other arithmetic  9.61 us
  transfers between devices with their start and end apart: 52, of which 11 were waited for; matrix products, arithmetic and copies ran while one was open for 39% of the time, Pallas kernels for 0%

profile of v1, /device:TPU:0, one launch (start us, length us, event | category | flops | bytes accessed | tf_op | source)
XLA Modules:
  0.0 379.1 jit_solution(7662096454810347266)
XLA Ops:
  3.1 3.0 collective-permute-start.1
  13.1 6.3 %all-to-all-start = ((bf16[32,136,128]{2,1,0:T(8,128)(2,1)}), bf16[32,136,128]{2,1,0:T(8,128)(2,1)S(1)}, u32[]{:S(2)}, u32[]{:S(2)}) async-start(bf16[32,136,128]{2,1,0:T(8,128)(2,1)} %bitcast.16), calls=%async_computation | async-start | bytes 2228224 | tf_op jit(solution)/shard_map/all_to_all | solution.py:58
  25.8 3.6 collective-permute-start.7
  31.6 4.8 %collective-permute-start.5 = (bf16[64,1024]{1,0:T(8,128)(2,1)}, bf16[64,1024]{1,0:T(8,128)(2,1)}, u32[]{:S(2)}, u32[]{:S(2)}) collective-permute-start(bf16[64,1024]{1,0:T(8,128)(2,1)} %param.20), channel_id=1, source_target_pairs={{1,0},{5,1},{9,2},{13,3},{17,4},{21,5},{25,6},{29,7},{2,8},{6,9},{... | collective-permute-start | bytes 393224 | tf_op jit(solution)/shard_map/ppermute | solution.py:68
  38.6 2.5 slice_convert_fusion.4
  44.2 2.9 fusion.73
  47.1 12.8 %collective-permute-start.25 = (bf16[128,1024]{1,0:T(8,128)(2,1)S(1)}, bf16[128,1024]{1,0:T(8,128)(2,1)S(1)}, u32[]{:S(2)}, u32[]{:S(2)}) collective-permute-start(bf16[128,1024]{1,0:T(8,128)(2,1)S(1)} %copy-done.9), channel_id=1, source_target_pairs={{0,4},{4,0},{1,5},{5,1},{2,6},{6,2},{3,7},{7,3},{8,12},{12,8},{9,1... | collective-permute-start | bytes 786440 | tf_op jit(solution)/shard_map/ppermute | solution.py:35
  66.1 2.4 collective-permute-start.19
  74.5 2.9 collective-permute-start.27
  80.5 2.6 fusion.2
  94.0 4.0 %fusion.120 = (f32[4,2,256]{2,1,0:T(2,128)S(1)}, f32[4,2,256,256]{2,3,1,0:T(8,128)}) fusion(pred[4,256,256]{1,2,0:T(8,128)(4,1)} %compare_and_fusion, bf16[4,256,64]{2,1,0:T(8,128)(2,1)} %bitcast.411, bf16[4,256,64]{2,1,0:T(8,128)(2,1)} %bitcast.409, bf16[4,256,2,64]{3,1,0,2:T(8,128)(2,1)S(1)} %bitcast.401, bf16[4,256,2,64]{3,1,0,2:T(8,128)(2,1)S(1)} %bitcast.399), kind=kOutput, calls=%fused_computation.328 | convolution fusion | flops 137888000 | bytes 3153920 | tf_op jit(solution)/shard_map/sub | solution.py:236
  112.3 10.3 %all-to-all-start.1 = ((bf16[32,192,128]{2,1,0:T(8,128)(2,1)}), bf16[32,192,128]{2,1,0:T(8,128)(2,1)}, u32[]{:S(2)}, u32[]{:S(2)}) async-start(bf16[32,192,128]{2,1,0:T(8,128)(2,1)} %bitcast.387), calls=%async_computation.1 | async-start | bytes 3145728 | tf_op jit(solution)/shard_map/all_to_all | solution.py:58
  122.6 3.8 fusion.110
  134.0 16.5 %collective-permute-done.9 = bf16[128,1024]{1,0:T(8,128)(2,1)S(1)} collective-permute-done((bf16[128,1024]{1,0:T(8,128)(2,1)}, bf16[128,1024]{1,0:T(8,128)(2,1)S(1)}, u32[]{:S(2)}, u32[]{:S(2)}) %collective-permute-start.9) | collective-permute-done | bytes 262176 | tf_op jit(solution)/shard_map/ppermute | solution.py:35
  155.0 2.5 collective-permute-start.14
  165.2 5.8 %collective-permute-done.13 = bf16[128,1024]{1,0:T(8,128)(2,1)S(1)} collective-permute-done((bf16[128,1024]{1,0:T(8,128)(2,1)S(1)}, bf16[128,1024]{1,0:T(8,128)(2,1)S(1)}, u32[]{:S(2)}, u32[]{:S(2)}) %collective-permute-start.13) | collective-permute-done | bytes 262176 | tf_op jit(solution)/shard_map/ppermute | solution.py:35
  178.0 3.6 fusion.123
  183.2 3.5 convolution_convert_fusion
  204.1 8.3 %collective-permute-done.29 = bf16[128,1024]{1,0:T(8,128)(2,1)S(1)} collective-permute-done((bf16[128,1024]{1,0:T(8,128)(2,1)S(1)}, bf16[128,1024]{1,0:T(8,128)(2,1)S(1)}, u32[]{:S(2)}, u32[]{:S(2)}) %collective-permute-start.29) | collective-permute-done | bytes 262176 | tf_op jit(solution)/shard_map/ppermute | solution.py:35
  214.9 3.1 collective-permute-start.44
  218.9 11.8 %collective-permute-done.21 = bf16[128,1024]{1,0:T(8,128)(2,1)S(1)} collective-permute-done((bf16[128,1024]{1,0:T(8,128)(2,1)S(1)}, bf16[128,1024]{1,0:T(8,128)(2,1)S(1)}, u32[]{:S(2)}, u32[]{:S(2)}) %collective-permute-start.21) | collective-permute-done | bytes 262176 | tf_op jit(solution)/shard_map/ppermute | solution.py:35
  232.9 6.3 %collective-permute-start.34 = (bf16[128,1024]{1,0:T(8,128)(2,1)S(1)}, bf16[128,1024]{1,0:T(8,128)(2,1)S(1)}, u32[]{:S(2)}, u32[]{:S(2)}) collective-permute-start(bf16[128,1024]{1,0:T(8,128)(2,1)S(1)} %get-tuple-element.34), channel_id=1, source_target_pairs={{0,5},{1,4},{4,1},{5,0},{2,7},{3,6},{6,3},{7,2},{8,13},{9,12},{12,... | collective-permute-start | bytes 786440 | tf_op jit(solution)/shard_map/ppermute | solution.py:43
  242.1 4.4 %collective-permute-done.34 = bf16[128,1024]{1,0:T(8,128)(2,1)S(1)} collective-permute-done((bf16[128,1024]{1,0:T(8,128)(2,1)S(1)}, bf16[128,1024]{1,0:T(8,128)(2,1)S(1)}, u32[]{:S(2)}, u32[]{:S(2)}) %collective-permute-start.34) | collective-permute-done | bytes 262176 | tf_op jit(solution)/shard_map/ppermute | solution.py:43
  246.5 4.7 %collective-permute-start.45 = (bf16[96,1024]{1,0:T(8,128)(2,1)}, bf16[96,1024]{1,0:T(8,128)(2,1)}, u32[]{:S(2)}, u32[]{:S(2)}) collective-permute-start(bf16[96,1024]{1,0:T(8,128)(2,1)} %get-tuple-element.89), channel_id=1, source_target_pairs={{0,1},{1,5},{2,9},{3,13},{4,17},{5,21},{6,25},{7,29},{8,2},{9,6},{... | collective-permute-start | bytes 589832 | tf_op jit(solution)/shard_map/ppermute | solution.py:82
  251.2 6.1 %collective-permute-start.47 = (bf16[96,1024]{1,0:T(8,128)(2,1)}, bf16[96,1024]{1,0:T(8,128)(2,1)}, u32[]{:S(2)}, u32[]{:S(2)}) collective-permute-start(bf16[96,1024]{1,0:T(8,128)(2,1)} %get-tuple-element.90), channel_id=1, source_target_pairs={{0,3},{1,7},{2,11},{3,15},{4,19},{5,23},{6,27},{7,31},{8,0},{9,4},... | collective-permute-start | bytes 589832 | tf_op jit(solution)/shard_map/ppermute | solution.py:82
  258.8 7.8 %all-to-all-start.3 = ((bf16[32,192,128]{2,1,0:T(8,128)(2,1)}), bf16[32,192,128]{2,1,0:T(8,128)(2,1)}, u32[]{:S(2)}, u32[]{:S(2)}) async-start(bf16[32,192,128]{2,1,0:T(8,128)(2,1)} %constant_dynamic-update-slice_fusion.31), calls=%async_computation.3 | async-start | bytes 3145728 | tf_op jit(solution)/shard_map/all_to_all | solution.py:58
  297.0 2.5 copy.176
  307.7 3.1 collective-permute-start.42
  310.8 8.6 %collective-permute-start.41 = (bf16[64,1024]{1,0:T(8,128)(2,1)S(1)}, bf16[64,1024]{1,0:T(8,128)(2,1)S(1)}, u32[]{:S(2)}, u32[]{:S(2)}) collective-permute-start(bf16[64,1024]{1,0:T(8,128)(2,1)S(1)} %get-tuple-element.101), channel_id=1, source_target_pairs={{0,1},{1,5},{2,9},{3,13},{4,17},{5,21},{6,25},{7,29},{8,2},{9,6},{... | collective-permute-start | bytes 393224 | tf_op jit(solution)/shard_map/ppermute | solution.py:82
  327.5 5.8 %collective-permute-done.42 = bf16[64,1024]{1,0:T(8,128)(2,1)S(1)} collective-permute-done((bf16[64,1024]{1,0:T(8,128)(2,1)S(1)}, bf16[64,1024]{1,0:T(8,128)(2,1)S(1)}, u32[]{:S(2)}, u32[]{:S(2)}) %collective-permute-start.42) | collective-permute-done | bytes 131104 | tf_op jit(solution)/shard_map/ppermute | solution.py:82
  334.1 8.3 %all-to-all-start.2 = ((bf16[32,136,128]{2,1,0:T(8,128)(2,1)}), bf16[32,136,128]{2,1,0:T(8,128)(2,1)S(1)}, u32[]{:S(2)}, u32[]{:S(2)}) async-start(bf16[32,136,128]{2,1,0:T(8,128)(2,1)} %constant_dynamic-update-slice_fusion.26), calls=%async_computation.2 | async-start | bytes 2228224 | tf_op jit(solution)/shard_map/all_to_all | solution.py:58
  359.3 13.3 %collective-permute-done.37 = bf16[128,1024]{1,0:T(8,128)(2,1)S(1)} collective-permute-done((bf16[128,1024]{1,0:T(8,128)(2,1)S(1)}, bf16[128,1024]{1,0:T(8,128)(2,1)S(1)}, u32[]{:S(2)}, u32[]{:S(2)}) %collective-permute-start.37) | collective-permute-done | bytes 262176 | tf_op jit(solution)/shard_map/ppermute | solution.py:35
  (400 shorter events, 188.8 us)
Async XLA Ops:
  3.1 16.4 %collective-permute-start.1 = (bf16[136,1024]{1,0:T(8,128)(2,1)S(1)}, bf16[136,1024]{1,0:T(8,128)(2,1)S(1)}, u32[]{:S(2)}, u32[]{:S(2)}) collective-permute-start(bf16[136,1024]{1,0:T(8,128)(2,1)S(1)} %get-tuple-element.108), channel_id=1, source_target_pairs={{0,4},{4,0},{1,5},{5,1},{2,6},{6,2},{3,7},{7,3},{8,12},{12,8},{9,1... | collective-permute-start | bytes 835592 | tf_op jit(solution)/shard_map/ppermute | solution.py:35
  13.1 67.2 %all-to-all-start = ((bf16[32,136,128]{2,1,0:T(8,128)(2,1)}), bf16[32,136,128]{2,1,0:T(8,128)(2,1)S(1)}, u32[]{:S(2)}, u32[]{:S(2)}) async-start(bf16[32,136,128]{2,1,0:T(8,128)(2,1)} %bitcast.16), calls=%async_computation | async-start | bytes 2228224 | tf_op jit(solution)/shard_map/all_to_all | solution.py:58
  25.8 37.5 %collective-permute-start.7 = (bf16[64,1024]{1,0:T(8,128)(2,1)}, bf16[64,1024]{1,0:T(8,128)(2,1)S(1)}, u32[]{:S(2)}, u32[]{:S(2)}) collective-permute-start(bf16[64,1024]{1,0:T(8,128)(2,1)} %param.20), channel_id=1, source_target_pairs={{3,0},{7,1},{11,2},{15,3},{19,4},{23,5},{27,6},{31,7},{0,8},{4,9},... | collective-permute-start | bytes 393224 | tf_op jit(solution)/shard_map/ppermute | solution.py:68
  29.4 33.9 %collective-permute-start.6 = (bf16[64,1024]{1,0:T(8,128)(2,1)}, bf16[64,1024]{1,0:T(8,128)(2,1)S(1)}, u32[]{:S(2)}, u32[]{:S(2)}) collective-permute-start(bf16[64,1024]{1,0:T(8,128)(2,1)} %param.20), channel_id=1, source_target_pairs={{2,0},{6,1},{10,2},{14,3},{18,4},{22,5},{26,6},{30,7},{3,8},{7,9},... | collective-permute-start | bytes 393224 | tf_op jit(solution)/shard_map/ppermute | solution.py:68
  31.6 29.2 %collective-permute-start.5 = (bf16[64,1024]{1,0:T(8,128)(2,1)}, bf16[64,1024]{1,0:T(8,128)(2,1)}, u32[]{:S(2)}, u32[]{:S(2)}) collective-permute-start(bf16[64,1024]{1,0:T(8,128)(2,1)} %param.20), channel_id=1, source_target_pairs={{1,0},{5,1},{9,2},{13,3},{17,4},{21,5},{25,6},{29,7},{2,8},{6,9},{... | collective-permute-start | bytes 393224 | tf_op jit(solution)/shard_map/ppermute | solution.py:68
  41.1 28.3 %collective-permute-start.26 = (bf16[128,1024]{1,0:T(8,128)(2,1)S(1)}, bf16[128,1024]{1,0:T(8,128)(2,1)S(1)}, u32[]{:S(2)}, u32[]{:S(2)}) collective-permute-start(bf16[128,1024]{1,0:T(8,128)(2,1)S(1)} %copy-done.9), channel_id=1, source_target_pairs={{0,5},{1,4},{4,1},{5,0},{2,7},{3,6},{6,3},{7,2},{8,13},{9,12},{12,... | collective-permute-start | bytes 786440 | tf_op jit(solution)/shard_map/ppermute | solution.py:43
  47.1 24.5 %collective-permute-start.25 = (bf16[128,1024]{1,0:T(8,128)(2,1)S(1)}, bf16[128,1024]{1,0:T(8,128)(2,1)S(1)}, u32[]{:S(2)}, u32[]{:S(2)}) collective-permute-start(bf16[128,1024]{1,0:T(8,128)(2,1)S(1)} %copy-done.9), channel_id=1, source_target_pairs={{0,4},{4,0},{1,5},{5,1},{2,6},{6,2},{3,7},{7,3},{8,12},{12,8},{9,1... | collective-permute-start | bytes 786440 | tf_op jit(solution)/shard_map/ppermute | solution.py:35
  66.1 40.4 %collective-permute-start.19 = (bf16[96,1024]{1,0:T(8,128)(2,1)}, bf16[96,1024]{1,0:T(8,128)(2,1)}, u32[]{:S(2)}, u32[]{:S(2)}) collective-permute-start(bf16[96,1024]{1,0:T(8,128)(2,1)} %param.26), channel_id=1, source_target_pairs={{3,0},{7,1},{11,2},{15,3},{19,4},{23,5},{27,6},{31,7},{0,8},{4,9},... | collective-permute-start | bytes 589832 | tf_op jit(solution)/shard_map/ppermute | solution.py:68
  68.5 36.4 %collective-permute-start.18 = (bf16[96,1024]{1,0:T(8,128)(2,1)}, bf16[96,1024]{1,0:T(8,128)(2,1)}, u32[]{:S(2)}, u32[]{:S(2)}) collective-permute-start(bf16[96,1024]{1,0:T(8,128)(2,1)} %param.26), channel_id=1, source_target_pairs={{2,0},{6,1},{10,2},{14,3},{18,4},{22,5},{26,6},{30,7},{3,8},{7,9},... | collective-permute-start | bytes 589832 | tf_op jit(solution)/shard_map/ppermute | solution.py:68
  69.4 33.8 %collective-permute-start.17 = (bf16[96,1024]{1,0:T(8,128)(2,1)}, bf16[96,1024]{1,0:T(8,128)(2,1)}, u32[]{:S(2)}, u32[]{:S(2)}) collective-permute-start(bf16[96,1024]{1,0:T(8,128)(2,1)} %param.26), channel_id=1, source_target_pairs={{1,0},{5,1},{9,2},{13,3},{17,4},{21,5},{25,6},{29,7},{2,8},{6,9},{... | collective-permute-start | bytes 589832 | tf_op jit(solution)/shard_map/ppermute | solution.py:68
  74.5 96.8 %collective-permute-start.27 = (bf16[4,128,1024]{2,1,0:T(8,128)(2,1)}, bf16[4,128,1024]{2,1,0:T(8,128)(2,1)}, u32[]{:S(2)}, u32[]{:S(2)}) collective-permute-start(bf16[4,128,1024]{2,1,0:T(8,128)(2,1)} %pad_maximum_fusion.4), channel_id=1, source_target_pairs={{0,2},{2,0},{1,3},{3,1},{4,6},{6,4},{5,7},{7,5},{8,10},{10,8},{9,1... | collective-permute-start | bytes 3145736 | tf_op jit(solution)/shard_map/ppermute | solution.py:35
  102.3 20.3 %collective-permute-start.8 = (bf16[4,128,1024]{2,1,0:T(8,128)(2,1)}, bf16[4,128,1024]{2,1,0:T(8,128)(2,1)}, u32[]{:S(2)}, u32[]{:S(2)}) collective-permute-start(bf16[4,128,1024]{2,1,0:T(8,128)(2,1)} %bitcast.40), channel_id=1, source_target_pairs={{0,2},{2,0},{1,3},{3,1},{4,6},{6,4},{5,7},{7,5},{8,10},{10,8},{9,1... | collective-permute-start | bytes 3145736 | tf_op jit(solution)/shard_map/ppermute | solution.py:35
  112.3 63.6 %all-to-all-start.1 = ((bf16[32,192,128]{2,1,0:T(8,128)(2,1)}), bf16[32,192,128]{2,1,0:T(8,128)(2,1)}, u32[]{:S(2)}, u32[]{:S(2)}) async-start(bf16[32,192,128]{2,1,0:T(8,128)(2,1)} %bitcast.387), calls=%async_computation.1 | async-start | bytes 3145728 | tf_op jit(solution)/shard_map/all_to_all | solution.py:58
  127.2 23.3 %collective-permute-start.9 = (bf16[128,1024]{1,0:T(8,128)(2,1)}, bf16[128,1024]{1,0:T(8,128)(2,1)S(1)}, u32[]{:S(2)}, u32[]{:S(2)}) collective-permute-start(bf16[128,1024]{1,0:T(8,128)(2,1)} %get-tuple-element.84), channel_id=1, source_target_pairs={{0,1},{1,0},{2,3},{3,2},{4,5},{5,4},{6,7},{7,6},{8,9},{9,8},{10,11... | collective-permute-start | bytes 786440 | tf_op jit(solution)/shard_map/ppermute | solution.py:35
  128.9 21.6 %collective-permute-start.11 = (bf16[128,1024]{1,0:T(8,128)(2,1)}, bf16[128,1024]{1,0:T(8,128)(2,1)S(1)}, u32[]{:S(2)}, u32[]{:S(2)}) collective-permute-start(bf16[128,1024]{1,0:T(8,128)(2,1)} %get-tuple-element.85), channel_id=1, source_target_pairs={{0,5},{1,4},{4,1},{5,0},{2,7},{3,6},{6,3},{7,2},{8,13},{9,12},{12,... | collective-permute-start | bytes 786440 | tf_op jit(solution)/shard_map/ppermute | solution.py:51
  130.4 21.7 %collective-permute-start.10 = (bf16[128,1024]{1,0:T(8,128)(2,1)S(1)}, bf16[128,1024]{1,0:T(8,128)(2,1)S(1)}, u32[]{:S(2)}, u32[]{:S(2)}) collective-permute-start(bf16[128,1024]{1,0:T(8,128)(2,1)S(1)} %get-tuple-element.86), channel_id=1, source_target_pairs={{0,4},{4,0},{1,5},{5,1},{2,6},{6,2},{3,7},{7,3},{8,12},{12,8},{9,1... | collective-permute-start | bytes 786440 | tf_op jit(solution)/shard_map/ppermute | solution.py:35
  199.1 15.7 %collective-permute-start.31 = (bf16[128,1024]{1,0:T(8,128)(2,1)S(1)}, bf16[128,1024]{1,0:T(8,128)(2,1)S(1)}, u32[]{:S(2)}, u32[]{:S(2)}) collective-permute-start(bf16[128,1024]{1,0:T(8,128)(2,1)S(1)} %get-tuple-element.79), channel_id=1, source_target_pairs={{0,5},{1,4},{4,1},{5,0},{2,7},{3,6},{6,3},{7,2},{8,13},{9,12},{12,... | collective-permute-start | bytes 786440 | tf_op jit(solution)/shard_map/ppermute | solution.py:51
  200.0 18.0 %collective-permute-start.30 = (bf16[128,1024]{1,0:T(8,128)(2,1)S(1)}, bf16[128,1024]{1,0:T(8,128)(2,1)S(1)}, u32[]{:S(2)}, u32[]{:S(2)}) collective-permute-start(bf16[128,1024]{1,0:T(8,128)(2,1)S(1)} %get-tuple-element.80), channel_id=1, source_target_pairs={{0,4},{4,0},{1,5},{5,1},{2,6},{6,2},{3,7},{7,3},{8,12},{12,8},{9,1... | collective-permute-start | bytes 786440 | tf_op jit(solution)/shard_map/ppermute | solution.py:35
  201.8 28.8 %collective-permute-start.21 = (bf16[128,1024]{1,0:T(8,128)(2,1)S(1)}, bf16[128,1024]{1,0:T(8,128)(2,1)S(1)}, u32[]{:S(2)}, u32[]{:S(2)}) collective-permute-start(bf16[128,1024]{1,0:T(8,128)(2,1)S(1)} %get-tuple-element.81), channel_id=1, source_target_pairs={{0,1},{1,0},{2,3},{3,2},{4,5},{5,4},{6,7},{7,6},{8,9},{9,8},{10,11... | collective-permute-start | bytes 786440 | tf_op jit(solution)/shard_map/ppermute | solution.py:35
  203.3 27.3 %collective-permute-start.23 = (bf16[128,1024]{1,0:T(8,128)(2,1)S(1)}, bf16[128,1024]{1,0:T(8,128)(2,1)S(1)}, u32[]{:S(2)}, u32[]{:S(2)}) collective-permute-start(bf16[128,1024]{1,0:T(8,128)(2,1)S(1)} %get-tuple-element.82), channel_id=1, source_target_pairs={{0,5},{1,4},{4,1},{5,0},{2,7},{3,6},{6,3},{7,2},{8,13},{9,12},{12,... | collective-permute-start | bytes 786440 | tf_op jit(solution)/shard_map/ppermute | solution.py:51
  212.5 18.2 %collective-permute-start.22 = (bf16[128,1024]{1,0:T(8,128)(2,1)S(1)}, bf16[128,1024]{1,0:T(8,128)(2,1)S(1)}, u32[]{:S(2)}, u32[]{:S(2)}) collective-permute-start(bf16[128,1024]{1,0:T(8,128)(2,1)S(1)} %get-tuple-element.83), channel_id=1, source_target_pairs={{0,4},{4,0},{1,5},{5,1},{2,6},{6,2},{3,7},{7,3},{8,12},{12,8},{9,1... | collective-permute-start | bytes 786440 | tf_op jit(solution)/shard_map/ppermute | solution.py:35
  214.9 51.7 %collective-permute-start.44 = (bf16[96,1024]{1,0:T(8,128)(2,1)}, bf16[96,1024]{1,0:T(8,128)(2,1)}, u32[]{:S(2)}, u32[]{:S(2)}) collective-permute-start(bf16[96,1024]{1,0:T(8,128)(2,1)} %get-tuple-element.87), channel_id=1, source_target_pairs={{0,0},{1,4},{2,8},{3,12},{4,16},{5,20},{6,24},{7,28},{8,1},{9,5},{... | collective-permute-start | bytes 589832 | tf_op jit(solution)/shard_map/ppermute | solution.py:82
  218.0 48.6 %collective-permute-start.46 = (bf16[96,1024]{1,0:T(8,128)(2,1)}, bf16[96,1024]{1,0:T(8,128)(2,1)}, u32[]{:S(2)}, u32[]{:S(2)}) collective-permute-start(bf16[96,1024]{1,0:T(8,128)(2,1)} %get-tuple-element.88), channel_id=1, source_target_pairs={{0,2},{1,6},{2,10},{3,14},{4,18},{5,22},{6,26},{7,30},{8,3},{9,7},... | collective-permute-start | bytes 589832 | tf_op jit(solution)/shard_map/ppermute | solution.py:82
  239.2 18.1 %collective-permute-start.32 = (bf16[128,1024]{1,0:T(8,128)(2,1)S(1)}, bf16[128,1024]{1,0:T(8,128)(2,1)S(1)}, u32[]{:S(2)}, u32[]{:S(2)}) collective-permute-start(bf16[128,1024]{1,0:T(8,128)(2,1)S(1)} %get-tuple-element.34), channel_id=1, source_target_pairs={{0,1},{1,0},{2,3},{3,2},{4,5},{5,4},{6,7},{7,6},{8,9},{9,8},{10,11... | collective-permute-start | bytes 786440 | tf_op jit(solution)/shard_map/ppermute | solution.py:35
  246.5 20.1 %collective-permute-start.45 = (bf16[96,1024]{1,0:T(8,128)(2,1)}, bf16[96,1024]{1,0:T(8,128)(2,1)}, u32[]{:S(2)}, u32[]{:S(2)}) collective-permute-start(bf16[96,1024]{1,0:T(8,128)(2,1)} %get-tuple-element.89), channel_id=1, source_target_pairs={{0,1},{1,5},{2,9},{3,13},{4,17},{5,21},{6,25},{7,29},{8,2},{9,6},{... | collective-permute-start | bytes 589832 | tf_op jit(solution)/shard_map/ppermute | solution.py:82
  258.8 75.3 %all-to-all-start.3 = ((bf16[32,192,128]{2,1,0:T(8,128)(2,1)}), bf16[32,192,128]{2,1,0:T(8,128)(2,1)}, u32[]{:S(2)}, u32[]{:S(2)}) async-start(bf16[32,192,128]{2,1,0:T(8,128)(2,1)} %constant_dynamic-update-slice_fusion.31), calls=%async_computation.3 | async-start | bytes 3145728 | tf_op jit(solution)/shard_map/all_to_all | solution.py:58
  307.0 20.5 %collective-permute-start.40 = (bf16[64,1024]{1,0:T(8,128)(2,1)S(1)}, bf16[64,1024]{1,0:T(8,128)(2,1)S(1)}, u32[]{:S(2)}, u32[]{:S(2)}) collective-permute-start(bf16[64,1024]{1,0:T(8,128)(2,1)S(1)} %get-tuple-element.99), channel_id=1, source_target_pairs={{0,0},{1,4},{2,8},{3,12},{4,16},{5,20},{6,24},{7,28},{8,1},{9,5},{... | collective-permute-start | bytes 393224 | tf_op jit(solution)/shard_map/ppermute | solution.py:82
  307.7 25.6 %collective-permute-start.42 = (bf16[64,1024]{1,0:T(8,128)(2,1)S(1)}, bf16[64,1024]{1,0:T(8,128)(2,1)S(1)}, u32[]{:S(2)}, u32[]{:S(2)}) collective-permute-start(bf16[64,1024]{1,0:T(8,128)(2,1)S(1)} %get-tuple-element.100), channel_id=1, source_target_pairs={{0,2},{1,6},{2,10},{3,14},{4,18},{5,22},{6,26},{7,30},{8,3},{9,7},... | collective-permute-start | bytes 393224 | tf_op jit(solution)/shard_map/ppermute | solution.py:82
  310.8 22.5 %collective-permute-start.41 = (bf16[64,1024]{1,0:T(8,128)(2,1)S(1)}, bf16[64,1024]{1,0:T(8,128)(2,1)S(1)}, u32[]{:S(2)}, u32[]{:S(2)}) collective-permute-start(bf16[64,1024]{1,0:T(8,128)(2,1)S(1)} %get-tuple-element.101), channel_id=1, source_target_pairs={{0,1},{1,5},{2,9},{3,13},{4,17},{5,21},{6,25},{7,29},{8,2},{9,6},{... | collective-permute-start | bytes 393224 | tf_op jit(solution)/shard_map/ppermute | solution.py:82
  321.6 31.6 %collective-permute-start.36 = (bf16[4,128,1024]{2,1,0:T(8,128)(2,1)}, bf16[4,128,1024]{2,1,0:T(8,128)(2,1)}, u32[]{:S(2)}, u32[]{:S(2)}) collective-permute-start(bf16[4,128,1024]{2,1,0:T(8,128)(2,1)} %bitcast.107), channel_id=1, source_target_pairs={{0,2},{2,0},{1,3},{3,1},{4,6},{6,4},{5,7},{7,5},{8,10},{10,8},{9,1... | collective-permute-start | bytes 3145736 | tf_op jit(solution)/shard_map/ppermute | solution.py:35
  334.1 41.1 %all-to-all-start.2 = ((bf16[32,136,128]{2,1,0:T(8,128)(2,1)}), bf16[32,136,128]{2,1,0:T(8,128)(2,1)S(1)}, u32[]{:S(2)}, u32[]{:S(2)}) async-start(bf16[32,136,128]{2,1,0:T(8,128)(2,1)} %constant_dynamic-update-slice_fusion.26), calls=%async_computation.2 | async-start | bytes 2228224 | tf_op jit(solution)/shard_map/all_to_all | solution.py:58
  355.0 17.6 %collective-permute-start.37 = (bf16[128,1024]{1,0:T(8,128)(2,1)S(1)}, bf16[128,1024]{1,0:T(8,128)(2,1)S(1)}, u32[]{:S(2)}, u32[]{:S(2)}) collective-permute-start(bf16[128,1024]{1,0:T(8,128)(2,1)S(1)} %get-tuple-element.75), channel_id=1, source_target_pairs={{0,1},{1,0},{2,3},{3,2},{4,5},{5,4},{6,7},{7,6},{8,9},{9,8},{10,11... | collective-permute-start | bytes 786440 | tf_op jit(solution)/shard_map/ppermute | solution.py:35
  (77 other events, 516.2 us)

commit v2 on v1

v2 whole, which is shorter than its diff:
```python
import functools

import jax
import jax.numpy as jnp
import numpy as np
from jax import lax
from jax.experimental import pallas as pl
from jax.experimental.pallas import tpu as pltpu
from jax.sharding import Mesh, PartitionSpec as P

QUERY_HEADS = 16
KEY_VALUE_HEADS = 8
HEAD_SIZE = 128
GROUP = QUERY_HEADS // KEY_VALUE_HEADS
HEADS_WIDTH = GROUP * HEAD_SIZE

EPS = 1e-06
THETA = 1000000.0
SCALE = HEAD_SIZE ** (-0.5)
EXTRA_ROWS = 16

ALL = ("data", "x", "core", "seq")
BF = jnp.bfloat16
F32 = jnp.float32
SWAP = [(0, 1), (1, 0)]


def mm(a, b):
    return lax.dot_general(a, b, (((1,), (0,)), ((), ())), preferred_element_type=F32)


def mm_nt(a, b):
    return lax.dot_general(a, b, (((1,), (1,)), ((), ())), preferred_element_type=F32)


def mm_tn(a, b):
    return lax.dot_general(a, b, (((0,), (0,)), ((), ())), preferred_element_type=F32)


def together(*values):
    return lax.optimization_barrier(values)


def flip(value, axis):
    return lax.ppermute(value, axis, SWAP)


def flip_diagonal(value):
    return lax.ppermute(value, ("x", "seq"), [(i, i ^ 3) for i in range(4)])


def gather_chips(block):
    from_d = flip_diagonal(block)
    return jnp.stack([block, flip(block, "seq"), flip(block, "x"), from_d])


def exchange(own, to_y, to_x, to_d):
    from_d = flip_diagonal(to_d)
    return own, flip(to_y, "seq"), flip(to_x, "x"), from_d


def in_plane_all(payload):
    return lax.all_to_all(payload, ALL[1:], split_axis=0, concat_axis=0, tiled=True)


def to_row_place(block, count):
    route = [(count * j + d, d * 8 + j) for d in range(count) for j in range(8)]
    return lax.ppermute(block, ALL, route)


def doubling_orders(count):
    orders, bit = [[0]], count // 2
    while bit:
        orders.append([o ^ bit for order in orders for o in order])
        bit //= 2
    return orders


def across(value, bit):
    return lax.ppermute(value, "data", [(d, d ^ bit) for d in range(lax.axis_size("data"))])


def double(arrays, last=False):
    arrays, bit = list(arrays), lax.axis_size("data") // 2
    while bit > 1 and not last:
        arrays.append(across(jnp.concatenate(arrays), bit))
        bit //= 2
    if last:
        arrays.append(across(jnp.concatenate(arrays), 1))
    return arrays


def plane_sum(value, *axes):
    for axis in axes or ("core", "x", "seq"):
        value = value + flip(value, axis)
    return value


def data_sum(value, last=False):
    bit = lax.axis_size("data") // 2
    while bit > 1 and not last:
        value = value + across(value, bit)
        bit //= 2
    return value + across(value, 1) if last else value


def to_row_owner(block, count):
    route = [(d * 8 + j, count * j + d) for d in range(count) for j in range(8)]
    return lax.ppermute(block, ALL, route)


def spec(kind, shape, at):
    zeros = (0,) * (len(shape) - 1)
    if kind == "blocks":
        return pl.BlockSpec((2,) + shape[1:], lambda g: (g,) + zeros)
    if kind == "half":
        return pl.BlockSpec((shape[0] // 2,) + shape[1:], lambda g: (g,) + zeros)
    if kind == "group":
        return pl.BlockSpec((shape[0] // 4,) + shape[1:], lambda g: (at + g,) + zeros)
    if kind == "scalars":
        return pl.BlockSpec(memory_space=pltpu.SMEM)
    if kind == "kept":
        return pl.BlockSpec(memory_space=pl.ANY)
    return pl.BlockSpec(shape, lambda g: (0,) + zeros)


def call_half(kernel, which, outs, args, kept=(), scratch=()):
    at = 2 * which
    given = list(args) + [("kept", array) for array in kept]
    aliases = {len(args) + k: k for k in range(len(kept))}
    n_args = len(args)

    def body(*refs):
        kernel(*refs[:n_args], *refs[n_args + len(kept) :])

    return pl.pallas_call(
        body,
        grid=(2,),
        out_shape=tuple(jax.ShapeDtypeStruct(shape, dtype) for _, shape, dtype in outs),
        in_specs=[spec(kind, arg.shape, at) for kind, arg in given],
        out_specs=tuple(spec(kind, shape, at) for kind, shape, _ in outs),
        scratch_shapes=list(scratch),
        input_output_aliases=aliases,
        compiler_params=pltpu.CompilerParams(
            vmem_limit_bytes=24 * 2**20, dimension_semantics=("arbitrary",)
        ),
    )(*[arg for _, arg in given])


def call(kernel, outs, *args):
    vmem = pl.BlockSpec(memory_space=pltpu.VMEM)
    return pl.pallas_call(
        kernel,
        out_shape=tuple(jax.ShapeDtypeStruct(shape, dtype) for shape, dtype in outs),
        in_specs=[vmem for _ in args],
        out_specs=tuple(vmem for _ in outs),
        compiler_params=pltpu.CompilerParams(vmem_limit_bytes=12 * 2**20),
    )(*args)


def whole(*arrays):
    return [("whole", array) for array in arrays]


def pack_kernel(widths, *refs):
    *weights, out = refs
    for j in range(8):
        at = 0
        for width, ref in zip(widths, weights):
            out[j, :, at : at + width] = ref[:, j * width : (j + 1) * width]
            at += width


def pack(*weights):
    widths = [w.shape[1] // 8 for w in weights]
    shape = (8, weights[0].shape[0], sum(widths))
    return pl.pallas_call(
        functools.partial(pack_kernel, widths),
        grid=(1,),
        out_shape=jax.ShapeDtypeStruct(shape, BF),
        in_specs=[spec("whole", w.shape, 0) for w in weights],
        out_specs=spec("whole", shape, 0),
    )(*weights)


def copy_kernel(tokens, payload, out):
    out[...] = tokens[...]


def ordered_after(tokens, payload):
    vmem = pl.BlockSpec(memory_space=pltpu.VMEM)
    return pl.pallas_call(
        copy_kernel,
        out_shape=jax.ShapeDtypeStruct(tokens.shape, tokens.dtype),
        in_specs=[vmem, pl.BlockSpec(memory_space=pl.ANY)],
        out_specs=vmem,
    )(tokens, payload)


def marks_kernel(scalars, norm_gain, mlp_gain, query_gain, key_gain, lengths, seq_order, out):
    width = out.shape[1]

    def placed(ref, at):
        line = ref[...].astype(F32)
        line = jnp.concatenate([line, jnp.zeros((1, width - line.shape[1]), F32)], axis=1)
        return pltpu.roll(line, at * ref.shape[1], 1)

    lines = [placed(ref, scalars[2]) for ref in (norm_gain, mlp_gain, query_gain, key_gain)]
    once = (1 - scalars[1]).astype(F32)
    lines += [placed(ref, scalars[2] // 2) * once for ref in (lengths, seq_order)]
    lines.append(jnp.zeros((2, width), F32))
    out[...] = jnp.concatenate(lines, axis=0).astype(BF)


def make_marks(scalars, width, *values):
    vmem = pl.BlockSpec(memory_space=pltpu.VMEM)
    return pl.pallas_call(
        marks_kernel,
        out_shape=jax.ShapeDtypeStruct((8, width), BF),
        in_specs=[pl.BlockSpec(memory_space=pltpu.SMEM)] + [vmem for _ in values],
        out_specs=vmem,
    )(scalars, *values)


def setup_kernel(n_seq, scalars, marks, gain_in, gain_mid, head_gains, starts):
    rows = marks[...].astype(F32)
    gain_in[...] = rows[0:1]
    gain_mid[...] = rows[1:2]
    head_gains[...] = rows[2:4, :HEAD_SIZE]
    width = rows.shape[1]
    lane = lax.broadcasted_iota(jnp.int32, (1, 128), 1).astype(F32)
    for k, relative in enumerate((0, 2, 1, 3)):
        back = width - lax.bitwise_xor(scalars[2] // 2, relative) * n_seq
        lengths, order = [pltpu.roll(rows[q : q + 1], back, 1)[:, :128] for q in (4, 5)]
        at = jnp.zeros((1, 1), F32)
        for q in range(n_seq):
            starts[k, q : q + 1, :] = jnp.broadcast_to(at, (1, 128))
            mine = (lane == order[:, q : q + 1]) & (lane < n_seq)
            at = at + jnp.sum(jnp.where(mine, lengths, 0.0), axis=1, keepdims=True)
        starts[k, n_seq:, :] = jnp.full((8 - n_seq, 128), 1e9, F32)


def setup(scalars, marks, n_seq):
    width = marks.shape[1]
    outs = [((1, width), F32), ((1, width), F32), ((2, HEAD_SIZE), F32), ((4, 8, 128), F32)]
    vmem = pl.BlockSpec(memory_space=pltpu.VMEM)
    return pl.pallas_call(
        functools.partial(setup_kernel, n_seq),
        out_shape=tuple(jax.ShapeDtypeStruct(shape, dtype) for shape, dtype in outs),
        in_specs=[pl.BlockSpec(memory_space=pltpu.SMEM), vmem],
        out_specs=tuple(vmem for _ in outs),
    )(scalars, marks)


def assemble_kernel(orders, cuts, scalars, *refs):
    arrays, outs = refs[: len(orders)], refs[len(orders) :]
    for order, ref in zip(orders, arrays):
        for k, relative in enumerate(order):
            place, start = lax.bitwise_xor(scalars[0], relative), 0
            for size, out in zip(cuts, outs):
                at = pl.multiple_of(place * size, size)
                out[pl.ds(at, size), :] = ref[k, start : start + size, :]
                start += size


def assemble(arrays, scalars, *cuts):
    count = sum(array.shape[0] for array in arrays)
    orders = doubling_orders(count)
    _, size, width = arrays[0].shape
    cuts = cuts or (size,)
    if any(cut % 16 for cut in cuts):
        came = jnp.concatenate(arrays)
        at = jnp.asarray(np.argsort([o for order in orders for o in order]))
        came = came[at[jnp.arange(count) ^ scalars[0]]]
        ends = np.cumsum(cuts)
        return [came[:, b - a : b].reshape(count * a, width) for a, b in zip(cuts, ends)]
    vmem = pl.BlockSpec(memory_space=pltpu.VMEM)
    return pl.pallas_call(
        functools.partial(assemble_kernel, orders, cuts),
        out_shape=tuple(jax.ShapeDtypeStruct((count * cut, width), BF) for cut in cuts),
        in_specs=[pl.BlockSpec(memory_space=pltpu.SMEM)] + [vmem for _ in arrays],
        out_specs=tuple(vmem for _ in cuts),
    )(scalars, *arrays)


def unpack_kernel(widths, start, got, gain, *refs):
    weights, outs, gain_out = refs[: len(widths)], refs[len(widths) : -1], refs[-1]
    sums = 0.0
    for j in range(8):
        at = start
        for width, weight, out in zip(widths, weights, outs):
            piece = got[j, :, at : at + width].astype(F32)
            out[:, j * width : (j + 1) * width] = piece
            kept = weight[:, j * width : (j + 1) * width].astype(F32)
            sums = sums + jnp.sum(piece * kept, axis=1, keepdims=True)
            at += width
    gain_out[...] = sums / gain[...]


def unpack(got, start, gain, *weights):
    widths = [w.shape[1] // 8 for w in weights]
    outs = [(w.shape, F32) for w in weights] + [((gain.shape[0], 1), F32)]
    *grads, gain_grad = call(
        functools.partial(unpack_kernel, widths, start),
        outs,
        got,
        gain.astype(F32)[:, None],
        *weights,
    )
    return grads, gain_grad[:, 0]


def merge_kernel(near, other, own, to_y, to_x, to_d):
    own[...] = near[0] + other[0].astype(F32)
    for k, out in ((1, to_y), (2, to_x), (3, to_d)):
        out[...] = (near[k] + other[k].astype(F32)).astype(BF)


def merge(near, other):
    shape = near.shape[1:]
    return call(merge_kernel, [(shape, F32)] + [(shape, BF)] * 3, near, other)


def inv_rms(values):
    return lax.rsqrt(jnp.mean(values * values, axis=-1, keepdims=True) + EPS)


def summed(own, from_y, from_x, from_d, rows):
    total = own[:rows]
    for ref in (from_y, from_x, from_d):
        total = total + ref[:rows].astype(F32)
    return total


def hidden_kernel(tokens, own, from_y, from_x, from_d, gain, hidden, normed):
    total = tokens[...].astype(F32) + summed(own, from_y, from_x, from_d, tokens.shape[0])
    hidden[...] = total
    normed[...] = (total * inv_rms(total) * gain[...]).astype(BF)


def result_kernel(hidden, own, from_y, from_x, from_d, result):
    total = hidden[...] + summed(own, from_y, from_x, from_d, hidden.shape[0])
    result[...] = total.astype(BF)


def norm_pull_kernel(values, base, own, from_y, from_x, from_d, gain, out, *low):
    v = values[...].astype(F32)
    u = summed(own, from_y, from_x, from_d, v.shape[0]) * gain[...]
    r = inv_rms(v)
    total = base[...].astype(F32) + r * u - v * (r * r * r) * jnp.mean(u * v, -1, keepdims=True)
    out[...] = total
    for ref in low:
        ref[...] = total.astype(BF)


def turn(values, cosine, sine):
    return values * cosine + pltpu.roll(values, HEAD_SIZE // 2, 1) * sine


def turned_mask(starts, in_seq, rows):
    span = 2 * rows

    def ids(dim):
        shape = (span, 1) if dim == 0 else (1, span)
        at = lax.broadcasted_iota(jnp.int32, shape, dim)
        return lax.rem(at + in_seq * rows, span).astype(F32)

    def of_sequence(row_ids):
        return sum((row_ids >= starts[0, k : k + 1, 0:1]).astype(F32) for k in range(8))

    down, along = ids(0), ids(1)
    allowed = (along <= down) & (of_sequence(along) == of_sequence(down))
    return jnp.where(allowed, 0.0, -1e30).astype(F32)


def softmax(query, key, bias):
    scores = mm_nt(query, key) * SCALE + bias
    exp_scores = jnp.exp(scores - jnp.max(scores, axis=-1, keepdims=True))
    return exp_scores / jnp.sum(exp_scores, axis=-1, keepdims=True)


def group_of(blocks, start, rows):
    return jnp.concatenate([blocks[0, start : start + rows, :], blocks[1, start : start + rows, :]])


def split_out(product, rows, parts):
    for k in range(2):
        parts[k, :rows, :] = product[k * rows : (k + 1) * rows].astype(parts.dtype)


def attend_kernel(
    rows, scalars, starts, blocks, weight, gain, head_gains, cosine, sine, *outs
):
    normed, raw, low, attn = outs
    x = group_of(blocks, 0, rows).astype(F32)
    x = (x * inv_rms(x) * gain[...]).astype(BF)
    normed[...] = x
    qkv = mm(x, weight[...])
    raw[...] = qkv[:, : HEADS_WIDTH + HEAD_SIZE]
    cos, sin = cosine[...], sine[...]
    bias = turned_mask(starts, scalars[1], rows)
    heads = []
    for h in range(GROUP + 1):
        part = qkv[:, h * HEAD_SIZE : (h + 1) * HEAD_SIZE]
        norm = head_gains[0:1, :] if h < GROUP else head_gains[1:2, :]
        heads.append(turn(part * inv_rms(part) * norm, cos, sin).astype(BF))
        low[:, h * HEAD_SIZE : (h + 1) * HEAD_SIZE] = heads[-1]
    value = qkv[:, HEADS_WIDTH + HEAD_SIZE :].astype(BF)
    low[:, HEADS_WIDTH + HEAD_SIZE :] = value
    for h in range(GROUP):
        probs = softmax(heads[h], heads[GROUP], bias).astype(BF)
        attn[:, h * HEAD_SIZE : (h + 1) * HEAD_SIZE] = mm(probs, value).astype(BF)


def project_kernel(rows, values, weight, parts):
    split_out(mm(values[...], weight[...]), rows, parts)


def project(values, weight, rows):
    return [
        call_half(
            functools.partial(project_kernel, rows),
            which,
            [("blocks", (4, rows, weight.shape[1]), dtype)],
            [("group", values), ("whole", weight)],
        )[0]
        for which, dtype in ((0, F32), (1, BF))
    ]


def feed_kernel(rows, mid, cot, gate_up, down, normed, mixed, grad_gu, parts):
    ff = down.shape[0]
    x = group_of(mid, 0, rows)
    normed[...] = x
    both = mm(x, gate_up[...])
    gate_pre, upward = both[:, :ff], both[:, ff:]
    grad_mixed = mm_nt(group_of(cot, 0, rows), down[...])
    sigma = 1.0 / (1.0 + jnp.exp(-gate_pre))
    silu = gate_pre * sigma
    mixed[...] = (silu * upward).astype(BF)
    grad_gate = (grad_mixed * upward * sigma * (1.0 + gate_pre * (1.0 - sigma))).astype(BF)
    grad_up = (grad_mixed * silu).astype(BF)
    grad_gu[:, :ff] = grad_gate
    grad_gu[:, ff:] = grad_up
    split_out(mm_nt(grad_gu[...], gate_up[...]), rows, parts)


def attend_pull_kernel(
    rows, scalars, starts, blocks, low, raw, head_gains, cosine, sine, weight, grad_qkv, gain_out
):
    grad_attn = mm_nt(group_of(blocks, 0, rows), weight[...]).astype(BF)
    cos, sin = cosine[...], sine[...]
    bias = turned_mask(starts, scalars[1], rows)
    key = low[:, HEADS_WIDTH : HEADS_WIDTH + HEAD_SIZE]
    value = low[:, HEADS_WIDTH + HEAD_SIZE :]
    grads, grad_key, grad_value = [], 0.0, 0.0
    for h in range(GROUP):
        query = low[:, h * HEAD_SIZE : (h + 1) * HEAD_SIZE]
        probs = softmax(query, key, bias)
        grad = grad_attn[:, h * HEAD_SIZE : (h + 1) * HEAD_SIZE]
        grad_probs = mm_nt(grad, value)
        row_dot = jnp.sum(probs * grad_probs, axis=-1, keepdims=True)
        grad_scores = (probs * (grad_probs - row_dot)).astype(BF)
        grads.append(mm(grad_scores, key) * SCALE)
        grad_key = grad_key + mm_tn(grad_scores, query)
        grad_value = grad_value + mm_tn(probs.astype(BF), grad)
    grads.append(grad_key * SCALE)
    gain_sums = [0.0, 0.0]
    for h in range(GROUP + 1):
        spot = slice(h * HEAD_SIZE, (h + 1) * HEAD_SIZE)
        which = 0 if h < GROUP else 1
        back = turn(grads[h], cos, -sin)
        part = raw[:, spot]
        r = inv_rms(part)
        u = back * head_gains[which : which + 1, :]
        gain_sums[which] = gain_sums[which] + jnp.sum(back * part * r, axis=0, keepdims=True)
        pulled = r * u - part * (r * r * r) * jnp.mean(u * part, -1, keepdims=True)
        grad_qkv[:, spot] = pulled.astype(BF)
    grad_qkv[:, HEADS_WIDTH + HEAD_SIZE :] = grad_value.astype(BF)
    sums = jnp.concatenate(gain_sums, axis=1)

    @pl.when(pl.program_id(0) == 0)
    def _():
        gain_out[...] = sums

    @pl.when(pl.program_id(0) > 0)
    def _():
        gain_out[...] += sums


def project_nt_kernel(rows, grad_qkv, weight, parts):
    split_out(mm_nt(grad_qkv[...], weight[...]), rows, parts)


def weigh_kernel(orders, scalars, values, *refs):
    *grads, extra, keep, send, total = refs
    if len(grads) == 1:
        grad = grads[0][...]
    else:
        near, far = [ref[...].reshape(-1, ref.shape[2]) for ref in grads]
        grad = jnp.where(pl.program_id(0) < 2, near, far)
    term = mm_tn(values[...], grad)

    @pl.when(pl.program_id(0) == 0)
    def _():
        total[...] = term

    @pl.when(pl.program_id(0) > 0)
    def _():
        total[...] += term

    size = total.shape[0] // (2 * keep.shape[0])
    more = keep.shape[1] - size

    @pl.when(pl.program_id(0) == pl.num_programs(0) - 1)
    def _():
        for order, out in zip(orders, (keep, send)):
            for k, relative in enumerate(order):
                at = lax.bitwise_xor(scalars[0], relative) * size
                block = total[pl.ds(pl.multiple_of(at, size), size), :]
                if not more:
                    out[k] = block.astype(out.dtype)
                    continue
                line = extra[...]
                rest = total.shape[1] - line.shape[1]
                line = jnp.concatenate([line, jnp.zeros((1, rest), F32)], axis=1)
                line = jnp.broadcast_to(line, (more, total.shape[1]))
                out[k] = jnp.concatenate([block, line], axis=0).astype(out.dtype)


def weigh(values, grads, scalars, count, extra=None):
    more = 0 if extra is None else EXTRA_ROWS
    extra = jnp.zeros((1, 128), F32) if extra is None else extra
    bits = [1 << k for k in range(1, count.bit_length() - 1)]
    evens = [o for o in range(count) if not o & 1]
    evens = sorted(evens, key=lambda o: [bool(o & bit) for bit in bits])
    orders = (evens, [o ^ 1 for o in evens])
    height, width = values.shape[1], grads[0].shape[-1]
    half = (count // 2, height // count + more, width)
    if len(grads) == 1:
        grad_specs = [spec("group", grads[0].shape, 0)]
    else:
        block = (2,) + grads[0].shape[1:]
        grad_specs = [
            pl.BlockSpec(block, lambda g: (jnp.minimum(g, 1), 0, 0)),
            pl.BlockSpec(block, lambda g: (jnp.maximum(g - 2, 0), 0, 0)),
        ]
    return pl.pallas_call(
        functools.partial(weigh_kernel, orders),
        grid=(4,),
        out_shape=(jax.ShapeDtypeStruct(half, F32), jax.ShapeDtypeStruct(half, BF)),
        in_specs=[spec("scalars", (), 0), spec("group", values.shape, 0)]
        + grad_specs
        + [spec("whole", extra.shape, 0)],
        out_specs=(spec("whole", half, 0), spec("whole", half, 0)),
        scratch_shapes=[pltpu.VMEM((height, width), F32)],
        compiler_params=pltpu.CompilerParams(
            vmem_limit_bytes=24 * 2**20, dimension_semantics=("arbitrary",)
        ),
    )(scalars, values, *grads, extra)


def add_kernel(keep, got, kept, send):
    total = keep[...] + got[...].astype(F32)
    size = kept.shape[0]
    kept[...] = total[:size]
    send[...] = total[size:].astype(BF)


def halve_on(keep, got):
    bit = 2
    while keep.shape[0] > 1:
        part = (keep.shape[0] // 2,) + keep.shape[1:]
        keep, send = call(add_kernel, [(part, F32), (part, BF)], keep, got)
        got = across(send, bit)
        bit *= 2
    return keep, got


def finish_kernel(*refs):
    *terms, out, line = refs
    rows, at = out.shape[0], 0
    for keep, got in zip(terms[::2], terms[1::2]):
        total = keep[0, :rows, :] + got[0, :rows, :].astype(F32)
        out[:, at : at + total.shape[1]] = total.astype(BF)
        at += total.shape[1]
    keep, got = terms[:2]
    line[...] = (keep[0, rows : rows + 8, :] + got[0, rows : rows + 8, :].astype(F32))[:, : 2 * HEAD_SIZE]


def finish(rows, *terms):
    shape = (rows, sum(term.shape[2] for term in terms[::2]))
    outs = [(shape, BF), ((8, 2 * HEAD_SIZE), F32)]
    return call(finish_kernel, outs, *terms)


def finish_rows_kernel(*refs):
    *terms, out = refs
    at = 0
    for keep, got in zip(terms[::2], terms[1::2]):
        total = (keep[0] + got[0].astype(F32)).astype(BF)
        out[at : at + total.shape[0], :] = total
        at += total.shape[0]


def finish_rows(*terms):
    shape = (sum(term.shape[1] for term in terms[::2]), terms[0].shape[2])
    return call(finish_rows_kernel, [(shape, BF)], *terms)[0]


def local(
    tokens,
    norm_gain,
    w_query,
    w_key,
    w_value,
    w_output,
    query_gain,
    key_gain,
    mlp_gain,
    w_gate,
    w_up,
    w_down,
    lengths,
    seq_order,
    cotangent,
):
    rows, width = tokens.shape
    count = lax.axis_size("data")
    place = lax.axis_index("data")
    in_seq = lax.axis_index("seq")
    in_plane = lax.axis_index("x") * 4 + lax.axis_index("core") * 2 + in_seq
    w_rows = w_query.shape[0]
    gains = query_gain.shape[0]
    n_seq = lengths.shape[1]
    plane_rows = 8 * rows
    me = place * 8 + in_plane
    scalars = jnp.stack([place, in_seq, me]).astype(jnp.int32)

    half = HEAD_SIZE // 2
    angles = np.arange(2 * rows)[:, None] * THETA ** (-np.arange(half) * (2.0 / HEAD_SIZE))
    turns = np.stack(
        [np.tile(np.cos(angles), 2), np.concatenate([-np.sin(angles), np.sin(angles)], axis=1)]
    ).astype(np.float32)
    turns = jnp.asarray(np.stack([turns, np.roll(turns, -rows, axis=1)]))
    turns = lax.dynamic_index_in_dim(turns, in_seq, 0, False)
    cosine, sine = turns[0], turns[1]

    payload = pack(w_query, w_key, w_value, w_gate, w_up)
    marks = make_marks(
        scalars, width,
        norm_gain[None], mlp_gain[None], query_gain[None], key_gain[None], lengths, seq_order,
    )
    got = in_plane_all(payload).reshape(8 * w_rows, -1)
    marks = plane_sum(data_sum(data_sum(marks), last=True), "core")
    near = gather_chips(ordered_after(tokens, payload))
    row_weights = to_row_place(jnp.concatenate([w_output, w_down]), count)
    got, marks, near, row_weights, cot = together(got, marks, near, row_weights, cotangent)

    qkv = double([got[None, :, : 4 * HEAD_SIZE]])
    gate_up = got[None, :, 4 * HEAD_SIZE :]
    marks = plane_sum(marks, "x", "seq")
    far = flip(near, "core")
    qkv, marks, near, far, row_weights, gate_up, cot = together(
        qkv, marks, near, far, row_weights, gate_up, cot
    )

    qkv = double(qkv, last=True)
    row_weights = double([row_weights[None]])
    cot_near = gather_chips(cot)
    gain_in, gain_mid, head_gains, starts = setup(scalars, marks, n_seq)
    qkv, gain_in, near, far, row_weights, gate_up, cot_near = together(
        qkv, gain_in, near, far, row_weights, gate_up, cot_near
    )

    cot_far = flip(cot_near, "core")
    qkv_full = assemble(qkv, scalars)[0]
    kept = ()
    for which, blocks in enumerate((near, far)):
        kept = call_half(
            functools.partial(attend_kernel, rows),
            which,
            [
                ("group", (plane_rows, width), BF),
                ("group", (plane_rows, HEADS_WIDTH + HEAD_SIZE), F32),
                ("group", (plane_rows, 4 * HEAD_SIZE), BF),
                ("group", (plane_rows, HEADS_WIDTH), BF),
            ],
            [("scalars", scalars), ("group", starts), ("blocks", blocks)]
            + whole(qkv_full, gain_in, head_gains, cosine, sine),
            kept=kept,
        )
    normed_in, raw, low, attn_low = kept
    row_weights = double(row_weights, last=True)
    gate_up = double([gate_up])
    attn_low, row_weights = together(attn_low, row_weights)

    out_full, down_full = assemble(row_weights, scalars, w_output.shape[0], w_down.shape[0])
    ff = down_full.shape[0]
    part_near, part_far = project(attn_low, out_full, rows)
    sums = exchange(*merge(part_near, flip(part_far, "core")))
    gate_up = double(gate_up, last=True)
    sums, gate_up = together(sums, gate_up)

    hidden, normed_mid = call(
        hidden_kernel, [((rows, width), F32), ((rows, width), BF)], tokens, *sums, gain_mid
    )
    mid_near = gather_chips(normed_mid)
    gu_full = assemble(gate_up, scalars)[0]
    mid_near, gu_full = together(mid_near, gu_full)
    u_parts, kept = [], ()
    mid_far = flip(mid_near, "core")
    for which, mid, cot, dtype in (
        (0, mid_near, cot_near, F32),
        (1, mid_far, cot_far, BF),
    ):
        *kept, u_part = call_half(
            functools.partial(feed_kernel, rows),
            which,
            [
                ("group", (plane_rows, width), BF),
                ("group", (plane_rows, ff), BF),
                ("group", (plane_rows, 2 * ff), BF),
                ("blocks", (4, rows, width), dtype),
            ],
            [("blocks", mid), ("blocks", cot)] + whole(gu_full, down_full),
            kept=kept,
        )
        u_parts.append(u_part)
    mid_all, mixed, grad_gu = kept
    sums = exchange(*merge(u_parts[0], flip(u_parts[1], "core")))
    gu_keep, gu_send = weigh(mid_all, [grad_gu], scalars, count)
    down_keep, down_send = weigh(mixed, [cot_near, cot_far], scalars, count)
    result_near, result_far = project(mixed, down_full, rows)
    sums, result_near, result_far, gu_send, down_send = together(
        sums, result_near, result_far, gu_send, down_send
    )

    grad_hidden, grad_out = call(
        norm_pull_kernel,
        [((rows, width), F32), ((rows, width), BF)],
        hidden, cotangent, *sums, gain_mid,
    )
    out_near = gather_chips(grad_out)
    gu_got = across(gu_send, 1)
    down_got = across(down_send, 1)
    out_near, gu_keep, gu_got = together(out_near, gu_keep, gu_got)

    out_far = flip(out_near, "core")
    result_parts = merge(result_near, flip(result_far, "core"))
    gu_keep, gu_got = halve_on(gu_keep, gu_got)
    gain_parts, kept = [], ()
    for which, blocks in enumerate((out_near, out_far)):
        *kept, gain_part = call_half(
            functools.partial(attend_pull_kernel, rows),
            which,
            [
                ("group", (plane_rows, 4 * HEAD_SIZE), BF),
                ("whole", (1, 2 * HEAD_SIZE), F32),
            ],
            [("scalars", scalars), ("group", starts), ("blocks", blocks)]
            + [("group", low), ("group", raw)]
            + whole(head_gains, cosine, sine, out_full),
            kept=kept,
        )
        gain_parts.append(gain_part)
    grad_qkv = kept[0]
    gains_sum = gain_parts[0] + gain_parts[1]
    out_keep, out_send = weigh(attn_low, [out_near, out_far], scalars, count)
    out_got = across(out_send, 1)
    grad_qkv, gains_sum, result_parts, gu_keep, gu_got, down_keep, down_got, out_keep, out_got = together(
        grad_qkv, gains_sum, result_parts, gu_keep, gu_got, down_keep, down_got, out_keep, out_got
    )

    qkv_keep, qkv_send = weigh(normed_in, [grad_qkv], scalars, count, gains_sum)
    qkv_got = across(qkv_send, 1)
    part_near, part_far = [
        call_half(
            functools.partial(project_nt_kernel, rows),
            which,
            [("blocks", (4, rows, width), dtype)],
            [("group", grad_qkv)] + whole(qkv_full),
        )[0]
        for which, dtype in ((0, F32), (1, BF))
    ]
    sums = exchange(*merge(part_near, flip(part_far, "core")))
    down_keep, down_got = halve_on(down_keep, down_got)
    qkv_keep, qkv_got, out_keep, out_got, result_parts = together(
        qkv_keep, qkv_got, out_keep, out_got, result_parts
    )

    qkv_keep, qkv_got = halve_on(qkv_keep, qkv_got)
    out_keep, out_got = halve_on(out_keep, out_got)
    grad_tokens = call(
        norm_pull_kernel, [((rows, width), F32)], tokens, grad_hidden, *sums, gain_in
    )[0]
    result_sums = exchange(*result_parts)
    qkv_keep, qkv_got, out_keep, out_got, down_keep, down_got, grad_tokens = together(
        qkv_keep, qkv_got, out_keep, out_got, down_keep, down_got, grad_tokens
    )

    got, gains_sum = finish(8 * w_rows, qkv_keep, qkv_got, gu_keep, gu_got)
    got = in_plane_all(got.reshape(8, w_rows, got.shape[1]))
    row_grads = to_row_owner(finish_rows(out_keep, out_got, down_keep, down_got), count)
    gains_sum = plane_sum(gains_sum)
    result = call(result_kernel, [((rows, width), BF)], hidden, *result_sums)[0]
    me = me * gains
    grad_query_gain = lax.dynamic_slice_in_dim(gains_sum[0, :HEAD_SIZE], me, gains)
    grad_key_gain = lax.dynamic_slice_in_dim(gains_sum[0, HEAD_SIZE:], me, gains)
    row_grads = row_grads.astype(F32)
    (grad_w_query, grad_w_key, grad_w_value), grad_norm_gain = unpack(
        got, 0, norm_gain, w_query, w_key, w_value
    )
    (grad_w_gate, grad_w_up), grad_mlp_gain = unpack(got, 4 * HEAD_SIZE, mlp_gain, w_gate, w_up)
    out_rows = w_output.shape[0]
    return (
        result,
        grad_tokens,
        grad_norm_gain,
        grad_w_query,
        grad_w_key,
        grad_w_value,
        row_grads[:out_rows],
        grad_query_gain,
        grad_key_gain,
        grad_mlp_gain,
        grad_w_gate,
        grad_w_up,
        row_grads[out_rows:],
    )


def solution(mesh):
    fsdp, seq = mesh.shape["fsdp"], mesh.shape["seq"]
    fine = Mesh(np.asarray(mesh.devices).reshape(fsdp // 4, 2, 2, seq), ALL)
    matrix, vector, group = P(ALL, None), P(ALL), P(ALL[:3], None)
    placed = (
        matrix, vector, matrix, matrix, matrix, matrix, vector, vector, vector,
        matrix, matrix, matrix, group, group, matrix,
    )
    outs = (
        matrix, matrix, vector, matrix, matrix, matrix, matrix, vector, vector, vector,
        matrix, matrix, matrix,
    )
    return jax.shard_map(local, mesh=fine, in_specs=placed, out_specs=outs, check_vma=False)
```

time: 385 us -> 317 us (0.82)
  the two profiles are of different devices: /device:TPU:0 before, /device:TPU:2 now
where the time goes in v2:
time: 317 us; the launch traced here: 316 us
  waiting for transfers between devices  153 us (48%)
  starting transfers between devices  69.9 us (22%)
  Pallas kernels  66.9 us (21%)
  local copies, waits for them, and re-layouts  13.7 us (4%)
  other arithmetic  11.2 us (4%)
    ppermute x16, waiting for transfers between devices, across(): lax.ppermute(value, 'data', [(d, d ^ bit) for d in range(lax.axis_size('d...  78.4 us
    ppermute x30, waiting for transfers between devices, flip(): return lax.ppermute(value, axis, SWAP)  39.2 us
    pallas_call x12, Pallas kernels, call_half(): pl.pallas_call(body, grid=(2,), out_shape=tuple((jax.ShapeDtypeStruct(sha...  29.3 us
    ppermute x30, starting transfers between devices, flip(): return lax.ppermute(value, axis, SWAP)  23.5 us
    ppermute x16, starting transfers between devices, across(): lax.ppermute(value, 'data', [(d, d ^ bit) for d in range(lax.axis_size('d...  20.2 us
    ppermute x8, waiting for transfers between devices, flip_diagonal(): return lax.ppermute(value, ('x', 'seq'), [(i, i ^ 3) for i in range(4)])  17.9 us
    ppermute x1, waiting for transfers between devices, to_row_owner(): return lax.ppermute(block, ALL, route)  17.2 us
    pallas_call x4, Pallas kernels, weigh(): pl.pallas_call(functools.partial(weigh_kernel, orders), grid=(4,), out_sh...  14.2 us
  transfers between devices with their start and end apart: 58, of which 34 were waited for; matrix products, arithmetic and copies ran while one was open for 3% of the time, Pallas kernels for 18%

profile of v2, /device:TPU:2, one launch (start us, length us, event | category | flops | bytes accessed | tf_op | source)
XLA Modules:
  0.0 315.9 jit_solution(17715962437618532747)
XLA Ops:
  2.8 4.3 %all-to-all-start = ((bf16[8,32,1280]{2,1,0:T(8,128)(2,1)}), bf16[8,32,1280]{2,1,0:T(8,128)(2,1)S(1)}, u32[]{:S(2)}, u32[]{:S(2)}) async-start(bf16[8,32,1280]{2,1,0:T(8,128)(2,1)} %shard_map.255.payload), calls=%async_computation | async-start | bytes 1310720 | tf_op jit(solution)/shard_map/all_to_all | solution.py:63
  12.2 3.4 %collective-permute-start.6 = (bf16[160,1024]{1,0:T(8,128)(2,1)S(1)}, bf16[160,1024]{1,0:T(8,128)(2,1)}, u32[]{:S(2)}, u32[]{:S(2)}) collective-permute-start(bf16[160,1024]{1,0:T(8,128)(2,1)S(1)} %pad_maximum_fusion.7), channel_id=1, source_target_pairs={{0,0},{4,1},{8,2},{12,3},{16,4},{20,5},{24,6},{28,7},{1,8},{5,9},{... | collective-permute-start | bytes 983048 | tf_op jit(solution)/shard_map/ppermute | solution.py:68
  20.1 7.1 %collective-permute-done = bf16[8,1024]{1,0:T(8,128)(2,1)S(1)} collective-permute-done((bf16[8,1024]{1,0:T(8,128)(2,1)}, bf16[8,1024]{1,0:T(8,128)(2,1)S(1)}, u32[]{:S(2)}, u32[]{:S(2)}) %collective-permute-start) | collective-permute-done | bytes 16416 | tf_op jit(solution)/shard_map/ppermute | solution.py:80
  27.9 3.7 %collective-permute-done.1 = bf16[8,1024]{1,0:T(8,128)(2,1)S(1)} collective-permute-done((bf16[8,1024]{1,0:T(8,128)(2,1)S(1)}, bf16[8,1024]{1,0:T(8,128)(2,1)S(1)}, u32[]{:S(2)}, u32[]{:S(2)}) %collective-permute-start.1) | collective-permute-done | bytes 16416 | tf_op jit(solution)/shard_map/ppermute | solution.py:80
  45.7 5.0 %collective-permute-done.7.refs_1_ = bf16[1,256,512]{2,1,0:T(8,128)(2,1)S(1)} collective-permute-done((bf16[1,256,512]{2,1,0:T(8,128)(2,1)S(1)}, bf16[1,256,512]{2,1,0:T(8,128)(2,1)S(1)}, u32[]{:S(2)}, u32[]{:S(2)}) %collective-permute-start.7) | collective-permute-done | bytes 262176 | tf_op jit(solution)/shard_map/ppermute | solution.py:80
  56.2 3.4 %collective-permute-start.12 = (bf16[1,160,1024]{2,1,0:T(8,128)(2,1)}, bf16[1,160,1024]{2,1,0:T(8,128)(2,1)S(1)}, u32[]{:S(2)}, u32[]{:S(2)}) collective-permute-start(bf16[1,160,1024]{2,1,0:T(8,128)(2,1)} %bitcast.14.refs_0_), channel_id=1, source_target_pairs={{0,16},{8,24},{16,0},{24,8},{1,17},{9,25},{17,1},{25,9},{2,18},{10... | collective-permute-start | bytes 983048 | tf_op jit(solution)/shard_map/ppermute | solution.py:80
  62.8 4.0 %collective-permute-done.14 = bf16[128,1024]{1,0:T(8,128)(2,1)} collective-permute-done((bf16[128,1024]{1,0:T(8,128)(2,1)S(1)}, bf16[128,1024]{1,0:T(8,128)(2,1)}, u32[]{:S(2)}, u32[]{:S(2)}) %collective-permute-start.14) | collective-permute-done | bytes 262176 | tf_op jit(solution)/shard_map/ppermute | solution.py:45
  84.8 4.0 %shard_map.260 = (bf16[1024,1024]{1,0:T(8,128)(2,1)S(1)}, f32[1024,384]{1,0:T(8,128)S(1)}, bf16[1024,512]{1,0:T(8,128)(2,1)S(1)}, bf16[1024,256]{1,0:T(8,128)(2,1)S(1)}) custom-call(s32[3]{0:T(128)S(1)} %copy-done.36, f32[4,8,128]{2,1,0:T(8,128)S(1)} %copy-done.29, bf16[4,128,1024]{2,1,0:T(8,128)(2,1)S(1)} %copy-done.13, bf16[1024,512]{1,0:T(8,128)(2,1)S(1)} %copy-done, ...), custom_call_target="tpu_custom_call" | custom-call | tf_op jit(solution)/shard_map/pallas_call | solution.py:136
  90.1 4.0 %shard_map.261 = (bf16[1024,1024]{1,0:T(8,128)(2,1)S(1)}, f32[1024,384]{1,0:T(8,128)S(1)}, bf16[1024,512]{1,0:T(8,128)(2,1)S(1)}, bf16[1024,256]{1,0:T(8,128)(2,1)S(1)}) custom-call(s32[3]{0:T(128)S(1)} %copy-done.36, f32[4,8,128]{2,1,0:T(8,128)S(1)} %copy-done.29, ...), custom_call_target="tpu_custom_call", output_to_operand_aliasing={{0}: (8, {}), {1}: (9, {}), {2}: (10, {}), {3}: (11, {})} | custom-call | tf_op jit(solution)/shard_map/pallas_call | solution.py:136
  96.5 3.9 %collective-permute-done.16.refs_2_ = bf16[2,160,1024]{2,1,0:T(8,128)(2,1)} collective-permute-done((bf16[2,160,1024]{2,1,0:T(8,128)(2,1)}, bf16[2,160,1024]{2,1,0:T(8,128)(2,1)}, u32[]{:S(2)}, u32[]{:S(2)}) %collective-permute-start.16) | collective-permute-done | bytes 655392 | tf_op jit(solution)/shard_map/ppermute | solution.py:80
  111.4 14.4 %collective-permute-done.22.refs_2_ = bf16[2,256,768]{2,1,0:T(8,128)(2,1)S(1)} collective-permute-done((bf16[2,256,768]{2,1,0:T(8,128)(2,1)S(1)}, bf16[2,256,768]{2,1,0:T(8,128)(2,1)S(1)}, u32[]{:S(2)}, u32[]{:S(2)}) %collective-permute-start.22) | collective-permute-done | bytes 786464 | tf_op jit(solution)/shard_map/ppermute | solution.py:80
  134.1 3.9 %collective-permute-done.25 = bf16[128,1024]{1,0:T(8,128)(2,1)} collective-permute-done((bf16[128,1024]{1,0:T(8,128)(2,1)}, bf16[128,1024]{1,0:T(8,128)(2,1)}, u32[]{:S(2)}, u32[]{:S(2)}) %collective-permute-start.25) | collective-permute-done | bytes 262176 | tf_op jit(solution)/shard_map/ppermute | solution.py:49
  138.0 4.2 %collective-permute-done.24 = bf16[128,1024]{1,0:T(8,128)(2,1)} collective-permute-done((bf16[128,1024]{1,0:T(8,128)(2,1)}, bf16[128,1024]{1,0:T(8,128)(2,1)}, u32[]{:S(2)}, u32[]{:S(2)}) %collective-permute-start.24) | collective-permute-done | bytes 262176 | tf_op jit(solution)/shard_map/ppermute | solution.py:45
  143.7 3.4 %shard_map.268 = (bf16[1024,1024]{1,0:T(8,128)(2,1)S(1)}, bf16[1024,384]{1,0:T(8,128)(2,1)S(1)}, bf16[1024,768]{1,0:T(8,128)(2,1)S(1)}, f32[4,128,1024]{2,1,0:T(8,128)S(1)}) custom-call(bf16[4,128,1024]{2,1,0:T(8,128)(2,1)S(1)} %pad_maximum_fusion.2.refs_0_, bf16[4,128,1024]{2,1,0:T(8,128)(2,1)S(1)} %pad_maximum_fusion.1.refs_1_.refs_0_, ...), custom_call_target="tpu_custom_call" | custom-call | tf_op jit(solution)/shard_map/pallas_call | solution.py:136
  147.1 4.5 %shard_map.269 = (bf16[1024,1024]{1,0:T(8,128)(2,1)S(1)}, bf16[1024,384]{1,0:T(8,128)(2,1)S(1)}, bf16[1024,768]{1,0:T(8,128)(2,1)S(1)}, bf16[4,128,1024]{2,1,0:T(8,128)(2,1)S(1)}) custom-call(bf16[4,128,1024]{2,1,0:T(8,128)(2,1)S(1)} %collective-permute-done.26.refs_0_, ...), custom_call_target="tpu_custom_call", output_to_operand_aliasing={{0}: (4, {}), {1}: (5, {}), {2}: (6, {})} | custom-call | tf_op jit(solution)/shard_map/pallas_call | solution.py:136
  160.4 4.4 %shard_map.273 = (f32[2,256,768]{2,1,0:T(8,128)S(1)}, bf16[2,256,768]{2,1,0:T(8,128)(2,1)S(1)}) custom-call(s32[3]{0:T(128)S(1)} %copy-done.37, bf16[1024,1024]{1,0:T(8,128)(2,1)S(1)} %get-tuple-element.222.values, bf16[1024,768]{1,0:T(8,128)(2,1)S(1)} %get-tuple-element.223.refs_0_, f32[1,128]{1,0:T(1,128)S(1)} %broadcast_1_refs_1__refs_2_.2.refs_1_.refs_2_), custom_call_target="tpu_custom_call" | custom-call | tf_op jit(solution)/shard_map/pallas_call | solution.py:548
  164.9 3.9 %shard_map.274 = (f32[2,96,1024]{2,1,0:T(8,128)S(1)}, bf16[2,96,1024]{2,1,0:T(8,128)(2,1)S(1)}) custom-call(s32[3]{0:T(128)S(1)} %copy-done.37, bf16[1024,384]{1,0:T(8,128)(2,1)S(1)} %get-tuple-element.221.refs_0_.values, bf16[4,128,1024]{2,1,0:T(8,128)(2,1)S(1)} %pad_maximum_fusion.1.refs_1_.refs_0_, bf16[4,128,1024]{2,1,0:T(8,128)(2,1)} %collective-permute-done.27.refs_1_, ...), custom_call_target="tpu_custom_call" | custom-call | tf_op jit(solution)/shard_map/pallas_call | solution.py:548
  175.2 6.7 %collective-permute-done.34 = bf16[128,1024]{1,0:T(8,128)(2,1)S(1)} collective-permute-done((bf16[128,1024]{1,0:T(8,128)(2,1)S(1)}, bf16[128,1024]{1,0:T(8,128)(2,1)S(1)}, u32[]{:S(2)}, u32[]{:S(2)}) %collective-permute-start.34) | collective-permute-done | bytes 262176 | tf_op jit(solution)/shard_map/ppermute | solution.py:49
  181.8 2.7 collective-permute-done.33
  185.8 4.0 %collective-permute-done.35.got = bf16[2,256,768]{2,1,0:T(8,128)(2,1)S(1)} collective-permute-done((bf16[2,256,768]{2,1,0:T(8,128)(2,1)S(1)}, bf16[2,256,768]{2,1,0:T(8,128)(2,1)S(1)}, u32[]{:S(2)}, u32[]{:S(2)}) %collective-permute-start.35) | collective-permute-done | bytes 786464 | tf_op jit(solution)/shard_map/ppermute | solution.py:80
  196.6 4.2 %shard_map.276 = (bf16[1024,512]{1,0:T(8,128)(2,1)S(1)}, f32[1,256]{1,0:T(1,128)S(1)}) custom-call(s32[3]{0:T(128)S(1)} %copy-done.37, f32[4,8,128]{2,1,0:T(8,128)S(1)} %copy-done.29, bf16[4,128,1024]{2,1,0:T(8,128)(2,1)S(1)} %pad_maximum_fusion.3.refs_2_.refs_0_, bf16[1024,512]{1,0:T(8,128)(2,1)S(1)} %copy-done.5, ...), custom_call_target="tpu_custom_call" | custom-call | tf_op jit(solution)/shard_map/pallas_call | solution.py:136
  201.8 4.2 %shard_map.277 = (bf16[1024,512]{1,0:T(8,128)(2,1)S(1)}, f32[1,256]{1,0:T(1,128)S(1)}) custom-call(s32[3]{0:T(128)S(1)} %copy-done.37, f32[4,8,128]{2,1,0:T(8,128)S(1)} %copy-done.29, bf16[4,128,1024]{2,1,0:T(8,128)(2,1)S(1)} %collective-permute-done.36.refs_2_.refs_1_, bf16[1024,512]{1,0:T(8,128)(2,1)S(1)} %copy-done.5, ...), custom_call_target="tpu_custom_call", output_to_operand_aliasing={{0}: (9, {})} | custom-call | tf_op jit(solution)/shard_map/pallas_call | solution.py:136
  206.1 4.4 %collective-permute-done.39.got = bf16[2,96,1024]{2,1,0:T(8,128)(2,1)S(1)} collective-permute-done((bf16[2,96,1024]{2,1,0:T(8,128)(2,1)S(1)}, bf16[2,96,1024]{2,1,0:T(8,128)(2,1)S(1)}, u32[]{:S(2)}, u32[]{:S(2)}) %collective-permute-start.39) | collective-permute-done | bytes 393248 | tf_op jit(solution)/shard_map/ppermute | solution.py:80
  211.0 4.5 %collective-permute-done.40.got = bf16[2,64,1024]{2,1,0:T(8,128)(2,1)S(1)} collective-permute-done((bf16[2,64,1024]{2,1,0:T(8,128)(2,1)S(1)}, bf16[2,64,1024]{2,1,0:T(8,128)(2,1)S(1)}, u32[]{:S(2)}, u32[]{:S(2)}) %collective-permute-start.40) | collective-permute-done | bytes 262176 | tf_op jit(solution)/shard_map/ppermute | solution.py:80
  216.6 3.3 %shard_map.281 = (f32[2,272,512]{2,1,0:T(8,128)S(1)}, bf16[2,272,512]{2,1,0:T(8,128)(2,1)S(1)}) custom-call(s32[3]{0:T(128)S(1)} %copy-done.37, bf16[1024,1024]{1,0:T(8,128)(2,1)S(1)} %copy-done.7, bf16[1024,512]{1,0:T(8,128)(2,1)S(1)} %get-tuple-element.254.refs_0_, f32[1,256]{1,0:T(1,128)S(1)} %add.53.refs_1_), custom_call_target="tpu_custom_call" | custom-call | tf_op jit(solution)/shard_map/pallas_call | solution.py:548
  222.1 12.9 %collective-permute-done.41.got = bf16[2,272,512]{2,1,0:T(8,128)(2,1)S(1)} collective-permute-done((bf16[2,272,512]{2,1,0:T(8,128)(2,1)S(1)}, bf16[2,272,512]{2,1,0:T(8,128)(2,1)S(1)}, u32[]{:S(2)}, u32[]{:S(2)}) %collective-permute-start.41) | collective-permute-done | bytes 557088 | tf_op jit(solution)/shard_map/ppermute | solution.py:80
  241.5 4.2 %collective-permute-done.50.from_x = bf16[128,1024]{1,0:T(8,128)(2,1)S(1)} collective-permute-done((bf16[128,1024]{1,0:T(8,128)(2,1)S(1)}, bf16[128,1024]{1,0:T(8,128)(2,1)S(1)}, u32[]{:S(2)}, u32[]{:S(2)}) %collective-permute-start.50) | collective-permute-done | bytes 262176 | tf_op jit(solution)/shard_map/ppermute | solution.py:45
  245.7 3.8 %collective-permute-done.51.from_d = bf16[128,1024]{1,0:T(8,128)(2,1)S(1)} collective-permute-done((bf16[128,1024]{1,0:T(8,128)(2,1)S(1)}, bf16[128,1024]{1,0:T(8,128)(2,1)S(1)}, u32[]{:S(2)}, u32[]{:S(2)}) %collective-permute-start.51) | collective-permute-done | bytes 262176 | tf_op jit(solution)/shard_map/ppermute | solution.py:49
  250.6 11.0 %collective-permute-done.47.refs_3_ = bf16[1,96,1024]{2,1,0:T(8,128)(2,1)S(1)} collective-permute-done((bf16[1,96,1024]{2,1,0:T(8,128)(2,1)S(1)}, bf16[1,96,1024]{2,1,0:T(8,128)(2,1)S(1)}, u32[]{:S(2)}, u32[]{:S(2)}) %collective-permute-start.47) | collective-permute-done | bytes 196640 | tf_op jit(solution)/shard_map/ppermute | solution.py:80
  268.8 4.9 %all-to-all-start.1 = ((bf16[8,32,1280]{2,1,0:T(8,128)(2,1)}), bf16[8,32,1280]{2,1,0:T(8,128)(2,1)S(1)}, u32[]{:S(2)}, u32[]{:S(2)}) async-start(bf16[8,32,1280]{2,1,0:T(8,128)(2,1)} %bitcast.29), calls=%async_computation.1 | async-start | bytes 1310720 | tf_op jit(solution)/shard_map/all_to_all | solution.py:63
  273.9 13.2 %collective-permute-done.54 = f32[8,256]{1,0:T(8,128)S(1)} collective-permute-done((f32[8,256]{1,0:T(8,128)S(1)}, f32[8,256]{1,0:T(8,128)S(1)}, u32[]{:S(2)}, u32[]{:S(2)}) %collective-permute-start.54) | collective-permute-done | bytes 8224 | tf_op jit(solution)/shard_map/ppermute | solution.py:45
  294.1 17.2 %collective-permute-done.52 = bf16[160,1024]{1,0:T(8,128)(2,1)S(1)} collective-permute-done((bf16[160,1024]{1,0:T(8,128)(2,1)S(1)}, bf16[160,1024]{1,0:T(8,128)(2,1)S(1)}, u32[]{:S(2)}, u32[]{:S(2)}) %collective-permute-start.52) | collective-permute-done | bytes 327712 | tf_op jit(solution)/shard_map/ppermute | solution.py:109
  (263 shorter events, 131.9 us)
Async XLA Ops:
  2.8 32.5 %all-to-all-start = ((bf16[8,32,1280]{2,1,0:T(8,128)(2,1)}), bf16[8,32,1280]{2,1,0:T(8,128)(2,1)S(1)}, u32[]{:S(2)}, u32[]{:S(2)}) async-start(bf16[8,32,1280]{2,1,0:T(8,128)(2,1)} %shard_map.255.payload), calls=%async_computation | async-start | bytes 1310720 | tf_op jit(solution)/shard_map/all_to_all | solution.py:63
  8.7 24.2 %collective-permute-start.5 = (bf16[128,1024]{1,0:T(8,128)(2,1)}, bf16[128,1024]{1,0:T(8,128)(2,1)S(1)}, u32[]{:S(2)}, u32[]{:S(2)}) collective-permute-start(bf16[128,1024]{1,0:T(8,128)(2,1)} %shard_map.257), channel_id=1, source_target_pairs={{0,5},{1,4},{4,1},{5,0},{2,7},{3,6},{6,3},{7,2},{8,13},{9,12},{12,... | collective-permute-start | bytes 786440 | tf_op jit(solution)/shard_map/ppermute | solution.py:49
  10.1 24.0 %collective-permute-start.4 = (bf16[128,1024]{1,0:T(8,128)(2,1)}, bf16[128,1024]{1,0:T(8,128)(2,1)S(1)}, u32[]{:S(2)}, u32[]{:S(2)}) collective-permute-start(bf16[128,1024]{1,0:T(8,128)(2,1)} %shard_map.257), channel_id=1, source_target_pairs={{0,4},{4,0},{1,5},{5,1},{2,6},{6,2},{3,7},{7,3},{8,12},{12,8},{9,1... | collective-permute-start | bytes 786440 | tf_op jit(solution)/shard_map/ppermute | solution.py:45
  11.6 22.5 %collective-permute-start.3 = (bf16[128,1024]{1,0:T(8,128)(2,1)}, bf16[128,1024]{1,0:T(8,128)(2,1)S(1)}, u32[]{:S(2)}, u32[]{:S(2)}) collective-permute-start(bf16[128,1024]{1,0:T(8,128)(2,1)} %shard_map.257), channel_id=1, source_target_pairs={{0,1},{1,0},{2,3},{3,2},{4,5},{5,4},{6,7},{7,6},{8,9},{9,8},{10,11... | collective-permute-start | bytes 786440 | tf_op jit(solution)/shard_map/ppermute | solution.py:45
  12.2 23.1 %collective-permute-start.6 = (bf16[160,1024]{1,0:T(8,128)(2,1)S(1)}, bf16[160,1024]{1,0:T(8,128)(2,1)}, u32[]{:S(2)}, u32[]{:S(2)}) collective-permute-start(bf16[160,1024]{1,0:T(8,128)(2,1)S(1)} %pad_maximum_fusion.7), channel_id=1, source_target_pairs={{0,0},{4,1},{8,2},{12,3},{16,4},{20,5},{24,6},{28,7},{1,8},{5,9},{... | collective-permute-start | bytes 983048 | tf_op jit(solution)/shard_map/ppermute | solution.py:68
  35.3 15.4 %collective-permute-start.10 = (bf16[4,128,1024]{2,1,0:T(8,128)(2,1)S(1)}, bf16[4,128,1024]{2,1,0:T(8,128)(2,1)S(1)}, u32[]{:S(2)}, u32[]{:S(2)}) collective-permute-start(bf16[4,128,1024]{2,1,0:T(8,128)(2,1)S(1)} %pad_maximum_fusion.refs_2_), channel_id=1, source_target_pairs={{0,2},{2,0},{1,3},{3,1},{4,6},{6,4},{5,7},{7,5},{8,10},{10,8},{9,1... | collective-permute-start | bytes 3145736 | tf_op jit(solution)/shard_map/ppermute | solution.py:45
  35.4 15.3 %collective-permute-start.7 = (bf16[1,256,512]{2,1,0:T(8,128)(2,1)S(1)}, bf16[1,256,512]{2,1,0:T(8,128)(2,1)S(1)}, u32[]{:S(2)}, u32[]{:S(2)}) collective-permute-start(bf16[1,256,512]{2,1,0:T(8,128)(2,1)S(1)} %slice_bitcast_fusion.1.refs_0_), channel_id=1, source_target_pairs={{0,16},{8,24},{16,0},{24,8},{1,17},{9,25},{17,1},{25,9},{2,18},{10... | collective-permute-start | bytes 786440 | tf_op jit(solution)/shard_map/ppermute | solution.py:80
  52.5 20.8 %collective-permute-start.11 = (bf16[2,256,512]{2,1,0:T(8,128)(2,1)}, bf16[2,256,512]{2,1,0:T(8,128)(2,1)S(1)}, u32[]{:S(2)}, u32[]{:S(2)}) collective-permute-start(bf16[2,256,512]{2,1,0:T(8,128)(2,1)} %pad_maximum_fusion.6), channel_id=1, source_target_pairs={{0,8},{8,0},{16,24},{24,16},{1,9},{9,1},{17,25},{25,17},{2,10},{10... | collective-permute-start | bytes 1572872 | tf_op jit(solution)/shard_map/ppermute | solution.py:80
  56.2 15.1 %collective-permute-start.12 = (bf16[1,160,1024]{2,1,0:T(8,128)(2,1)}, bf16[1,160,1024]{2,1,0:T(8,128)(2,1)S(1)}, u32[]{:S(2)}, u32[]{:S(2)}) collective-permute-start(bf16[1,160,1024]{2,1,0:T(8,128)(2,1)} %bitcast.14.refs_0_), channel_id=1, source_target_pairs={{0,16},{8,24},{16,0},{24,8},{1,17},{9,25},{17,1},{25,9},{2,18},{10... | collective-permute-start | bytes 983048 | tf_op jit(solution)/shard_map/ppermute | solution.py:80
  75.4 24.9 %collective-permute-start.16 = (bf16[2,160,1024]{2,1,0:T(8,128)(2,1)}, bf16[2,160,1024]{2,1,0:T(8,128)(2,1)}, u32[]{:S(2)}, u32[]{:S(2)}) collective-permute-start(bf16[2,160,1024]{2,1,0:T(8,128)(2,1)} %pad_maximum_fusion.5), channel_id=1, source_target_pairs={{0,8},{8,0},{16,24},{24,16},{1,9},{9,1},{17,25},{25,17},{2,10},{10... | collective-permute-start | bytes 1966088 | tf_op jit(solution)/shard_map/ppermute | solution.py:80
  78.2 26.3 %collective-permute-start.21 = (bf16[1,256,768]{2,1,0:T(8,128)(2,1)}, bf16[1,256,768]{2,1,0:T(8,128)(2,1)}, u32[]{:S(2)}, u32[]{:S(2)}) collective-permute-start(bf16[1,256,768]{2,1,0:T(8,128)(2,1)} %slice_bitcast_fusion.refs_0_), channel_id=1, source_target_pairs={{0,16},{8,24},{16,0},{24,8},{1,17},{9,25},{17,1},{25,9},{2,18},{10... | collective-permute-start | bytes 1179656 | tf_op jit(solution)/shard_map/ppermute | solution.py:80
  105.7 20.0 %collective-permute-start.22 = (bf16[2,256,768]{2,1,0:T(8,128)(2,1)S(1)}, bf16[2,256,768]{2,1,0:T(8,128)(2,1)S(1)}, u32[]{:S(2)}, u32[]{:S(2)}) collective-permute-start(bf16[2,256,768]{2,1,0:T(8,128)(2,1)S(1)} %pad_maximum_fusion.4), channel_id=1, source_target_pairs={{0,8},{8,0},{16,24},{24,16},{1,9},{9,1},{17,25},{25,17},{2,10},{10... | collective-permute-start | bytes 2359304 | tf_op jit(solution)/shard_map/ppermute | solution.py:80
  107.3 18.4 %collective-permute-start.18 = (bf16[128,1024]{1,0:T(8,128)(2,1)S(1)}, bf16[128,1024]{1,0:T(8,128)(2,1)S(1)}, u32[]{:S(2)}, u32[]{:S(2)}) collective-permute-start(bf16[128,1024]{1,0:T(8,128)(2,1)S(1)} %get-tuple-element.193), channel_id=1, source_target_pairs={{0,1},{1,0},{2,3},{3,2},{4,5},{5,4},{6,7},{7,6},{8,9},{9,8},{10,11... | collective-permute-start | bytes 786440 | tf_op jit(solution)/shard_map/ppermute | solution.py:45
  108.5 17.3 %collective-permute-start.19 = (bf16[128,1024]{1,0:T(8,128)(2,1)S(1)}, bf16[128,1024]{1,0:T(8,128)(2,1)S(1)}, u32[]{:S(2)}, u32[]{:S(2)}) collective-permute-start(bf16[128,1024]{1,0:T(8,128)(2,1)S(1)} %get-tuple-element.194), channel_id=1, source_target_pairs={{0,4},{4,0},{1,5},{5,1},{2,6},{6,2},{3,7},{7,3},{8,12},{12,8},{9,1... | collective-permute-start | bytes 786440 | tf_op jit(solution)/shard_map/ppermute | solution.py:45
  110.2 15.6 %collective-permute-start.20 = (bf16[128,1024]{1,0:T(8,128)(2,1)S(1)}, bf16[128,1024]{1,0:T(8,128)(2,1)S(1)}, u32[]{:S(2)}, u32[]{:S(2)}) collective-permute-start(bf16[128,1024]{1,0:T(8,128)(2,1)S(1)} %get-tuple-element.195), channel_id=1, source_target_pairs={{0,5},{1,4},{4,1},{5,0},{2,7},{3,6},{6,3},{7,2},{8,13},{9,12},{12,... | collective-permute-start | bytes 786440 | tf_op jit(solution)/shard_map/ppermute | solution.py:49
  131.5 15.6 %collective-permute-start.27 = (bf16[4,128,1024]{2,1,0:T(8,128)(2,1)S(1)}, bf16[4,128,1024]{2,1,0:T(8,128)(2,1)}, u32[]{:S(2)}, u32[]{:S(2)}) collective-permute-start(bf16[4,128,1024]{2,1,0:T(8,128)(2,1)S(1)} %pad_maximum_fusion.1.refs_1_.refs_0_), channel_id=1, source_target_pairs={{0,2},{2,0},{1,3},{3,1},{4,6},{6,4},{5,7},{7,5},{8,10},{10,8},{9,1... | collective-permute-start | bytes 3145736 | tf_op jit(solution)/shard_map/ppermute | solution.py:45
  154.6 14.2 %collective-permute-start.29 = (bf16[128,1024]{1,0:T(8,128)(2,1)S(1)}, bf16[128,1024]{1,0:T(8,128)(2,1)S(1)}, u32[]{:S(2)}, u32[]{:S(2)}) collective-permute-start(bf16[128,1024]{1,0:T(8,128)(2,1)S(1)} %get-tuple-element.218), channel_id=1, source_target_pairs={{0,1},{1,0},{2,3},{3,2},{4,5},{5,4},{6,7},{7,6},{8,9},{9,8},{10,11... | collective-permute-start | bytes 786440 | tf_op jit(solution)/shard_map/ppermute | solution.py:45
  170.8 19.0 %collective-permute-start.35 = (bf16[2,256,768]{2,1,0:T(8,128)(2,1)S(1)}, bf16[2,256,768]{2,1,0:T(8,128)(2,1)S(1)}, u32[]{:S(2)}, u32[]{:S(2)}) collective-permute-start(bf16[2,256,768]{2,1,0:T(8,128)(2,1)S(1)} %get-tuple-element.232), channel_id=1, source_target_pairs={{0,8},{8,0},{16,24},{24,16},{1,9},{9,1},{17,25},{25,17},{2,10},{10... | collective-permute-start | bytes 2359304 | tf_op jit(solution)/shard_map/ppermute | solution.py:80
  190.4 20.1 %collective-permute-start.39 = (bf16[2,96,1024]{2,1,0:T(8,128)(2,1)S(1)}, bf16[2,96,1024]{2,1,0:T(8,128)(2,1)S(1)}, u32[]{:S(2)}, u32[]{:S(2)}) collective-permute-start(bf16[2,96,1024]{2,1,0:T(8,128)(2,1)S(1)} %get-tuple-element.251), channel_id=1, source_target_pairs={{0,8},{8,0},{16,24},{24,16},{1,9},{9,1},{17,25},{25,17},{2,10},{10... | collective-permute-start | bytes 1179656 | tf_op jit(solution)/shard_map/ppermute | solution.py:80
  191.0 20.0 %collective-permute-start.38 = (bf16[1,256,768]{2,1,0:T(8,128)(2,1)S(1)}, bf16[1,256,768]{2,1,0:T(8,128)(2,1)S(1)}, u32[]{:S(2)}, u32[]{:S(2)}) collective-permute-start(bf16[1,256,768]{2,1,0:T(8,128)(2,1)S(1)} %get-tuple-element.249), channel_id=1, source_target_pairs={{0,16},{8,24},{16,0},{24,8},{1,17},{9,25},{17,1},{25,9},{2,18},{10... | collective-permute-start | bytes 1179656 | tf_op jit(solution)/shard_map/ppermute | solution.py:80
  196.0 19.5 %collective-permute-start.40 = (bf16[2,64,1024]{2,1,0:T(8,128)(2,1)S(1)}, bf16[2,64,1024]{2,1,0:T(8,128)(2,1)S(1)}, u32[]{:S(2)}, u32[]{:S(2)}) collective-permute-start(bf16[2,64,1024]{2,1,0:T(8,128)(2,1)S(1)} %get-tuple-element.253), channel_id=1, source_target_pairs={{0,8},{8,0},{16,24},{24,16},{1,9},{9,1},{17,25},{25,17},{2,10},{10... | collective-permute-start | bytes 786440 | tf_op jit(solution)/shard_map/ppermute | solution.py:80
  219.9 15.1 %collective-permute-start.41 = (bf16[2,272,512]{2,1,0:T(8,128)(2,1)S(1)}, bf16[2,272,512]{2,1,0:T(8,128)(2,1)S(1)}, u32[]{:S(2)}, u32[]{:S(2)}) collective-permute-start(bf16[2,272,512]{2,1,0:T(8,128)(2,1)S(1)} %get-tuple-element.257), channel_id=1, source_target_pairs={{0,8},{8,0},{16,24},{24,16},{1,9},{9,1},{17,25},{25,17},{2,10},{10... | collective-permute-start | bytes 1671176 | tf_op jit(solution)/shard_map/ppermute | solution.py:80
  221.7 18.4 %collective-permute-start.49 = (bf16[128,1024]{1,0:T(8,128)(2,1)S(1)}, bf16[128,1024]{1,0:T(8,128)(2,1)S(1)}, u32[]{:S(2)}, u32[]{:S(2)}) collective-permute-start(bf16[128,1024]{1,0:T(8,128)(2,1)S(1)} %get-tuple-element.282), channel_id=1, source_target_pairs={{0,1},{1,0},{2,3},{3,2},{4,5},{5,4},{6,7},{7,6},{8,9},{9,8},{10,11... | collective-permute-start | bytes 786440 | tf_op jit(solution)/shard_map/ppermute | solution.py:45
  235.1 29.2 %collective-permute-start.45 = (bf16[1,272,512]{2,1,0:T(8,128)(2,1)S(1)}, bf16[1,272,512]{2,1,0:T(8,128)(2,1)S(1)}, u32[]{:S(2)}, u32[]{:S(2)}) collective-permute-start(bf16[1,272,512]{2,1,0:T(8,128)(2,1)S(1)} %get-tuple-element.271), channel_id=1, source_target_pairs={{0,16},{8,24},{16,0},{24,8},{1,17},{9,25},{17,1},{25,9},{2,18},{10... | collective-permute-start | bytes 835592 | tf_op jit(solution)/shard_map/ppermute | solution.py:80
  238.3 23.2 %collective-permute-start.47 = (bf16[1,96,1024]{2,1,0:T(8,128)(2,1)S(1)}, bf16[1,96,1024]{2,1,0:T(8,128)(2,1)S(1)}, u32[]{:S(2)}, u32[]{:S(2)}) collective-permute-start(bf16[1,96,1024]{2,1,0:T(8,128)(2,1)S(1)} %get-tuple-element.279), channel_id=1, source_target_pairs={{0,16},{8,24},{16,0},{24,8},{1,17},{9,25},{17,1},{25,9},{2,18},{10... | collective-permute-start | bytes 589832 | tf_op jit(solution)/shard_map/ppermute | solution.py:80
  240.1 24.2 %collective-permute-start.46 = (bf16[1,64,1024]{2,1,0:T(8,128)(2,1)S(1)}, bf16[1,64,1024]{2,1,0:T(8,128)(2,1)S(1)}, u32[]{:S(2)}, u32[]{:S(2)}) collective-permute-start(bf16[1,64,1024]{2,1,0:T(8,128)(2,1)S(1)} %get-tuple-element.275), channel_id=1, source_target_pairs={{0,16},{8,24},{16,0},{24,8},{1,17},{9,25},{17,1},{25,9},{2,18},{10... | collective-permute-start | bytes 393224 | tf_op jit(solution)/shard_map/ppermute | solution.py:80
  265.3 23.7 %collective-permute-start.42 = (bf16[128,1024]{1,0:T(8,128)(2,1)}, bf16[128,1024]{1,0:T(8,128)(2,1)S(1)}, u32[]{:S(2)}, u32[]{:S(2)}) collective-permute-start(bf16[128,1024]{1,0:T(8,128)(2,1)} %get-tuple-element.265), channel_id=1, source_target_pairs={{0,1},{1,0},{2,3},{3,2},{4,5},{5,4},{6,7},{7,6},{8,9},{9,8},{10,11... | collective-permute-start | bytes 786440 | tf_op jit(solution)/shard_map/ppermute | solution.py:45
  265.7 23.3 %collective-permute-start.43 = (bf16[128,1024]{1,0:T(8,128)(2,1)}, bf16[128,1024]{1,0:T(8,128)(2,1)S(1)}, u32[]{:S(2)}, u32[]{:S(2)}) collective-permute-start(bf16[128,1024]{1,0:T(8,128)(2,1)} %get-tuple-element.266), channel_id=1, source_target_pairs={{0,4},{4,0},{1,5},{5,1},{2,6},{6,2},{3,7},{7,3},{8,12},{12,8},{9,1... | collective-permute-start | bytes 786440 | tf_op jit(solution)/shard_map/ppermute | solution.py:45
  267.4 21.7 %collective-permute-start.44 = (bf16[128,1024]{1,0:T(8,128)(2,1)}, bf16[128,1024]{1,0:T(8,128)(2,1)}, u32[]{:S(2)}, u32[]{:S(2)}) collective-permute-start(bf16[128,1024]{1,0:T(8,128)(2,1)} %get-tuple-element.267), channel_id=1, source_target_pairs={{0,5},{1,4},{4,1},{5,0},{2,7},{3,6},{6,3},{7,2},{8,13},{9,12},{12,... | collective-permute-start | bytes 786440 | tf_op jit(solution)/shard_map/ppermute | solution.py:49
  268.8 44.0 %all-to-all-start.1 = ((bf16[8,32,1280]{2,1,0:T(8,128)(2,1)}), bf16[8,32,1280]{2,1,0:T(8,128)(2,1)S(1)}, u32[]{:S(2)}, u32[]{:S(2)}) async-start(bf16[8,32,1280]{2,1,0:T(8,128)(2,1)} %bitcast.29), calls=%async_computation.1 | async-start | bytes 1310720 | tf_op jit(solution)/shard_map/all_to_all | solution.py:63
  273.7 13.4 %collective-permute-start.54 = (f32[8,256]{1,0:T(8,128)S(1)}, f32[8,256]{1,0:T(8,128)S(1)}, u32[]{:S(2)}, u32[]{:S(2)}) collective-permute-start(f32[8,256]{1,0:T(8,128)S(1)} %add.54), channel_id=1, source_target_pairs={{0,4},{4,0},{1,5},{5,1},{2,6},{6,2},{3,7},{7,3},{8,12},{12,8},{9,1... | collective-permute-start | bytes 24584 | tf_op jit(solution)/shard_map/ppermute | solution.py:45
  291.0 20.3 %collective-permute-start.52 = (bf16[160,1024]{1,0:T(8,128)(2,1)S(1)}, bf16[160,1024]{1,0:T(8,128)(2,1)S(1)}, u32[]{:S(2)}, u32[]{:S(2)}) collective-permute-start(bf16[160,1024]{1,0:T(8,128)(2,1)S(1)} %shard_map.292), channel_id=1, source_target_pairs={{0,0},{1,4},{2,8},{3,12},{4,16},{5,20},{6,24},{7,28},{8,1},{9,5},{... | collective-permute-start | bytes 983048 | tf_op jit(solution)/shard_map/ppermute | solution.py:109
  (80 other events, 895.6 us)

commit v3 on v2

--- a/solution.py
+++ b/solution.py
@@ -181,20 +181,6 @@
         in_specs=[spec("whole", w.shape, 0) for w in weights],
         out_specs=spec("whole", shape, 0),
     )(*weights)
-
-
-def copy_kernel(tokens, payload, out):
-    out[...] = tokens[...]
-
-
-def ordered_after(tokens, payload):
-    vmem = pl.BlockSpec(memory_space=pltpu.VMEM)
-    return pl.pallas_call(
-        copy_kernel,
-        out_shape=jax.ShapeDtypeStruct(tokens.shape, tokens.dtype),
-        in_specs=[vmem, pl.BlockSpec(memory_space=pl.ANY)],
-        out_specs=vmem,
-    )(tokens, payload)
 
 
 def marks_kernel(scalars, norm_gain, mlp_gain, query_gain, key_gain, lengths, seq_order, out):
@@ -283,37 +269,66 @@
     )(scalars, *arrays)
 
 
-def unpack_kernel(widths, start, got, gain, *refs):
-    weights, outs, gain_out = refs[: len(widths)], refs[len(widths) : -1], refs[-1]
-    sums = 0.0
+def unpack_kernel(widths, start, scalars, got, gain, *refs):
+    weights, outs = refs[: len(widths)], refs[len(widths) : -2]
+    gain_out, head_gains = refs[-2:]
+    rows, sums, line = gain.shape[0], 0.0, 0.0
     for j in range(8):
         at = start
         for width, weight, out in zip(widths, weights, outs):
-            piece = got[j, :, at : at + width].astype(F32)
+            piece = got[j, :rows, at : at + width].astype(F32)
             out[:, j * width : (j + 1) * width] = piece
             kept = weight[:, j * width : (j + 1) * width].astype(F32)
             sums = sums + jnp.sum(piece * kept, axis=1, keepdims=True)
             at += width
+        line = line + got[j, rows : rows + 8, : 2 * HEAD_SIZE].astype(F32)
     gain_out[...] = sums / gain[...]
-
-
-def unpack(got, start, gain, *weights):
+    each = head_gains.shape[1]
+    for k in range(2):
+        part = line[0:1, k * HEAD_SIZE : (k + 1) * HEAD_SIZE]
+        back = lax.rem(HEAD_SIZE - scalars[2] * each, HEAD_SIZE)
+        head_gains[k : k + 1, :] = pltpu.roll(part, back, 1)[:, :each]
+
+
+def unpack(got, start, gain, scalars, gains, *weights):
     widths = [w.shape[1] // 8 for w in weights]
-    outs = [(w.shape, F32) for w in weights] + [((gain.shape[0], 1), F32)]
-    *grads, gain_grad = call(
+    outs = [(w.shape, F32) for w in weights] + [((gain.shape[0], 1), F32), ((2, gains), F32)]
+    vmem = pl.BlockSpec(memory_space=pltpu.VMEM)
+    *grads, gain_grad, head_gains = pl.pallas_call(
         functools.partial(unpack_kernel, widths, start),
-        outs,
-        got,
-        gain.astype(F32)[:, None],
-        *weights,
-    )
-    return grads, gain_grad[:, 0]
+        out_shape=tuple(jax.ShapeDtypeStruct(shape, dtype) for shape, dtype in outs),
+        in_specs=[pl.BlockSpec(memory_space=pltpu.SMEM)] + [vmem] * (2 + len(weights)),
+        out_specs=tuple(vmem for _ in outs),
+        compiler_params=pltpu.CompilerParams(vmem_limit_bytes=12 * 2**20),
+    )(scalars, got, gain.astype(F32)[:, None], *weights)
+    return grads, gain_grad[:, 0], head_gains
 
 
 def merge_kernel(near, other, own, to_y, to_x, to_d):
     own[...] = near[0] + other[0].astype(F32)
     for k, out in ((1, to_y), (2, to_x), (3, to_d)):
         out[...] = (near[k] + other[k].astype(F32)).astype(BF)
+
+
+def merge_all_kernel(scalars, near, other, own, out):
+    own[...] = near[0] + other[0].astype(F32)
+    for k in range(4):
+        part = near[k] + other[k].astype(F32) if k else jnp.zeros_like(near[0])
+        out[lax.bitwise_xor(scalars[3], k)] = part.astype(BF)
+
+
+def merge_all(scalars, near, other):
+    vmem = pl.BlockSpec(memory_space=pltpu.VMEM)
+    return pl.pallas_call(
+        merge_all_kernel,
+        out_shape=(
+            jax.ShapeDtypeStruct(near.shape[1:], F32),
+            jax.ShapeDtypeStruct(near.shape, BF),
+        ),
+        in_specs=[pl.BlockSpec(memory_space=pltpu.SMEM), vmem, vmem],
+        out_specs=(vmem, vmem),
+        compiler_params=pltpu.CompilerParams(vmem_limit_bytes=12 * 2**20),
+    )(scalars, near, other)
 
 
 def merge(near, other):
@@ -338,8 +353,10 @@
     normed[...] = (total * inv_rms(total) * gain[...]).astype(BF)
 
 
-def result_kernel(hidden, own, from_y, from_x, from_d, result):
-    total = hidden[...] + summed(own, from_y, from_x, from_d, hidden.shape[0])
+def result_kernel(hidden, own, others, result):
+    total = hidden[...] + own[...]
+    for k in range(4):
+        total = total + others[k].astype(F32)
     result[...] = total.astype(BF)
 
 
@@ -428,12 +445,12 @@
     ]
 
 
-def feed_kernel(rows, mid, cot, gate_up, down, normed, mixed, grad_gu, parts):
+def feed_kernel(rows, mid, cot, w_gate, w_up, down, normed, mixed, grad_gu, parts):
     ff = down.shape[0]
     x = group_of(mid, 0, rows)
     normed[...] = x
-    both = mm(x, gate_up[...])
-    gate_pre, upward = both[:, :ff], both[:, ff:]
+    gate_pre = mm(x, w_gate[...])
+    upward = mm(x, w_up[...])
     grad_mixed = mm_nt(group_of(cot, 0, rows), down[...])
     sigma = 1.0 / (1.0 + jnp.exp(-gate_pre))
     silu = gate_pre * sigma
@@ -442,7 +459,7 @@
     grad_up = (grad_mixed * silu).astype(BF)
     grad_gu[:, :ff] = grad_gate
     grad_gu[:, ff:] = grad_up
-    split_out(mm_nt(grad_gu[...], gate_up[...]), rows, parts)
+    split_out(mm_nt(grad_gate, w_gate[...]) + mm_nt(grad_up, w_up[...]), rows, parts)
 
 
 def attend_pull_kernel(
@@ -567,31 +584,40 @@
     send[...] = total[size:].astype(BF)
 
 
-def halve_on(keep, got):
-    bit = 2
+def halve_add(keep, got):
+    part = (keep.shape[0] // 2,) + keep.shape[1:]
+    return call(add_kernel, [(part, F32), (part, BF)], keep, got)
+
+
+def halve_on(keep, send):
+    got, bit = across(send, 2), 4
     while keep.shape[0] > 1:
-        part = (keep.shape[0] // 2,) + keep.shape[1:]
-        keep, send = call(add_kernel, [(part, F32), (part, BF)], keep, got)
+        keep, send = halve_add(keep, got)
         got = across(send, bit)
         bit *= 2
     return keep, got
 
 
-def finish_kernel(*refs):
-    *terms, out, line = refs
-    rows, at = out.shape[0], 0
+def finish_kernel(rows, *refs):
+    *terms, out = refs
+    at = 0
     for keep, got in zip(terms[::2], terms[1::2]):
-        total = keep[0, :rows, :] + got[0, :rows, :].astype(F32)
-        out[:, at : at + total.shape[1]] = total.astype(BF)
-        at += total.shape[1]
-    keep, got = terms[:2]
-    line[...] = (keep[0, rows : rows + 8, :] + got[0, rows : rows + 8, :].astype(F32))[:, : 2 * HEAD_SIZE]
+        size = 8 * rows
+        total = (keep[0, :size, :] + got[0, :size, :].astype(F32)).astype(BF)
+        width = total.shape[1]
+        for j in range(8):
+            out[j, :rows, at : at + width] = total[j * rows : (j + 1) * rows]
+            if at == 0:
+                line = keep[0, size : size + 8, :] + got[0, size : size + 8, :].astype(F32)
+                out[j, rows:, :width] = line.astype(BF)
+            else:
+                out[j, rows:, at : at + width] = jnp.zeros((8, width), BF)
+        at += width
 
 
 def finish(rows, *terms):
-    shape = (rows, sum(term.shape[2] for term in terms[::2]))
-    outs = [(shape, BF), ((8, 2 * HEAD_SIZE), F32)]
-    return call(finish_kernel, outs, *terms)
+    shape = (8, rows + 8, sum(term.shape[2] for term in terms[::2]))
+    return call(functools.partial(finish_kernel, rows), [(shape, BF)], *terms)[0]
 
 
 def finish_rows_kernel(*refs):
@@ -635,7 +661,8 @@
     n_seq = lengths.shape[1]
     plane_rows = 8 * rows
     me = place * 8 + in_plane
-    scalars = jnp.stack([place, in_seq, me]).astype(jnp.int32)
+    in_chips = lax.axis_index("x") * 2 + in_seq
+    scalars = jnp.stack([place, in_seq, me, in_chips]).astype(jnp.int32)
 
     half = HEAD_SIZE // 2
     angles = np.arange(2 * rows)[:, None] * THETA ** (-np.arange(half) * (2.0 / HEAD_SIZE))
@@ -646,31 +673,35 @@
     turns = lax.dynamic_index_in_dim(turns, in_seq, 0, False)
     cosine, sine = turns[0], turns[1]
 
-    payload = pack(w_query, w_key, w_value, w_gate, w_up)
+    payload = pack(w_query, w_key, w_value)
     marks = make_marks(
         scalars, width,
         norm_gain[None], mlp_gain[None], query_gain[None], key_gain[None], lengths, seq_order,
     )
     got = in_plane_all(payload).reshape(8 * w_rows, -1)
-    marks = plane_sum(data_sum(data_sum(marks), last=True), "core")
-    near = gather_chips(ordered_after(tokens, payload))
-    row_weights = to_row_place(jnp.concatenate([w_output, w_down]), count)
-    got, marks, near, row_weights, cot = together(got, marks, near, row_weights, cotangent)
-
-    qkv = double([got[None, :, : 4 * HEAD_SIZE]])
-    gate_up = got[None, :, 4 * HEAD_SIZE :]
-    marks = plane_sum(marks, "x", "seq")
+    marks = data_sum(data_sum(marks), last=True)
+    near = gather_chips(tokens)
+    payload, row_weights = together(payload, jnp.concatenate([w_output, w_down]))
+    row_weights = to_row_place(row_weights, count)
+    got, marks, near, row_weights, cot, gate, up = together(
+        got, marks, near, row_weights, cotangent, w_gate, w_up
+    )
+
+    qkv = double([got[None]])
+    marks = plane_sum(marks)
     far = flip(near, "core")
-    qkv, marks, near, far, row_weights, gate_up, cot = together(
-        qkv, marks, near, far, row_weights, gate_up, cot
+    gate = in_plane_all(pack(gate)).reshape(1, 8 * w_rows, -1)
+    qkv, marks, near, far, row_weights, gate, up, cot = together(
+        qkv, marks, near, far, row_weights, gate, up, cot
     )
 
     qkv = double(qkv, last=True)
     row_weights = double([row_weights[None]])
     cot_near = gather_chips(cot)
     gain_in, gain_mid, head_gains, starts = setup(scalars, marks, n_seq)
-    qkv, gain_in, near, far, row_weights, gate_up, cot_near = together(
-        qkv, gain_in, near, far, row_weights, gate_up, cot_near
+    up = in_plane_all(pack(up)).reshape(1, 8 * w_rows, -1)
+    qkv, gain_in, near, far, row_weights, gate, up, cot_near = together(
+        qkv, gain_in, near, far, row_weights, gate, up, cot_near
     )
 
     cot_far = flip(cot_near, "core")
@@ -692,22 +723,24 @@
         )
     normed_in, raw, low, attn_low = kept
     row_weights = double(row_weights, last=True)
-    gate_up = double([gate_up])
-    attn_low, row_weights = together(attn_low, row_weights)
+    gate = double([gate])
+    attn_low, row_weights, gate, up = together(attn_low, row_weights, gate, up)
 
     out_full, down_full = assemble(row_weights, scalars, w_output.shape[0], w_down.shape[0])
     ff = down_full.shape[0]
     part_near, part_far = project(attn_low, out_full, rows)
     sums = exchange(*merge(part_near, flip(part_far, "core")))
-    gate_up = double(gate_up, last=True)
-    sums, gate_up = together(sums, gate_up)
+    gate = double(gate, last=True)
+    up = double([up])
+    sums, gate, up = together(sums, gate, up)
 
     hidden, normed_mid = call(
         hidden_kernel, [((rows, width), F32), ((rows, width), BF)], tokens, *sums, gain_mid
     )
     mid_near = gather_chips(normed_mid)
-    gu_full = assemble(gate_up, scalars)[0]
-    mid_near, gu_full = together(mid_near, gu_full)
+    gate_full = assemble(gate, scalars)[0]
+    up_full = assemble(double(up, last=True), scalars)[0]
+    mid_near, gate_full, up_full = together(mid_near, gate_full, up_full)
     u_parts, kept = [], ()
     mid_far = flip(mid_near, "core")
     for which, mid, cot, dtype in (
@@ -723,17 +756,20 @@
                 ("group", (plane_rows, 2 * ff), BF),
                 ("blocks", (4, rows, width), dtype),
             ],
-            [("blocks", mid), ("blocks", cot)] + whole(gu_full, down_full),
+            [("blocks", mid), ("blocks", cot)] + whole(gate_full, up_full, down_full),
             kept=kept,
         )
         u_parts.append(u_part)
     mid_all, mixed, grad_gu = kept
     sums = exchange(*merge(u_parts[0], flip(u_parts[1], "core")))
+    down_keep, down_send = weigh(mixed, [cot_near, cot_far], scalars, count)
+    down_got = across(down_send, 1)
+    mid_all, _ = together(mid_all, down_send)
     gu_keep, gu_send = weigh(mid_all, [grad_gu], scalars, count)
-    down_keep, down_send = weigh(mixed, [cot_near, cot_far], scalars, count)
     result_near, result_far = project(mixed, down_full, rows)
-    sums, result_near, result_far, gu_send, down_send = together(
-        sums, result_near, result_far, gu_send, down_send
+    result_own, result_parts = merge_all(scalars, result_near, flip(result_far, "core"))
+    sums, result_own, result_parts, gu_send, down_got = together(
+        sums, result_own, result_parts, gu_send, down_got
     )
 
     grad_hidden, grad_out = call(
@@ -743,12 +779,15 @@
     )
     out_near = gather_chips(grad_out)
     gu_got = across(gu_send, 1)
-    down_got = across(down_send, 1)
-    out_near, gu_keep, gu_got = together(out_near, gu_keep, gu_got)
+    down_keep, down_got = halve_on(*halve_add(down_keep, down_got))
+    gu_keep, gu_send = halve_add(gu_keep, gu_got)
+    out_near, gu_keep, gu_send, down_keep, down_got = together(
+        out_near, gu_keep, gu_send, down_keep, down_got
+    )
 
     out_far = flip(out_near, "core")
-    result_parts = merge(result_near, flip(result_far, "core"))
-    gu_keep, gu_got = halve_on(gu_keep, gu_got)
+    gu_keep, gu_got = halve_on(gu_keep, gu_send)
+    down_rows = to_row_owner(finish_rows(down_keep, down_got), count)
     gain_parts, kept = [], ()
     for which, blocks in enumerate((out_near, out_far)):
         *kept, gain_part = call_half(
@@ -766,14 +805,7 @@
         gain_parts.append(gain_part)
     grad_qkv = kept[0]
     gains_sum = gain_parts[0] + gain_parts[1]
-    out_keep, out_send = weigh(attn_low, [out_near, out_far], scalars, count)
-    out_got = across(out_send, 1)
-    grad_qkv, gains_sum, result_parts, gu_keep, gu_got, down_keep, down_got, out_keep, out_got = together(
-        grad_qkv, gains_sum, result_parts, gu_keep, gu_got, down_keep, down_got, out_keep, out_got
-    )
-
     qkv_keep, qkv_send = weigh(normed_in, [grad_qkv], scalars, count, gains_sum)
-    qkv_got = across(qkv_send, 1)
     part_near, part_far = [
         call_half(
             functools.partial(project_nt_kernel, rows),
@@ -783,36 +815,41 @@
         )[0]
         for which, dtype in ((0, F32), (1, BF))
     ]
+    part_near, part_far, qkv_keep, qkv_send, attn_low, down_rows, gu_keep, gu_got = together(
+        part_near, part_far, qkv_keep, qkv_send, attn_low, down_rows, gu_keep, gu_got
+    )
+
+    qkv_got = across(qkv_send, 1)
     sums = exchange(*merge(part_near, flip(part_far, "core")))
-    down_keep, down_got = halve_on(down_keep, down_got)
-    qkv_keep, qkv_got, out_keep, out_got, result_parts = together(
-        qkv_keep, qkv_got, out_keep, out_got, result_parts
-    )
-
-    qkv_keep, qkv_got = halve_on(qkv_keep, qkv_got)
-    out_keep, out_got = halve_on(out_keep, out_got)
+    out_keep, out_send = weigh(attn_low, [out_near, out_far], scalars, count)
+    out_got = across(out_send, 1)
+    result_got = lax.all_to_all(
+        result_parts, ("x", "seq"), split_axis=0, concat_axis=0, tiled=True
+    )
+    qkv_keep, qkv_got = together(qkv_keep, qkv_got)
+
+    qkv_keep, qkv_send = halve_add(qkv_keep, qkv_got)
+    qkv_keep, qkv_got = halve_on(qkv_keep, qkv_send)
+    out_keep, out_got, _ = together(out_keep, out_got, qkv_send)
+    out_keep, out_got = halve_on(*halve_add(out_keep, out_got))
     grad_tokens = call(
         norm_pull_kernel, [((rows, width), F32)], tokens, grad_hidden, *sums, gain_in
     )[0]
-    result_sums = exchange(*result_parts)
-    qkv_keep, qkv_got, out_keep, out_got, down_keep, down_got, grad_tokens = together(
-        qkv_keep, qkv_got, out_keep, out_got, down_keep, down_got, grad_tokens
-    )
-
-    got, gains_sum = finish(8 * w_rows, qkv_keep, qkv_got, gu_keep, gu_got)
-    got = in_plane_all(got.reshape(8, w_rows, got.shape[1]))
-    row_grads = to_row_owner(finish_rows(out_keep, out_got, down_keep, down_got), count)
-    gains_sum = plane_sum(gains_sum)
-    result = call(result_kernel, [((rows, width), BF)], hidden, *result_sums)[0]
-    me = me * gains
-    grad_query_gain = lax.dynamic_slice_in_dim(gains_sum[0, :HEAD_SIZE], me, gains)
-    grad_key_gain = lax.dynamic_slice_in_dim(gains_sum[0, HEAD_SIZE:], me, gains)
-    row_grads = row_grads.astype(F32)
-    (grad_w_query, grad_w_key, grad_w_value), grad_norm_gain = unpack(
-        got, 0, norm_gain, w_query, w_key, w_value
-    )
-    (grad_w_gate, grad_w_up), grad_mlp_gain = unpack(got, 4 * HEAD_SIZE, mlp_gain, w_gate, w_up)
-    out_rows = w_output.shape[0]
+    result = call(
+        result_kernel, [((rows, width), BF)], hidden, result_own, result_got
+    )[0]
+    qkv_keep, qkv_got, out_keep, out_got, grad_tokens = together(
+        qkv_keep, qkv_got, out_keep, out_got, grad_tokens
+    )
+
+    got = in_plane_all(finish(w_rows, qkv_keep, qkv_got, gu_keep, gu_got))
+    out_rows = to_row_owner(finish_rows(out_keep, out_got), count)
+    (grad_w_query, grad_w_key, grad_w_value), grad_norm_gain, head_gain_grads = unpack(
+        got, 0, norm_gain, scalars, gains, w_query, w_key, w_value
+    )
+    (grad_w_gate, grad_w_up), grad_mlp_gain, _ = unpack(
+        got, 4 * HEAD_SIZE, mlp_gain, scalars, gains, w_gate, w_up
+    )
     return (
         result,
         grad_tokens,
@@ -820,13 +857,13 @@
         grad_w_query,
         grad_w_key,
         grad_w_value,
-        row_grads[:out_rows],
-        grad_query_gain,
-        grad_key_gain,
+        out_rows.astype(F32),
+        head_gain_grads[0],
+        head_gain_grads[1],
         grad_mlp_gain,
         grad_w_gate,
         grad_w_up,
-        row_grads[out_rows:],
+        down_rows.astype(F32),
     )
 
 

time: 317 us -> 284 us (0.90)
  waiting for transfers between devices: 153 us -> 85 us
  starting transfers between devices: 69.9 us -> 86.7 us
  Pallas kernels: 66.9 us -> 74.8 us
  other arithmetic: 11.2 us -> 16.5 us
  local copies, waits for them, and re-layouts: 13.7 us -> 17.9 us
    ppermute x16 -> x18, waiting for transfers between devices: 78.4 us -> 37.9 us  [across(): lax.ppermute(value, 'data', [(d, d ^ bit) for d in range(lax.axis_size('d...]
    ppermute x30 -> x25, waiting for transfers between devices: 39.2 us -> 18.2 us  [flip(): return lax.ppermute(value, axis, SWAP)]
    all_to_all x2 -> x4, starting transfers between devices: 9.14 us -> 18.4 us  [in_plane_all(): lax.all_to_all(payload, ALL[1:], split_axis=0, concat_axis=0, tiled=True)]
    unnamed x108 -> x130, local copies, waits for them, and re-layouts: 9.67 us -> 16.2 us
    ppermute x1 -> x2, waiting for transfers between devices: 17.2 us -> 11.7 us  [to_row_owner(): return lax.ppermute(block, ALL, route)]
    all_to_all x0 -> x1, starting transfers between devices: none -> 4.27 us  [local(): lax.all_to_all(result_parts, ('x', 'seq'), split_axis=0, concat_axis=0, t...]
    ppermute x1 -> x2, starting transfers between devices: 2.45 us -> 5.72 us  [to_row_owner(): return lax.ppermute(block, ALL, route)]
    ppermute x8 -> x7, waiting for transfers between devices: 17.9 us -> 15.8 us  [flip_diagonal(): return lax.ppermute(value, ('x', 'seq'), [(i, i ^ 3) for i in range(4)])]
  transfers between devices with their start and end apart: 58 -> 58, of which waited for: 34 -> 24; matrix products, arithmetic and copies ran while one was open for 3% -> 5% of each run, Pallas kernels for 18% -> 22%
where the time goes in v3:
time: 284 us; the launch traced here: 282 us
  starting transfers between devices  86.7 us (31%)
  waiting for transfers between devices  85 us (30%)
  Pallas kernels  74.8 us (26%)
  local copies, waits for them, and re-layouts  17.9 us (6%)
  other arithmetic  16.5 us (6%)
    ppermute x18, waiting for transfers between devices, across(): lax.ppermute(value, 'data', [(d, d ^ bit) for d in range(lax.axis_size('d...  37.9 us
    pallas_call x12, Pallas kernels, call_half(): pl.pallas_call(body, grid=(2,), out_shape=tuple((jax.ShapeDtypeStruct(sha...  29.8 us
    ppermute x25, starting transfers between devices, flip(): return lax.ppermute(value, axis, SWAP)  25.1 us
    ppermute x18, starting transfers between devices, across(): lax.ppermute(value, 'data', [(d, d ^ bit) for d in range(lax.axis_size('d...  19.9 us
    all_to_all x4, starting transfers between devices, in_plane_all(): lax.all_to_all(payload, ALL[1:], split_axis=0, concat_axis=0, tiled=True)  18.4 us
    ppermute x25, waiting for transfers between devices, flip(): return lax.ppermute(value, axis, SWAP)  18.2 us
    unnamed x130, local copies, waits for them, and re-layouts  16.2 us
    ppermute x7, waiting for transfers between devices, flip_diagonal(): return lax.ppermute(value, ('x', 'seq'), [(i, i ^ 3) for i in range(4)])  15.8 us
  transfers between devices with their start and end apart: 58, of which 24 were waited for; matrix products, arithmetic and copies ran while one was open for 5% of the time, Pallas kernels for 22%

profile of v3, /device:TPU:2, one launch (start us, length us, event | category | flops | bytes accessed | tf_op | source)
XLA Modules:
  0.0 282.5 jit_solution(8107324666220320152)
XLA Ops:
  6.9 3.4 %collective-permute-start.5 = (bf16[160,1024]{1,0:T(8,128)(2,1)S(1)}, bf16[160,1024]{1,0:T(8,128)(2,1)}, u32[]{:S(2)}, u32[]{:S(2)}) collective-permute-start(bf16[160,1024]{1,0:T(8,128)(2,1)S(1)} %pad_maximum_fusion.8), channel_id=1, source_target_pairs={{0,0},{4,1},{8,2},{12,3},{16,4},{20,5},{24,6},{28,7},{1,8},{5,9},{... | collective-permute-start | bytes 983048 | tf_op jit(solution)/shard_map/ppermute | solution.py:68
  10.3 6.1 %all-to-all-start = ((bf16[8,32,512]{2,1,0:T(8,128)(2,1)}), bf16[8,32,512]{2,1,0:T(8,128)(2,1)S(1)}, u32[]{:S(2)}, u32[]{:S(2)}) async-start(bf16[8,32,512]{2,1,0:T(8,128)(2,1)} %shard_map.255), calls=%async_computation | async-start | bytes 524288 | tf_op jit(solution)/shard_map/all_to_all | solution.py:63
  19.1 4.3 %collective-permute-done = bf16[8,1024]{1,0:T(8,128)(2,1)S(1)} collective-permute-done((bf16[8,1024]{1,0:T(8,128)(2,1)}, bf16[8,1024]{1,0:T(8,128)(2,1)S(1)}, u32[]{:S(2)}, u32[]{:S(2)}) %collective-permute-start) | collective-permute-done | bytes 16416 | tf_op jit(solution)/shard_map/ppermute | solution.py:80
  24.1 3.7 %collective-permute-done.1 = bf16[8,1024]{1,0:T(8,128)(2,1)S(1)} collective-permute-done((bf16[8,1024]{1,0:T(8,128)(2,1)S(1)}, bf16[8,1024]{1,0:T(8,128)(2,1)S(1)}, u32[]{:S(2)}, u32[]{:S(2)}) %collective-permute-start.1) | collective-permute-done | bytes 16416 | tf_op jit(solution)/shard_map/ppermute | solution.py:80
  31.4 4.2 %all-to-all-start.1 = ((bf16[8,32,384]{2,1,0:T(8,128)(2,1)}), bf16[8,32,384]{2,1,0:T(8,128)(2,1)}, u32[]{:S(2)}, u32[]{:S(2)}) async-start(bf16[8,32,384]{2,1,0:T(8,128)(2,1)} %shard_map.257), calls=%async_computation.1 | async-start | bytes 393216 | tf_op jit(solution)/shard_map/all_to_all | solution.py:63
  36.9 3.6 %collective-permute-done.8 = bf16[8,1024]{1,0:T(8,128)(2,1)S(1)} collective-permute-done((bf16[8,1024]{1,0:T(8,128)(2,1)S(1)}, bf16[8,1024]{1,0:T(8,128)(2,1)S(1)}, u32[]{:S(2)}, u32[]{:S(2)}) %collective-permute-start.8) | collective-permute-done | bytes 16416 | tf_op jit(solution)/shard_map/ppermute | solution.py:45
  53.4 4.6 %all-to-all-start.2 = ((bf16[8,32,384]{2,1,0:T(8,128)(2,1)}), bf16[8,32,384]{2,1,0:T(8,128)(2,1)}, u32[]{:S(2)}, u32[]{:S(2)}) async-start(bf16[8,32,384]{2,1,0:T(8,128)(2,1)} %shard_map.259), calls=%async_computation.2 | async-start | bytes 393216 | tf_op jit(solution)/shard_map/all_to_all | solution.py:63
  77.0 4.0 %shard_map.261 = (bf16[1024,1024]{1,0:T(8,128)(2,1)S(1)}, f32[1024,384]{1,0:T(8,128)S(1)}, bf16[1024,512]{1,0:T(8,128)(2,1)S(1)}, bf16[1024,256]{1,0:T(8,128)(2,1)S(1)}) custom-call(s32[4]{0:T(128)S(1)} %copy-done.47, f32[4,8,128]{2,1,0:T(8,128)S(1)} %copy-done.44, bf16[4,128,1024]{2,1,0:T(8,128)(2,1)S(1)} %copy-done.19, bf16[1024,512]{1,0:T(8,128)(2,1)S(1)} %copy-done, ...), custom_call_target="tpu_custom_call" | custom-call | tf_op jit(solution)/shard_map/pallas_call | solution.py:136
  82.3 4.0 %shard_map.262 = (bf16[1024,1024]{1,0:T(8,128)(2,1)S(1)}, f32[1024,384]{1,0:T(8,128)S(1)}, bf16[1024,512]{1,0:T(8,128)(2,1)S(1)}, bf16[1024,256]{1,0:T(8,128)(2,1)S(1)}) custom-call(s32[4]{0:T(128)S(1)} %copy-done.47, f32[4,8,128]{2,1,0:T(8,128)S(1)} %copy-done.44, ...), custom_call_target="tpu_custom_call", output_to_operand_aliasing={{0}: (8, {}), {1}: (9, {}), {2}: (10, {}), {3}: (11, {})} | custom-call | tf_op jit(solution)/shard_map/pallas_call | solution.py:136
  88.7 2.7 shard_map.263
  101.0 6.9 %collective-permute-done.23.refs_1_ = bf16[1,256,384]{2,1,0:T(8,128)(2,1)S(1)} collective-permute-done((bf16[1,256,384]{2,1,0:T(8,128)(2,1)}, bf16[1,256,384]{2,1,0:T(8,128)(2,1)S(1)}, u32[]{:S(2)}, u32[]{:S(2)}) %collective-permute-start.23) | collective-permute-done | bytes 196640 | tf_op jit(solution)/shard_map/ppermute | solution.py:80
  122.7 3.6 %collective-permute-done.25 = bf16[128,1024]{1,0:T(8,128)(2,1)} collective-permute-done((bf16[128,1024]{1,0:T(8,128)(2,1)}, bf16[128,1024]{1,0:T(8,128)(2,1)}, u32[]{:S(2)}, u32[]{:S(2)}) %collective-permute-start.25) | collective-permute-done | bytes 262176 | tf_op jit(solution)/shard_map/ppermute | solution.py:45
  134.3 3.3 %shard_map.270 = (bf16[1024,1024]{1,0:T(8,128)(2,1)S(1)}, bf16[1024,384]{1,0:T(8,128)(2,1)S(1)}, bf16[1024,768]{1,0:T(8,128)(2,1)S(1)}, f32[4,128,1024]{2,1,0:T(8,128)S(1)}) custom-call(bf16[4,128,1024]{2,1,0:T(8,128)(2,1)S(1)} %copy-done.17, bf16[4,128,1024]{2,1,0:T(8,128)(2,1)S(1)} %pad_maximum_fusion.1.refs_1_.refs_0_, bf16[1024,384]{1,0:T(8,128)(2,1)S(1)} %copy-done.13, ...), custom_call_target="tpu_custom_call" | custom-call | tf_op jit(solution)/shard_map/pallas_call | solution.py:136
  137.6 4.3 %shard_map.271 = (bf16[1024,1024]{1,0:T(8,128)(2,1)S(1)}, bf16[1024,384]{1,0:T(8,128)(2,1)S(1)}, bf16[1024,768]{1,0:T(8,128)(2,1)S(1)}, bf16[4,128,1024]{2,1,0:T(8,128)(2,1)S(1)}) custom-call(bf16[4,128,1024]{2,1,0:T(8,128)(2,1)S(1)} %collective-permute-done.28.refs_0_, ...), custom_call_target="tpu_custom_call", output_to_operand_aliasing={{0}: (5, {}), {1}: (6, {}), {2}: (7, {})} | custom-call | tf_op jit(solution)/shard_map/pallas_call | solution.py:136
  143.5 3.8 %shard_map.276 = (f32[2,96,1024]{2,1,0:T(8,128)S(1)}, bf16[2,96,1024]{2,1,0:T(8,128)(2,1)S(1)}) custom-call(s32[4]{0:T(128)S(1)} %copy-done.48, bf16[1024,384]{1,0:T(8,128)(2,1)S(1)} %get-tuple-element.232.refs_0_.values, bf16[4,128,1024]{2,1,0:T(8,128)(2,1)S(1)} %pad_maximum_fusion.1.refs_1_.refs_0_, bf16[4,128,1024]{2,1,0:T(8,128)(2,1)} %collective-permute-done.29.refs_1_, ...), custom_call_target="tpu_custom_call" | custom-call | tf_op jit(solution)/shard_map/pallas_call | solution.py:565
  153.4 4.6 %shard_map.277 = (f32[2,256,768]{2,1,0:T(8,128)S(1)}, bf16[2,256,768]{2,1,0:T(8,128)(2,1)S(1)}) custom-call(s32[4]{0:T(128)S(1)} %copy-done.48, bf16[1024,1024]{1,0:T(8,128)(2,1)S(1)} %get-tuple-element.237.values, bf16[1024,768]{1,0:T(8,128)(2,1)S(1)} %get-tuple-element.238.refs_0_, f32[1,128]{1,0:T(1,128)S(1)} %broadcast_1_refs_2__refs_1_.2.refs_2_.refs_1_), custom_call_target="tpu_custom_call" | custom-call | tf_op jit(solution)/shard_map/pallas_call | solution.py:565
  159.7 4.5 %collective-permute-done.33.from_d = bf16[128,1024]{1,0:T(8,128)(2,1)S(1)} collective-permute-done((bf16[128,1024]{1,0:T(8,128)(2,1)S(1)}, bf16[128,1024]{1,0:T(8,128)(2,1)S(1)}, u32[]{:S(2)}, u32[]{:S(2)}) %collective-permute-start.33) | collective-permute-done | bytes 262176 | tf_op jit(solution)/shard_map/ppermute | solution.py:49
  171.1 5.1 %collective-permute-done.38 = bf16[128,1024]{1,0:T(8,128)(2,1)S(1)} collective-permute-done((bf16[128,1024]{1,0:T(8,128)(2,1)S(1)}, bf16[128,1024]{1,0:T(8,128)(2,1)S(1)}, u32[]{:S(2)}, u32[]{:S(2)}) %collective-permute-start.38) | collective-permute-done | bytes 262176 | tf_op jit(solution)/shard_map/ppermute | solution.py:49
  176.2 3.3 %collective-permute-done.37 = bf16[128,1024]{1,0:T(8,128)(2,1)S(1)} collective-permute-done((bf16[128,1024]{1,0:T(8,128)(2,1)S(1)}, bf16[128,1024]{1,0:T(8,128)(2,1)S(1)}, u32[]{:S(2)}, u32[]{:S(2)}) %collective-permute-start.37) | collective-permute-done | bytes 262176 | tf_op jit(solution)/shard_map/ppermute | solution.py:45
  179.7 7.2 %collective-permute-done.39.got = bf16[2,256,768]{2,1,0:T(8,128)(2,1)S(1)} collective-permute-done((bf16[2,256,768]{2,1,0:T(8,128)(2,1)S(1)}, bf16[2,256,768]{2,1,0:T(8,128)(2,1)S(1)}, u32[]{:S(2)}, u32[]{:S(2)}) %collective-permute-start.39) | collective-permute-done | bytes 786464 | tf_op jit(solution)/shard_map/ppermute | solution.py:80
  188.5 3.8 %collective-permute-start.42 = (bf16[96,1024]{1,0:T(8,128)(2,1)S(1)}, bf16[96,1024]{1,0:T(8,128)(2,1)S(1)}, u32[]{:S(2)}, u32[]{:S(2)}) collective-permute-start(bf16[96,1024]{1,0:T(8,128)(2,1)S(1)} %shard_map.287), channel_id=1, source_target_pairs={{0,0},{1,4},{2,8},{3,12},{4,16},{5,20},{6,24},{7,28},{8,1},{9,5},{... | collective-permute-start | bytes 589832 | tf_op jit(solution)/shard_map/ppermute | solution.py:109
  192.4 4.2 %shard_map.282 = (bf16[1024,512]{1,0:T(8,128)(2,1)S(1)}, f32[1,256]{1,0:T(1,128)S(1)}) custom-call(s32[4]{0:T(128)S(1)} %copy-done.48, f32[4,8,128]{2,1,0:T(8,128)S(1)} %copy-done.44, bf16[4,128,1024]{2,1,0:T(8,128)(2,1)S(1)} %pad_maximum_fusion.3.refs_2_.refs_0_, bf16[1024,512]{1,0:T(8,128)(2,1)S(1)} %copy-done.4, ...), custom_call_target="tpu_custom_call" | custom-call | tf_op jit(solution)/shard_map/pallas_call | solution.py:136
  196.6 4.2 %shard_map.283 = (bf16[1024,512]{1,0:T(8,128)(2,1)S(1)}, f32[1,256]{1,0:T(1,128)S(1)}) custom-call(s32[4]{0:T(128)S(1)} %copy-done.48, f32[4,8,128]{2,1,0:T(8,128)S(1)} %copy-done.44, bf16[4,128,1024]{2,1,0:T(8,128)(2,1)S(1)} %collective-permute-done.41.refs_2_.refs_1_, bf16[1024,512]{1,0:T(8,128)(2,1)S(1)} %copy-done.4, ...), custom_call_target="tpu_custom_call", output_to_operand_aliasing={{0}: (9, {})} | custom-call | tf_op jit(solution)/shard_map/pallas_call | solution.py:136
  204.5 4.1 %shard_map.286 = (f32[2,272,512]{2,1,0:T(8,128)S(1)}, bf16[2,272,512]{2,1,0:T(8,128)(2,1)}) custom-call(s32[4]{0:T(128)S(1)} %copy-done.48, bf16[1024,1024]{1,0:T(8,128)(2,1)S(1)} %copy-done.8, bf16[1024,512]{1,0:T(8,128)(2,1)S(1)} %get-tuple-element.259.refs_0_, f32[1,256]{1,0:T(1,128)S(1)} %add.44.refs_1_), custom_call_target="tpu_custom_call" | custom-call | tf_op jit(solution)/shard_map/pallas_call | solution.py:565
  210.5 7.6 %collective-permute-start.48 = (bf16[4,128,1024]{2,1,0:T(8,128)(2,1)}, bf16[4,128,1024]{2,1,0:T(8,128)(2,1)}, u32[]{:S(2)}, u32[]{:S(2)}) collective-permute-start(bf16[4,128,1024]{2,1,0:T(8,128)(2,1)} %shard_map.285), channel_id=1, source_target_pairs={{0,2},{2,0},{1,3},{3,1},{4,6},{6,4},{5,7},{7,5},{8,10},{10,8},{9,1... | collective-permute-start | bytes 3145736 | tf_op jit(solution)/shard_map/ppermute | solution.py:45
  218.2 4.3 %all-to-all-start.3 = ((bf16[4,128,1024]{2,1,0:T(8,128)(2,1)}), bf16[4,128,1024]{2,1,0:T(8,128)(2,1)}, u32[]{:S(2)}, u32[]{:S(2)}) async-start(bf16[4,128,1024]{2,1,0:T(8,128)(2,1)} %copy-done.28), calls=%async_computation.3 | async-start | bytes 2097152 | tf_op jit(solution)/shard_map/all_to_all | solution.py:826
  226.9 7.0 %collective-permute-done.44.got = bf16[2,272,512]{2,1,0:T(8,128)(2,1)} collective-permute-done((bf16[2,272,512]{2,1,0:T(8,128)(2,1)}, bf16[2,272,512]{2,1,0:T(8,128)(2,1)}, u32[]{:S(2)}, u32[]{:S(2)}) %collective-permute-start.44) | collective-permute-done | bytes 557088 | tf_op jit(solution)/shard_map/ppermute | solution.py:80
  241.5 2.9 %collective-permute-start.47 = (bf16[1,64,1024]{2,1,0:T(8,128)(2,1)S(1)}, bf16[1,64,1024]{2,1,0:T(8,128)(2,1)S(1)}, u32[]{:S(2)}, u32[]{:S(2)}) collective-permute-start(bf16[1,64,1024]{2,1,0:T(8,128)(2,1)S(1)} %get-tuple-element.281), channel_id=1, source_target_pairs={{0,16},{8,24},{16,0},{24,8},{1,17},{9,25},{17,1},{25,9},{2,18},{10... | collective-permute-start | bytes 393224 | tf_op jit(solution)/shard_map/ppermute | solution.py:80
  248.0 3.2 %collective-permute-done.51.from_d = bf16[128,1024]{1,0:T(8,128)(2,1)S(1)} collective-permute-done((bf16[128,1024]{1,0:T(8,128)(2,1)S(1)}, bf16[128,1024]{1,0:T(8,128)(2,1)S(1)}, u32[]{:S(2)}, u32[]{:S(2)}) %collective-permute-start.51) | collective-permute-done | bytes 262176 | tf_op jit(solution)/shard_map/ppermute | solution.py:49
  252.3 3.2 %collective-permute-done.47.refs_1_ = bf16[1,64,1024]{2,1,0:T(8,128)(2,1)S(1)} collective-permute-done((bf16[1,64,1024]{2,1,0:T(8,128)(2,1)S(1)}, bf16[1,64,1024]{2,1,0:T(8,128)(2,1)S(1)}, u32[]{:S(2)}, u32[]{:S(2)}) %collective-permute-start.47) | collective-permute-done | bytes 131104 | tf_op jit(solution)/shard_map/ppermute | solution.py:80
  256.6 3.5 %all-to-all-start.4 = ((bf16[8,40,1280]{2,1,0:T(8,128)(2,1)}), bf16[8,40,1280]{2,1,0:T(8,128)(2,1)S(1)}, u32[]{:S(2)}, u32[]{:S(2)}) async-start(bf16[8,40,1280]{2,1,0:T(8,128)(2,1)} %shard_map.293), calls=%async_computation.4 | async-start | bytes 1638400 | tf_op jit(solution)/shard_map/all_to_all | solution.py:63
  265.3 11.7 %collective-permute-done.52 = bf16[64,1024]{1,0:T(8,128)(2,1)S(1)} collective-permute-done((bf16[64,1024]{1,0:T(8,128)(2,1)S(1)}, bf16[64,1024]{1,0:T(8,128)(2,1)S(1)}, u32[]{:S(2)}, u32[]{:S(2)}) %collective-permute-start.52) | collective-permute-done | bytes 131104 | tf_op jit(solution)/shard_map/ppermute | solution.py:109
  (283 shorter events, 133.7 us)
Async XLA Ops:
  0.6 27.2 %collective-permute-start.4 = (bf16[128,1024]{1,0:T(8,128)(2,1)}, bf16[128,1024]{1,0:T(8,128)(2,1)S(1)}, u32[]{:S(2)}, u32[]{:S(2)}) collective-permute-start(bf16[128,1024]{1,0:T(8,128)(2,1)} %values.1), channel_id=1, source_target_pairs={{0,5},{1,4},{4,1},{5,0},{2,7},{3,6},{6,3},{7,2},{8,13},{9,12},{12,... | collective-permute-start | bytes 786440 | tf_op jit(solution)/shard_map/ppermute | solution.py:49
  2.2 25.7 %collective-permute-start.3 = (bf16[128,1024]{1,0:T(8,128)(2,1)}, bf16[128,1024]{1,0:T(8,128)(2,1)S(1)}, u32[]{:S(2)}, u32[]{:S(2)}) collective-permute-start(bf16[128,1024]{1,0:T(8,128)(2,1)} %values.1), channel_id=1, source_target_pairs={{0,4},{4,0},{1,5},{5,1},{2,6},{6,2},{3,7},{7,3},{8,12},{12,8},{9,1... | collective-permute-start | bytes 786440 | tf_op jit(solution)/shard_map/ppermute | solution.py:45
  3.7 24.2 %collective-permute-start.2 = (bf16[128,1024]{1,0:T(8,128)(2,1)}, bf16[128,1024]{1,0:T(8,128)(2,1)S(1)}, u32[]{:S(2)}, u32[]{:S(2)}) collective-permute-start(bf16[128,1024]{1,0:T(8,128)(2,1)} %values.1), channel_id=1, source_target_pairs={{0,1},{1,0},{2,3},{3,2},{4,5},{5,4},{6,7},{7,6},{8,9},{9,8},{10,11... | collective-permute-start | bytes 786440 | tf_op jit(solution)/shard_map/ppermute | solution.py:45
  6.9 22.1 %collective-permute-start.5 = (bf16[160,1024]{1,0:T(8,128)(2,1)S(1)}, bf16[160,1024]{1,0:T(8,128)(2,1)}, u32[]{:S(2)}, u32[]{:S(2)}) collective-permute-start(bf16[160,1024]{1,0:T(8,128)(2,1)S(1)} %pad_maximum_fusion.8), channel_id=1, source_target_pairs={{0,0},{4,1},{8,2},{12,3},{16,4},{20,5},{24,6},{28,7},{1,8},{5,9},{... | collective-permute-start | bytes 983048 | tf_op jit(solution)/shard_map/ppermute | solution.py:68
  10.3 18.7 %all-to-all-start = ((bf16[8,32,512]{2,1,0:T(8,128)(2,1)}), bf16[8,32,512]{2,1,0:T(8,128)(2,1)S(1)}, u32[]{:S(2)}, u32[]{:S(2)}) async-start(bf16[8,32,512]{2,1,0:T(8,128)(2,1)} %shard_map.255), calls=%async_computation | async-start | bytes 524288 | tf_op jit(solution)/shard_map/all_to_all | solution.py:63
  29.0 16.0 %collective-permute-start.10 = (bf16[4,128,1024]{2,1,0:T(8,128)(2,1)S(1)}, bf16[4,128,1024]{2,1,0:T(8,128)(2,1)S(1)}, u32[]{:S(2)}, u32[]{:S(2)}) collective-permute-start(bf16[4,128,1024]{2,1,0:T(8,128)(2,1)S(1)} %pad_maximum_fusion.refs_2_), channel_id=1, source_target_pairs={{0,2},{2,0},{1,3},{3,1},{4,6},{6,4},{5,7},{7,5},{8,10},{10,8},{9,1... | collective-permute-start | bytes 3145736 | tf_op jit(solution)/shard_map/ppermute | solution.py:45
  29.1 15.9 %collective-permute-start.6 = (bf16[1,256,512]{2,1,0:T(8,128)(2,1)S(1)}, bf16[1,256,512]{2,1,0:T(8,128)(2,1)S(1)}, u32[]{:S(2)}, u32[]{:S(2)}) collective-permute-start(bf16[1,256,512]{2,1,0:T(8,128)(2,1)S(1)} %bitcast.46), channel_id=1, source_target_pairs={{0,16},{8,24},{16,0},{24,8},{1,17},{9,25},{17,1},{25,9},{2,18},{10... | collective-permute-start | bytes 786440 | tf_op jit(solution)/shard_map/ppermute | solution.py:80
  31.4 13.6 %all-to-all-start.1 = ((bf16[8,32,384]{2,1,0:T(8,128)(2,1)}), bf16[8,32,384]{2,1,0:T(8,128)(2,1)}, u32[]{:S(2)}, u32[]{:S(2)}) async-start(bf16[8,32,384]{2,1,0:T(8,128)(2,1)} %shard_map.257), calls=%async_computation.1 | async-start | bytes 393216 | tf_op jit(solution)/shard_map/all_to_all | solution.py:63
  45.9 19.9 %collective-permute-start.11 = (bf16[2,256,512]{2,1,0:T(8,128)(2,1)}, bf16[2,256,512]{2,1,0:T(8,128)(2,1)S(1)}, u32[]{:S(2)}, u32[]{:S(2)}) collective-permute-start(bf16[2,256,512]{2,1,0:T(8,128)(2,1)} %pad_maximum_fusion.5), channel_id=1, source_target_pairs={{0,8},{8,0},{16,24},{24,16},{1,9},{9,1},{17,25},{25,17},{2,10},{10... | collective-permute-start | bytes 1572872 | tf_op jit(solution)/shard_map/ppermute | solution.py:80
  46.3 13.3 %collective-permute-start.15 = (bf16[128,1024]{1,0:T(8,128)(2,1)S(1)}, bf16[128,1024]{1,0:T(8,128)(2,1)}, u32[]{:S(2)}, u32[]{:S(2)}) collective-permute-start(bf16[128,1024]{1,0:T(8,128)(2,1)S(1)} %copy-done.31), channel_id=1, source_target_pairs={{0,5},{1,4},{4,1},{5,0},{2,7},{3,6},{6,3},{7,2},{8,13},{9,12},{12,... | collective-permute-start | bytes 786440 | tf_op jit(solution)/shard_map/ppermute | solution.py:49
  49.8 13.9 %collective-permute-start.12 = (bf16[1,160,1024]{2,1,0:T(8,128)(2,1)}, bf16[1,160,1024]{2,1,0:T(8,128)(2,1)}, u32[]{:S(2)}, u32[]{:S(2)}) collective-permute-start(bf16[1,160,1024]{2,1,0:T(8,128)(2,1)} %bitcast.15.refs_0_), channel_id=1, source_target_pairs={{0,16},{8,24},{16,0},{24,8},{1,17},{9,25},{17,1},{25,9},{2,18},{10... | collective-permute-start | bytes 983048 | tf_op jit(solution)/shard_map/ppermute | solution.py:80
  68.0 20.7 %collective-permute-start.16 = (bf16[2,160,1024]{2,1,0:T(8,128)(2,1)}, bf16[2,160,1024]{2,1,0:T(8,128)(2,1)}, u32[]{:S(2)}, u32[]{:S(2)}) collective-permute-start(bf16[2,160,1024]{2,1,0:T(8,128)(2,1)} %pad_maximum_fusion.4), channel_id=1, source_target_pairs={{0,8},{8,0},{16,24},{24,16},{1,9},{9,1},{17,25},{25,17},{2,10},{10... | collective-permute-start | bytes 1966088 | tf_op jit(solution)/shard_map/ppermute | solution.py:80
  69.8 18.8 %collective-permute-start.17 = (bf16[1,256,384]{2,1,0:T(8,128)(2,1)}, bf16[1,256,384]{2,1,0:T(8,128)(2,1)}, u32[]{:S(2)}, u32[]{:S(2)}) collective-permute-start(bf16[1,256,384]{2,1,0:T(8,128)(2,1)} %bitcast.14.refs_0_), channel_id=1, source_target_pairs={{0,16},{8,24},{16,0},{24,8},{1,17},{9,25},{17,1},{25,9},{2,18},{10... | collective-permute-start | bytes 589832 | tf_op jit(solution)/shard_map/ppermute | solution.py:80
  94.2 15.8 %collective-permute-start.22 = (bf16[2,256,384]{2,1,0:T(8,128)(2,1)S(1)}, bf16[2,256,384]{2,1,0:T(8,128)(2,1)S(1)}, u32[]{:S(2)}, u32[]{:S(2)}) collective-permute-start(bf16[2,256,384]{2,1,0:T(8,128)(2,1)S(1)} %pad_maximum_fusion.6), channel_id=1, source_target_pairs={{0,8},{8,0},{16,24},{24,16},{1,9},{9,1},{17,25},{25,17},{2,10},{10... | collective-permute-start | bytes 1179656 | tf_op jit(solution)/shard_map/ppermute | solution.py:80
  96.0 14.0 %collective-permute-start.19 = (bf16[128,1024]{1,0:T(8,128)(2,1)S(1)}, bf16[128,1024]{1,0:T(8,128)(2,1)S(1)}, u32[]{:S(2)}, u32[]{:S(2)}) collective-permute-start(bf16[128,1024]{1,0:T(8,128)(2,1)S(1)} %get-tuple-element.200), channel_id=1, source_target_pairs={{0,1},{1,0},{2,3},{3,2},{4,5},{5,4},{6,7},{7,6},{8,9},{9,8},{10,11... | collective-permute-start | bytes 786440 | tf_op jit(solution)/shard_map/ppermute | solution.py:45
  97.5 12.5 %collective-permute-start.20 = (bf16[128,1024]{1,0:T(8,128)(2,1)S(1)}, bf16[128,1024]{1,0:T(8,128)(2,1)S(1)}, u32[]{:S(2)}, u32[]{:S(2)}) collective-permute-start(bf16[128,1024]{1,0:T(8,128)(2,1)S(1)} %get-tuple-element.201), channel_id=1, source_target_pairs={{0,4},{4,0},{1,5},{5,1},{2,6},{6,2},{3,7},{7,3},{8,12},{12,8},{9,1... | collective-permute-start | bytes 786440 | tf_op jit(solution)/shard_map/ppermute | solution.py:45
  98.3 12.9 %collective-permute-start.21 = (bf16[128,1024]{1,0:T(8,128)(2,1)S(1)}, bf16[128,1024]{1,0:T(8,128)(2,1)S(1)}, u32[]{:S(2)}, u32[]{:S(2)}) collective-permute-start(bf16[128,1024]{1,0:T(8,128)(2,1)S(1)} %get-tuple-element.202), channel_id=1, source_target_pairs={{0,5},{1,4},{4,1},{5,0},{2,7},{3,6},{6,3},{7,2},{8,13},{9,12},{12,... | collective-permute-start | bytes 786440 | tf_op jit(solution)/shard_map/ppermute | solution.py:49
  118.6 18.9 %collective-permute-start.29 = (bf16[4,128,1024]{2,1,0:T(8,128)(2,1)S(1)}, bf16[4,128,1024]{2,1,0:T(8,128)(2,1)}, u32[]{:S(2)}, u32[]{:S(2)}) collective-permute-start(bf16[4,128,1024]{2,1,0:T(8,128)(2,1)S(1)} %pad_maximum_fusion.1.refs_1_.refs_0_), channel_id=1, source_target_pairs={{0,2},{2,0},{1,3},{3,1},{4,6},{6,4},{5,7},{7,5},{8,10},{10,8},{9,1... | collective-permute-start | bytes 3145736 | tf_op jit(solution)/shard_map/ppermute | solution.py:45
  143.4 14.7 %collective-permute-start.34 = (bf16[4,128,1024]{2,1,0:T(8,128)(2,1)S(1)}, bf16[4,128,1024]{2,1,0:T(8,128)(2,1)S(1)}, u32[]{:S(2)}, u32[]{:S(2)}) collective-permute-start(bf16[4,128,1024]{2,1,0:T(8,128)(2,1)S(1)} %shard_map.274), channel_id=1, source_target_pairs={{0,2},{2,0},{1,3},{3,1},{4,6},{6,4},{5,7},{7,5},{8,10},{10,8},{9,1... | collective-permute-start | bytes 3145736 | tf_op jit(solution)/shard_map/ppermute | solution.py:45
  151.2 13.0 %collective-permute-start.33 = (bf16[128,1024]{1,0:T(8,128)(2,1)S(1)}, bf16[128,1024]{1,0:T(8,128)(2,1)S(1)}, u32[]{:S(2)}, u32[]{:S(2)}) collective-permute-start(bf16[128,1024]{1,0:T(8,128)(2,1)S(1)} %get-tuple-element.231), channel_id=1, source_target_pairs={{0,5},{1,4},{4,1},{5,0},{2,7},{3,6},{6,3},{7,2},{8,13},{9,12},{12,... | collective-permute-start | bytes 786440 | tf_op jit(solution)/shard_map/ppermute | solution.py:49
  164.2 22.7 %collective-permute-start.39 = (bf16[2,256,768]{2,1,0:T(8,128)(2,1)S(1)}, bf16[2,256,768]{2,1,0:T(8,128)(2,1)S(1)}, u32[]{:S(2)}, u32[]{:S(2)}) collective-permute-start(bf16[2,256,768]{2,1,0:T(8,128)(2,1)S(1)} %get-tuple-element.248), channel_id=1, source_target_pairs={{0,8},{8,0},{16,24},{24,16},{1,9},{9,1},{17,25},{25,17},{2,10},{10... | collective-permute-start | bytes 2359304 | tf_op jit(solution)/shard_map/ppermute | solution.py:80
  169.6 17.5 %collective-permute-start.40 = (bf16[1,96,1024]{2,1,0:T(8,128)(2,1)S(1)}, bf16[1,96,1024]{2,1,0:T(8,128)(2,1)S(1)}, u32[]{:S(2)}, u32[]{:S(2)}) collective-permute-start(bf16[1,96,1024]{2,1,0:T(8,128)(2,1)S(1)} %get-tuple-element.254), channel_id=1, source_target_pairs={{0,16},{8,24},{16,0},{24,8},{1,17},{9,25},{17,1},{25,9},{2,18},{10... | collective-permute-start | bytes 589832 | tf_op jit(solution)/shard_map/ppermute | solution.py:80
  187.2 22.6 %collective-permute-start.43 = (bf16[1,256,768]{2,1,0:T(8,128)(2,1)S(1)}, bf16[1,256,768]{2,1,0:T(8,128)(2,1)S(1)}, u32[]{:S(2)}, u32[]{:S(2)}) collective-permute-start(bf16[1,256,768]{2,1,0:T(8,128)(2,1)S(1)} %get-tuple-element.268), channel_id=1, source_target_pairs={{0,16},{8,24},{16,0},{24,8},{1,17},{9,25},{17,1},{25,9},{2,18},{10... | collective-permute-start | bytes 1179656 | tf_op jit(solution)/shard_map/ppermute | solution.py:80
  188.5 21.2 %collective-permute-start.42 = (bf16[96,1024]{1,0:T(8,128)(2,1)S(1)}, bf16[96,1024]{1,0:T(8,128)(2,1)S(1)}, u32[]{:S(2)}, u32[]{:S(2)}) collective-permute-start(bf16[96,1024]{1,0:T(8,128)(2,1)S(1)} %shard_map.287), channel_id=1, source_target_pairs={{0,0},{1,4},{2,8},{3,12},{4,16},{5,20},{6,24},{7,28},{8,1},{9,5},{... | collective-permute-start | bytes 589832 | tf_op jit(solution)/shard_map/ppermute | solution.py:109
  210.5 26.0 %collective-permute-start.48 = (bf16[4,128,1024]{2,1,0:T(8,128)(2,1)}, bf16[4,128,1024]{2,1,0:T(8,128)(2,1)}, u32[]{:S(2)}, u32[]{:S(2)}) collective-permute-start(bf16[4,128,1024]{2,1,0:T(8,128)(2,1)} %shard_map.285), channel_id=1, source_target_pairs={{0,2},{2,0},{1,3},{3,1},{4,6},{6,4},{5,7},{7,5},{8,10},{10,8},{9,1... | collective-permute-start | bytes 3145736 | tf_op jit(solution)/shard_map/ppermute | solution.py:45
  218.1 15.8 %collective-permute-start.44 = (bf16[2,272,512]{2,1,0:T(8,128)(2,1)}, bf16[2,272,512]{2,1,0:T(8,128)(2,1)}, u32[]{:S(2)}, u32[]{:S(2)}) collective-permute-start(bf16[2,272,512]{2,1,0:T(8,128)(2,1)} %get-tuple-element.270), channel_id=1, source_target_pairs={{0,8},{8,0},{16,24},{24,16},{1,9},{9,1},{17,25},{25,17},{2,10},{10... | collective-permute-start | bytes 1671176 | tf_op jit(solution)/shard_map/ppermute | solution.py:80
  218.2 38.4 %all-to-all-start.3 = ((bf16[4,128,1024]{2,1,0:T(8,128)(2,1)}), bf16[4,128,1024]{2,1,0:T(8,128)(2,1)}, u32[]{:S(2)}, u32[]{:S(2)}) async-start(bf16[4,128,1024]{2,1,0:T(8,128)(2,1)} %copy-done.28), calls=%async_computation.3 | async-start | bytes 2097152 | tf_op jit(solution)/shard_map/all_to_all | solution.py:826
  224.9 16.6 %collective-permute-start.46 = (bf16[2,64,1024]{2,1,0:T(8,128)(2,1)S(1)}, bf16[2,64,1024]{2,1,0:T(8,128)(2,1)S(1)}, u32[]{:S(2)}, u32[]{:S(2)}) collective-permute-start(bf16[2,64,1024]{2,1,0:T(8,128)(2,1)S(1)} %get-tuple-element.277), channel_id=1, source_target_pairs={{0,8},{8,0},{16,24},{24,16},{1,9},{9,1},{17,25},{25,17},{2,10},{10... | collective-permute-start | bytes 786440 | tf_op jit(solution)/shard_map/ppermute | solution.py:80
  236.3 19.2 %collective-permute-start.45 = (bf16[1,272,512]{2,1,0:T(8,128)(2,1)S(1)}, bf16[1,272,512]{2,1,0:T(8,128)(2,1)S(1)}, u32[]{:S(2)}, u32[]{:S(2)}) collective-permute-start(bf16[1,272,512]{2,1,0:T(8,128)(2,1)S(1)} %get-tuple-element.274), channel_id=1, source_target_pairs={{0,16},{8,24},{16,0},{24,8},{1,17},{9,25},{17,1},{25,9},{2,18},{10... | collective-permute-start | bytes 835592 | tf_op jit(solution)/shard_map/ppermute | solution.py:80
  241.5 14.0 %collective-permute-start.47 = (bf16[1,64,1024]{2,1,0:T(8,128)(2,1)S(1)}, bf16[1,64,1024]{2,1,0:T(8,128)(2,1)S(1)}, u32[]{:S(2)}, u32[]{:S(2)}) collective-permute-start(bf16[1,64,1024]{2,1,0:T(8,128)(2,1)S(1)} %get-tuple-element.281), channel_id=1, source_target_pairs={{0,16},{8,24},{16,0},{24,8},{1,17},{9,25},{17,1},{25,9},{2,18},{10... | collective-permute-start | bytes 393224 | tf_op jit(solution)/shard_map/ppermute | solution.py:80
  256.6 21.1 %all-to-all-start.4 = ((bf16[8,40,1280]{2,1,0:T(8,128)(2,1)}), bf16[8,40,1280]{2,1,0:T(8,128)(2,1)S(1)}, u32[]{:S(2)}, u32[]{:S(2)}) async-start(bf16[8,40,1280]{2,1,0:T(8,128)(2,1)} %shard_map.293), calls=%async_computation.4 | async-start | bytes 1638400 | tf_op jit(solution)/shard_map/all_to_all | solution.py:63
  260.3 16.7 %collective-permute-start.52 = (bf16[64,1024]{1,0:T(8,128)(2,1)S(1)}, bf16[64,1024]{1,0:T(8,128)(2,1)S(1)}, u32[]{:S(2)}, u32[]{:S(2)}) collective-permute-start(bf16[64,1024]{1,0:T(8,128)(2,1)S(1)} %shard_map.295), channel_id=1, source_target_pairs={{0,0},{1,4},{2,8},{3,12},{4,16},{5,20},{6,24},{7,28},{8,1},{9,5},{... | collective-permute-start | bytes 393224 | tf_op jit(solution)/shard_map/ppermute | solution.py:109
  (91 other events, 892.0 us)

commit v4 on v3

--- a/solution.py
+++ b/solution.py
@@ -282,7 +282,8 @@
             sums = sums + jnp.sum(piece * kept, axis=1, keepdims=True)
             at += width
         line = line + got[j, rows : rows + 8, : 2 * HEAD_SIZE].astype(F32)
-    gain_out[...] = sums / gain[...]
+    sums = jnp.broadcast_to(sums / gain[...], (rows, 128))
+    gain_out[...] = jnp.transpose(sums)[0:1]
     each = head_gains.shape[1]
     for k in range(2):
         part = line[0:1, k * HEAD_SIZE : (k + 1) * HEAD_SIZE]
@@ -292,7 +293,7 @@
 
 def unpack(got, start, gain, scalars, gains, *weights):
     widths = [w.shape[1] // 8 for w in weights]
-    outs = [(w.shape, F32) for w in weights] + [((gain.shape[0], 1), F32), ((2, gains), F32)]
+    outs = [(w.shape, F32) for w in weights] + [((1, gain.shape[0]), F32), ((2, gains), F32)]
     vmem = pl.BlockSpec(memory_space=pltpu.VMEM)
     *grads, gain_grad, head_gains = pl.pallas_call(
         functools.partial(unpack_kernel, widths, start),
@@ -301,7 +302,7 @@
         out_specs=tuple(vmem for _ in outs),
         compiler_params=pltpu.CompilerParams(vmem_limit_bytes=12 * 2**20),
     )(scalars, got, gain.astype(F32)[:, None], *weights)
-    return grads, gain_grad[:, 0], head_gains
+    return grads, gain_grad[0], head_gains
 
 
 def merge_kernel(near, other, own, to_y, to_x, to_d):
@@ -681,13 +682,13 @@
     got = in_plane_all(payload).reshape(8 * w_rows, -1)
     marks = data_sum(data_sum(marks), last=True)
     near = gather_chips(tokens)
-    payload, row_weights = together(payload, jnp.concatenate([w_output, w_down]))
-    row_weights = to_row_place(row_weights, count)
+    row_weights = jnp.concatenate([w_output, w_down])
     got, marks, near, row_weights, cot, gate, up = together(
         got, marks, near, row_weights, cotangent, w_gate, w_up
     )
 
     qkv = double([got[None]])
+    row_weights = to_row_place(row_weights, count)
     marks = plane_sum(marks)
     far = flip(near, "core")
     gate = in_plane_all(pack(gate)).reshape(1, 8 * w_rows, -1)

time: 284 us -> 283 us (level)
  waiting for transfers between devices: 85 us -> 80.8 us
  starting transfers between devices: 86.7 us -> 90.8 us
    ppermute x18, starting transfers between devices: 19.9 us -> 26.1 us  [across(): lax.ppermute(value, 'data', [(d, d ^ bit) for d in range(lax.axis_size('d...]
    ppermute x18, waiting for transfers between devices: 37.9 us -> 33.2 us  [across(): lax.ppermute(value, 'data', [(d, d ^ bit) for d in range(lax.axis_size('d...]
where the time goes in v4:
time: 283 us; the launch traced here: 281 us
  starting transfers between devices  90.8 us (32%)
  waiting for transfers between devices  80.8 us (29%)
  Pallas kernels  74.8 us (26%)
  local copies, waits for them, and re-layouts  17.9 us (6%)
  other arithmetic  15.2 us (5%)
    ppermute x18, waiting for transfers between devices, across(): lax.ppermute(value, 'data', [(d, d ^ bit) for d in range(lax.axis_size('d...  33.2 us
    pallas_call x12, Pallas kernels, call_half(): pl.pallas_call(body, grid=(2,), out_shape=tuple((jax.ShapeDtypeStruct(sha...  29.8 us
    ppermute x25, starting transfers between devices, flip(): return lax.ppermute(value, axis, SWAP)  26.2 us
    ppermute x18, starting transfers between devices, across(): lax.ppermute(value, 'data', [(d, d ^ bit) for d in range(lax.axis_size('d...  26.1 us
    ppermute x25, waiting for transfers between devices, flip(): return lax.ppermute(value, axis, SWAP)  20.7 us
    all_to_all x4, starting transfers between devices, in_plane_all(): lax.all_to_all(payload, ALL[1:], split_axis=0, concat_axis=0, tiled=True)  16.9 us
    unnamed x130, local copies, waits for them, and re-layouts  16.2 us
    ppermute x7, waiting for transfers between devices, flip_diagonal(): return lax.ppermute(value, ('x', 'seq'), [(i, i ^ 3) for i in range(4)])  15 us
  transfers between devices with their start and end apart: 58, of which 24 were waited for; matrix products, arithmetic and copies ran while one was open for 5% of the time, Pallas kernels for 22%

profile of v4, /device:TPU:2, one launch (start us, length us, event | category | flops | bytes accessed | tf_op | source)
XLA Modules:
  0.0 281.2 jit_solution(8181125635575439210)
XLA Ops:
  10.6 4.3 %all-to-all-start = ((bf16[8,32,512]{2,1,0:T(8,128)(2,1)}), bf16[8,32,512]{2,1,0:T(8,128)(2,1)S(1)}, u32[]{:S(2)}, u32[]{:S(2)}) async-start(bf16[8,32,512]{2,1,0:T(8,128)(2,1)} %shard_map.255), calls=%async_computation | async-start | bytes 524288 | tf_op jit(solution)/shard_map/all_to_all | solution.py:63
  20.6 3.4 %collective-permute-start.10 = (bf16[160,1024]{1,0:T(8,128)(2,1)S(1)}, bf16[160,1024]{1,0:T(8,128)(2,1)}, u32[]{:S(2)}, u32[]{:S(2)}) collective-permute-start(bf16[160,1024]{1,0:T(8,128)(2,1)S(1)} %pad_maximum_fusion.8), channel_id=1, source_target_pairs={{0,0},{4,1},{8,2},{12,3},{16,4},{20,5},{24,6},{28,7},{1,8},{5,9},{... | collective-permute-start | bytes 983048 | tf_op jit(solution)/shard_map/ppermute | solution.py:68
  28.0 4.5 %all-to-all-start.1 = ((bf16[8,32,384]{2,1,0:T(8,128)(2,1)}), bf16[8,32,384]{2,1,0:T(8,128)(2,1)}, u32[]{:S(2)}, u32[]{:S(2)}) async-start(bf16[8,32,384]{2,1,0:T(8,128)(2,1)} %shard_map.257), calls=%async_computation.1 | async-start | bytes 393216 | tf_op jit(solution)/shard_map/all_to_all | solution.py:63
  33.9 3.6 %collective-permute-done.7 = bf16[8,1024]{1,0:T(8,128)(2,1)S(1)} collective-permute-done((bf16[8,1024]{1,0:T(8,128)(2,1)S(1)}, bf16[8,1024]{1,0:T(8,128)(2,1)S(1)}, u32[]{:S(2)}, u32[]{:S(2)}) %collective-permute-start.7) | collective-permute-done | bytes 16416 | tf_op jit(solution)/shard_map/ppermute | solution.py:45
  41.9 3.8 %collective-permute-done.5.refs_1_ = bf16[1,256,512]{2,1,0:T(8,128)(2,1)S(1)} collective-permute-done((bf16[1,256,512]{2,1,0:T(8,128)(2,1)S(1)}, bf16[1,256,512]{2,1,0:T(8,128)(2,1)S(1)}, u32[]{:S(2)}, u32[]{:S(2)}) %collective-permute-start.5) | collective-permute-done | bytes 262176 | tf_op jit(solution)/shard_map/ppermute | solution.py:80
  51.8 4.5 %all-to-all-start.2 = ((bf16[8,32,384]{2,1,0:T(8,128)(2,1)}), bf16[8,32,384]{2,1,0:T(8,128)(2,1)}, u32[]{:S(2)}, u32[]{:S(2)}) async-start(bf16[8,32,384]{2,1,0:T(8,128)(2,1)} %shard_map.259), calls=%async_computation.2 | async-start | bytes 393216 | tf_op jit(solution)/shard_map/all_to_all | solution.py:63
  66.2 2.7 collective-permute-start.16
  76.4 4.0 %shard_map.261 = (bf16[1024,1024]{1,0:T(8,128)(2,1)S(1)}, f32[1024,384]{1,0:T(8,128)S(1)}, bf16[1024,512]{1,0:T(8,128)(2,1)S(1)}, bf16[1024,256]{1,0:T(8,128)(2,1)S(1)}) custom-call(s32[4]{0:T(128)S(1)} %copy-done.47, f32[4,8,128]{2,1,0:T(8,128)S(1)} %copy-done.44, bf16[4,128,1024]{2,1,0:T(8,128)(2,1)S(1)} %copy-done.19, bf16[1024,512]{1,0:T(8,128)(2,1)S(1)} %copy-done, ...), custom_call_target="tpu_custom_call" | custom-call | tf_op jit(solution)/shard_map/pallas_call | solution.py:136
  81.7 4.0 %shard_map.262 = (bf16[1024,1024]{1,0:T(8,128)(2,1)S(1)}, f32[1024,384]{1,0:T(8,128)S(1)}, bf16[1024,512]{1,0:T(8,128)(2,1)S(1)}, bf16[1024,256]{1,0:T(8,128)(2,1)S(1)}) custom-call(s32[4]{0:T(128)S(1)} %copy-done.47, f32[4,8,128]{2,1,0:T(8,128)S(1)} %copy-done.44, ...), custom_call_target="tpu_custom_call", output_to_operand_aliasing={{0}: (8, {}), {1}: (9, {}), {2}: (10, {}), {3}: (11, {})} | custom-call | tf_op jit(solution)/shard_map/pallas_call | solution.py:136
  88.0 2.7 shard_map.263
  101.6 9.8 %collective-permute-done.23.refs_1_ = bf16[1,256,384]{2,1,0:T(8,128)(2,1)S(1)} collective-permute-done((bf16[1,256,384]{2,1,0:T(8,128)(2,1)}, bf16[1,256,384]{2,1,0:T(8,128)(2,1)S(1)}, u32[]{:S(2)}, u32[]{:S(2)}) %collective-permute-start.23) | collective-permute-done | bytes 196640 | tf_op jit(solution)/shard_map/ppermute | solution.py:80
  123.1 3.4 %collective-permute-done.25 = bf16[128,1024]{1,0:T(8,128)(2,1)} collective-permute-done((bf16[128,1024]{1,0:T(8,128)(2,1)}, bf16[128,1024]{1,0:T(8,128)(2,1)}, u32[]{:S(2)}, u32[]{:S(2)}) %collective-permute-start.25) | collective-permute-done | bytes 262176 | tf_op jit(solution)/shard_map/ppermute | solution.py:45
  134.8 3.3 %shard_map.270 = (bf16[1024,1024]{1,0:T(8,128)(2,1)S(1)}, bf16[1024,384]{1,0:T(8,128)(2,1)S(1)}, bf16[1024,768]{1,0:T(8,128)(2,1)S(1)}, f32[4,128,1024]{2,1,0:T(8,128)S(1)}) custom-call(bf16[4,128,1024]{2,1,0:T(8,128)(2,1)S(1)} %copy-done.17, bf16[4,128,1024]{2,1,0:T(8,128)(2,1)S(1)} %pad_maximum_fusion.1.refs_1_.refs_0_, bf16[1024,384]{1,0:T(8,128)(2,1)S(1)} %copy-done.13, ...), custom_call_target="tpu_custom_call" | custom-call | tf_op jit(solution)/shard_map/pallas_call | solution.py:136
  138.1 4.3 %shard_map.271 = (bf16[1024,1024]{1,0:T(8,128)(2,1)S(1)}, bf16[1024,384]{1,0:T(8,128)(2,1)S(1)}, bf16[1024,768]{1,0:T(8,128)(2,1)S(1)}, bf16[4,128,1024]{2,1,0:T(8,128)(2,1)S(1)}) custom-call(bf16[4,128,1024]{2,1,0:T(8,128)(2,1)S(1)} %collective-permute-done.28.refs_0_, ...), custom_call_target="tpu_custom_call", output_to_operand_aliasing={{0}: (5, {}), {1}: (6, {}), {2}: (7, {})} | custom-call | tf_op jit(solution)/shard_map/pallas_call | solution.py:136
  144.1 3.8 %shard_map.276 = (f32[2,96,1024]{2,1,0:T(8,128)S(1)}, bf16[2,96,1024]{2,1,0:T(8,128)(2,1)S(1)}) custom-call(s32[4]{0:T(128)S(1)} %copy-done.48, bf16[1024,384]{1,0:T(8,128)(2,1)S(1)} %get-tuple-element.230.refs_0_.values, bf16[4,128,1024]{2,1,0:T(8,128)(2,1)S(1)} %pad_maximum_fusion.1.refs_1_.refs_0_, bf16[4,128,1024]{2,1,0:T(8,128)(2,1)} %collective-permute-done.29.refs_1_, ...), custom_call_target="tpu_custom_call" | custom-call | tf_op jit(solution)/shard_map/pallas_call | solution.py:566
  153.3 4.6 %shard_map.277 = (f32[2,256,768]{2,1,0:T(8,128)S(1)}, bf16[2,256,768]{2,1,0:T(8,128)(2,1)S(1)}) custom-call(s32[4]{0:T(128)S(1)} %copy-done.48, bf16[1024,1024]{1,0:T(8,128)(2,1)S(1)} %get-tuple-element.235.values, bf16[1024,768]{1,0:T(8,128)(2,1)S(1)} %get-tuple-element.236.refs_0_, f32[1,128]{1,0:T(1,128)S(1)} %broadcast_1_refs_2__refs_1_.2.refs_2_.refs_1_), custom_call_target="tpu_custom_call" | custom-call | tf_op jit(solution)/shard_map/pallas_call | solution.py:566
  159.6 4.5 %collective-permute-done.33.from_d = bf16[128,1024]{1,0:T(8,128)(2,1)S(1)} collective-permute-done((bf16[128,1024]{1,0:T(8,128)(2,1)S(1)}, bf16[128,1024]{1,0:T(8,128)(2,1)S(1)}, u32[]{:S(2)}, u32[]{:S(2)}) %collective-permute-start.33) | collective-permute-done | bytes 262176 | tf_op jit(solution)/shard_map/ppermute | solution.py:49
  171.9 4.8 %collective-permute-done.38 = bf16[128,1024]{1,0:T(8,128)(2,1)S(1)} collective-permute-done((bf16[128,1024]{1,0:T(8,128)(2,1)S(1)}, bf16[128,1024]{1,0:T(8,128)(2,1)S(1)}, u32[]{:S(2)}, u32[]{:S(2)}) %collective-permute-start.38) | collective-permute-done | bytes 262176 | tf_op jit(solution)/shard_map/ppermute | solution.py:49
  176.8 3.0 %collective-permute-done.37 = bf16[128,1024]{1,0:T(8,128)(2,1)S(1)} collective-permute-done((bf16[128,1024]{1,0:T(8,128)(2,1)S(1)}, bf16[128,1024]{1,0:T(8,128)(2,1)S(1)}, u32[]{:S(2)}, u32[]{:S(2)}) %collective-permute-start.37) | collective-permute-done | bytes 262176 | tf_op jit(solution)/shard_map/ppermute | solution.py:45
  180.2 6.5 %collective-permute-done.39.got = bf16[2,256,768]{2,1,0:T(8,128)(2,1)S(1)} collective-permute-done((bf16[2,256,768]{2,1,0:T(8,128)(2,1)S(1)}, bf16[2,256,768]{2,1,0:T(8,128)(2,1)S(1)}, u32[]{:S(2)}, u32[]{:S(2)}) %collective-permute-start.39) | collective-permute-done | bytes 786464 | tf_op jit(solution)/shard_map/ppermute | solution.py:80
  189.1 2.9 %collective-permute-start.42 = (bf16[96,1024]{1,0:T(8,128)(2,1)S(1)}, bf16[96,1024]{1,0:T(8,128)(2,1)S(1)}, u32[]{:S(2)}, u32[]{:S(2)}) collective-permute-start(bf16[96,1024]{1,0:T(8,128)(2,1)S(1)} %shard_map.287), channel_id=1, source_target_pairs={{0,0},{1,4},{2,8},{3,12},{4,16},{5,20},{6,24},{7,28},{8,1},{9,5},{... | collective-permute-start | bytes 589832 | tf_op jit(solution)/shard_map/ppermute | solution.py:109
  192.0 4.2 %shard_map.282 = (bf16[1024,512]{1,0:T(8,128)(2,1)S(1)}, f32[1,256]{1,0:T(1,128)S(1)}) custom-call(s32[4]{0:T(128)S(1)} %copy-done.48, f32[4,8,128]{2,1,0:T(8,128)S(1)} %copy-done.44, bf16[4,128,1024]{2,1,0:T(8,128)(2,1)S(1)} %pad_maximum_fusion.3.refs_2_.refs_0_, bf16[1024,512]{1,0:T(8,128)(2,1)S(1)} %copy-done.4, ...), custom_call_target="tpu_custom_call" | custom-call | tf_op jit(solution)/shard_map/pallas_call | solution.py:136
  196.3 4.2 %shard_map.283 = (bf16[1024,512]{1,0:T(8,128)(2,1)S(1)}, f32[1,256]{1,0:T(1,128)S(1)}) custom-call(s32[4]{0:T(128)S(1)} %copy-done.48, f32[4,8,128]{2,1,0:T(8,128)S(1)} %copy-done.44, bf16[4,128,1024]{2,1,0:T(8,128)(2,1)S(1)} %collective-permute-done.41.refs_2_.refs_1_, bf16[1024,512]{1,0:T(8,128)(2,1)S(1)} %copy-done.4, ...), custom_call_target="tpu_custom_call", output_to_operand_aliasing={{0}: (9, {})} | custom-call | tf_op jit(solution)/shard_map/pallas_call | solution.py:136
  204.2 4.2 %shard_map.286 = (f32[2,272,512]{2,1,0:T(8,128)S(1)}, bf16[2,272,512]{2,1,0:T(8,128)(2,1)}) custom-call(s32[4]{0:T(128)S(1)} %copy-done.48, bf16[1024,1024]{1,0:T(8,128)(2,1)S(1)} %copy-done.8, bf16[1024,512]{1,0:T(8,128)(2,1)S(1)} %get-tuple-element.257.refs_0_, f32[1,256]{1,0:T(1,128)S(1)} %add.44.refs_1_), custom_call_target="tpu_custom_call" | custom-call | tf_op jit(solution)/shard_map/pallas_call | solution.py:566
  210.1 7.5 %collective-permute-start.48 = (bf16[4,128,1024]{2,1,0:T(8,128)(2,1)}, bf16[4,128,1024]{2,1,0:T(8,128)(2,1)}, u32[]{:S(2)}, u32[]{:S(2)}) collective-permute-start(bf16[4,128,1024]{2,1,0:T(8,128)(2,1)} %shard_map.285), channel_id=1, source_target_pairs={{0,2},{2,0},{1,3},{3,1},{4,6},{6,4},{5,7},{7,5},{8,10},{10,8},{9,1... | collective-permute-start | bytes 3145736 | tf_op jit(solution)/shard_map/ppermute | solution.py:45
  217.8 4.3 %all-to-all-start.3 = ((bf16[4,128,1024]{2,1,0:T(8,128)(2,1)}), bf16[4,128,1024]{2,1,0:T(8,128)(2,1)}, u32[]{:S(2)}, u32[]{:S(2)}) async-start(bf16[4,128,1024]{2,1,0:T(8,128)(2,1)} %copy-done.28), calls=%async_computation.3 | async-start | bytes 2097152 | tf_op jit(solution)/shard_map/all_to_all | solution.py:827
  226.5 7.0 %collective-permute-done.44.got = bf16[2,272,512]{2,1,0:T(8,128)(2,1)} collective-permute-done((bf16[2,272,512]{2,1,0:T(8,128)(2,1)}, bf16[2,272,512]{2,1,0:T(8,128)(2,1)}, u32[]{:S(2)}, u32[]{:S(2)}) %collective-permute-start.44) | collective-permute-done | bytes 557088 | tf_op jit(solution)/shard_map/ppermute | solution.py:80
  241.4 2.6 collective-permute-start.47
  245.8 3.0 %collective-permute-done.50.from_x = bf16[128,1024]{1,0:T(8,128)(2,1)S(1)} collective-permute-done((bf16[128,1024]{1,0:T(8,128)(2,1)S(1)}, bf16[128,1024]{1,0:T(8,128)(2,1)S(1)}, u32[]{:S(2)}, u32[]{:S(2)}) %collective-permute-start.50) | collective-permute-done | bytes 262176 | tf_op jit(solution)/shard_map/ppermute | solution.py:45
  248.8 3.2 %collective-permute-done.51.from_d = bf16[128,1024]{1,0:T(8,128)(2,1)S(1)} collective-permute-done((bf16[128,1024]{1,0:T(8,128)(2,1)S(1)}, bf16[128,1024]{1,0:T(8,128)(2,1)S(1)}, u32[]{:S(2)}, u32[]{:S(2)}) %collective-permute-start.51) | collective-permute-done | bytes 262176 | tf_op jit(solution)/shard_map/ppermute | solution.py:49
  256.2 3.7 %all-to-all-start.4 = ((bf16[8,40,1280]{2,1,0:T(8,128)(2,1)}), bf16[8,40,1280]{2,1,0:T(8,128)(2,1)S(1)}, u32[]{:S(2)}, u32[]{:S(2)}) async-start(bf16[8,40,1280]{2,1,0:T(8,128)(2,1)} %shard_map.293), calls=%async_computation.4 | async-start | bytes 1638400 | tf_op jit(solution)/shard_map/all_to_all | solution.py:63
  265.1 11.9 %collective-permute-done.52 = bf16[64,1024]{1,0:T(8,128)(2,1)S(1)} collective-permute-done((bf16[64,1024]{1,0:T(8,128)(2,1)S(1)}, bf16[64,1024]{1,0:T(8,128)(2,1)S(1)}, u32[]{:S(2)}, u32[]{:S(2)}) %collective-permute-start.52) | collective-permute-done | bytes 131104 | tf_op jit(solution)/shard_map/ppermute | solution.py:109
  (281 shorter events, 135.3 us)
Async XLA Ops:
  0.6 18.7 %collective-permute-start.4 = (bf16[128,1024]{1,0:T(8,128)(2,1)}, bf16[128,1024]{1,0:T(8,128)(2,1)S(1)}, u32[]{:S(2)}, u32[]{:S(2)}) collective-permute-start(bf16[128,1024]{1,0:T(8,128)(2,1)} %values.1), channel_id=1, source_target_pairs={{0,5},{1,4},{4,1},{5,0},{2,7},{3,6},{6,3},{7,2},{8,13},{9,12},{12,... | collective-permute-start | bytes 786440 | tf_op jit(solution)/shard_map/ppermute | solution.py:49
  2.2 17.2 %collective-permute-start.3 = (bf16[128,1024]{1,0:T(8,128)(2,1)}, bf16[128,1024]{1,0:T(8,128)(2,1)S(1)}, u32[]{:S(2)}, u32[]{:S(2)}) collective-permute-start(bf16[128,1024]{1,0:T(8,128)(2,1)} %values.1), channel_id=1, source_target_pairs={{0,4},{4,0},{1,5},{5,1},{2,6},{6,2},{3,7},{7,3},{8,12},{12,8},{9,1... | collective-permute-start | bytes 786440 | tf_op jit(solution)/shard_map/ppermute | solution.py:45
  3.7 15.7 %collective-permute-start.2 = (bf16[128,1024]{1,0:T(8,128)(2,1)}, bf16[128,1024]{1,0:T(8,128)(2,1)S(1)}, u32[]{:S(2)}, u32[]{:S(2)}) collective-permute-start(bf16[128,1024]{1,0:T(8,128)(2,1)} %values.1), channel_id=1, source_target_pairs={{0,1},{1,0},{2,3},{3,2},{4,5},{5,4},{6,7},{7,6},{8,9},{9,8},{10,11... | collective-permute-start | bytes 786440 | tf_op jit(solution)/shard_map/ppermute | solution.py:45
  20.5 25.2 %collective-permute-start.9 = (bf16[4,128,1024]{2,1,0:T(8,128)(2,1)S(1)}, bf16[4,128,1024]{2,1,0:T(8,128)(2,1)S(1)}, u32[]{:S(2)}, u32[]{:S(2)}) collective-permute-start(bf16[4,128,1024]{2,1,0:T(8,128)(2,1)S(1)} %pad_maximum_fusion.refs_2_), channel_id=1, source_target_pairs={{0,2},{2,0},{1,3},{3,1},{4,6},{6,4},{5,7},{7,5},{8,10},{10,8},{9,1... | collective-permute-start | bytes 3145736 | tf_op jit(solution)/shard_map/ppermute | solution.py:45
  20.6 25.1 %collective-permute-start.10 = (bf16[160,1024]{1,0:T(8,128)(2,1)S(1)}, bf16[160,1024]{1,0:T(8,128)(2,1)}, u32[]{:S(2)}, u32[]{:S(2)}) collective-permute-start(bf16[160,1024]{1,0:T(8,128)(2,1)S(1)} %pad_maximum_fusion.8), channel_id=1, source_target_pairs={{0,0},{4,1},{8,2},{12,3},{16,4},{20,5},{24,6},{28,7},{1,8},{5,9},{... | collective-permute-start | bytes 983048 | tf_op jit(solution)/shard_map/ppermute | solution.py:68
  24.0 21.7 %collective-permute-start.5 = (bf16[1,256,512]{2,1,0:T(8,128)(2,1)S(1)}, bf16[1,256,512]{2,1,0:T(8,128)(2,1)S(1)}, u32[]{:S(2)}, u32[]{:S(2)}) collective-permute-start(bf16[1,256,512]{2,1,0:T(8,128)(2,1)S(1)} %bitcast.48), channel_id=1, source_target_pairs={{0,16},{8,24},{16,0},{24,8},{1,17},{9,25},{17,1},{25,9},{2,18},{10... | collective-permute-start | bytes 786440 | tf_op jit(solution)/shard_map/ppermute | solution.py:80
  28.0 13.9 %all-to-all-start.1 = ((bf16[8,32,384]{2,1,0:T(8,128)(2,1)}), bf16[8,32,384]{2,1,0:T(8,128)(2,1)}, u32[]{:S(2)}, u32[]{:S(2)}) async-start(bf16[8,32,384]{2,1,0:T(8,128)(2,1)} %shard_map.257), calls=%async_computation.1 | async-start | bytes 393216 | tf_op jit(solution)/shard_map/all_to_all | solution.py:63
  46.7 17.4 %collective-permute-start.11 = (bf16[2,256,512]{2,1,0:T(8,128)(2,1)}, bf16[2,256,512]{2,1,0:T(8,128)(2,1)S(1)}, u32[]{:S(2)}, u32[]{:S(2)}) collective-permute-start(bf16[2,256,512]{2,1,0:T(8,128)(2,1)} %pad_maximum_fusion.5), channel_id=1, source_target_pairs={{0,8},{8,0},{16,24},{24,16},{1,9},{9,1},{17,25},{25,17},{2,10},{10... | collective-permute-start | bytes 1572872 | tf_op jit(solution)/shard_map/ppermute | solution.py:80
  50.2 12.8 %collective-permute-start.12 = (bf16[1,160,1024]{2,1,0:T(8,128)(2,1)}, bf16[1,160,1024]{2,1,0:T(8,128)(2,1)}, u32[]{:S(2)}, u32[]{:S(2)}) collective-permute-start(bf16[1,160,1024]{2,1,0:T(8,128)(2,1)} %bitcast.15.refs_0_), channel_id=1, source_target_pairs={{0,16},{8,24},{16,0},{24,8},{1,17},{9,25},{17,1},{25,9},{2,18},{10... | collective-permute-start | bytes 983048 | tf_op jit(solution)/shard_map/ppermute | solution.py:80
  66.2 21.8 %collective-permute-start.16 = (bf16[2,160,1024]{2,1,0:T(8,128)(2,1)}, bf16[2,160,1024]{2,1,0:T(8,128)(2,1)}, u32[]{:S(2)}, u32[]{:S(2)}) collective-permute-start(bf16[2,160,1024]{2,1,0:T(8,128)(2,1)} %pad_maximum_fusion.4), channel_id=1, source_target_pairs={{0,8},{8,0},{16,24},{24,16},{1,9},{9,1},{17,25},{25,17},{2,10},{10... | collective-permute-start | bytes 1966088 | tf_op jit(solution)/shard_map/ppermute | solution.py:80
  68.9 19.1 %collective-permute-start.17 = (bf16[1,256,384]{2,1,0:T(8,128)(2,1)}, bf16[1,256,384]{2,1,0:T(8,128)(2,1)}, u32[]{:S(2)}, u32[]{:S(2)}) collective-permute-start(bf16[1,256,384]{2,1,0:T(8,128)(2,1)} %bitcast.14.refs_0_), channel_id=1, source_target_pairs={{0,16},{8,24},{16,0},{24,8},{1,17},{9,25},{17,1},{25,9},{2,18},{10... | collective-permute-start | bytes 589832 | tf_op jit(solution)/shard_map/ppermute | solution.py:80
  93.5 17.9 %collective-permute-start.22 = (bf16[2,256,384]{2,1,0:T(8,128)(2,1)S(1)}, bf16[2,256,384]{2,1,0:T(8,128)(2,1)S(1)}, u32[]{:S(2)}, u32[]{:S(2)}) collective-permute-start(bf16[2,256,384]{2,1,0:T(8,128)(2,1)S(1)} %pad_maximum_fusion.6), channel_id=1, source_target_pairs={{0,8},{8,0},{16,24},{24,16},{1,9},{9,1},{17,25},{25,17},{2,10},{10... | collective-permute-start | bytes 1179656 | tf_op jit(solution)/shard_map/ppermute | solution.py:80
  96.3 15.1 %collective-permute-start.19 = (bf16[128,1024]{1,0:T(8,128)(2,1)S(1)}, bf16[128,1024]{1,0:T(8,128)(2,1)S(1)}, u32[]{:S(2)}, u32[]{:S(2)}) collective-permute-start(bf16[128,1024]{1,0:T(8,128)(2,1)S(1)} %get-tuple-element.198), channel_id=1, source_target_pairs={{0,1},{1,0},{2,3},{3,2},{4,5},{5,4},{6,7},{7,6},{8,9},{9,8},{10,11... | collective-permute-start | bytes 786440 | tf_op jit(solution)/shard_map/ppermute | solution.py:45
  97.6 13.9 %collective-permute-start.20 = (bf16[128,1024]{1,0:T(8,128)(2,1)S(1)}, bf16[128,1024]{1,0:T(8,128)(2,1)S(1)}, u32[]{:S(2)}, u32[]{:S(2)}) collective-permute-start(bf16[128,1024]{1,0:T(8,128)(2,1)S(1)} %get-tuple-element.199), channel_id=1, source_target_pairs={{0,4},{4,0},{1,5},{5,1},{2,6},{6,2},{3,7},{7,3},{8,12},{12,8},{9,1... | collective-permute-start | bytes 786440 | tf_op jit(solution)/shard_map/ppermute | solution.py:45
  98.3 13.3 %collective-permute-start.21 = (bf16[128,1024]{1,0:T(8,128)(2,1)S(1)}, bf16[128,1024]{1,0:T(8,128)(2,1)S(1)}, u32[]{:S(2)}, u32[]{:S(2)}) collective-permute-start(bf16[128,1024]{1,0:T(8,128)(2,1)S(1)} %get-tuple-element.200), channel_id=1, source_target_pairs={{0,5},{1,4},{4,1},{5,0},{2,7},{3,6},{6,3},{7,2},{8,13},{9,12},{12,... | collective-permute-start | bytes 786440 | tf_op jit(solution)/shard_map/ppermute | solution.py:49
  114.0 12.5 %collective-permute-start.25 = (bf16[128,1024]{1,0:T(8,128)(2,1)}, bf16[128,1024]{1,0:T(8,128)(2,1)}, u32[]{:S(2)}, u32[]{:S(2)}) collective-permute-start(bf16[128,1024]{1,0:T(8,128)(2,1)} %get-tuple-element.210), channel_id=1, source_target_pairs={{0,4},{4,0},{1,5},{5,1},{2,6},{6,2},{3,7},{7,3},{8,12},{12,8},{9,1... | collective-permute-start | bytes 786440 | tf_op jit(solution)/shard_map/ppermute | solution.py:45
  118.6 19.5 %collective-permute-start.29 = (bf16[4,128,1024]{2,1,0:T(8,128)(2,1)S(1)}, bf16[4,128,1024]{2,1,0:T(8,128)(2,1)}, u32[]{:S(2)}, u32[]{:S(2)}) collective-permute-start(bf16[4,128,1024]{2,1,0:T(8,128)(2,1)S(1)} %pad_maximum_fusion.1.refs_1_.refs_0_), channel_id=1, source_target_pairs={{0,2},{2,0},{1,3},{3,1},{4,6},{6,4},{5,7},{7,5},{8,10},{10,8},{9,1... | collective-permute-start | bytes 3145736 | tf_op jit(solution)/shard_map/ppermute | solution.py:45
  143.9 14.0 %collective-permute-start.34 = (bf16[4,128,1024]{2,1,0:T(8,128)(2,1)S(1)}, bf16[4,128,1024]{2,1,0:T(8,128)(2,1)S(1)}, u32[]{:S(2)}, u32[]{:S(2)}) collective-permute-start(bf16[4,128,1024]{2,1,0:T(8,128)(2,1)S(1)} %shard_map.274), channel_id=1, source_target_pairs={{0,2},{2,0},{1,3},{3,1},{4,6},{6,4},{5,7},{7,5},{8,10},{10,8},{9,1... | collective-permute-start | bytes 3145736 | tf_op jit(solution)/shard_map/ppermute | solution.py:45
  150.8 13.3 %collective-permute-start.33 = (bf16[128,1024]{1,0:T(8,128)(2,1)S(1)}, bf16[128,1024]{1,0:T(8,128)(2,1)S(1)}, u32[]{:S(2)}, u32[]{:S(2)}) collective-permute-start(bf16[128,1024]{1,0:T(8,128)(2,1)S(1)} %get-tuple-element.229), channel_id=1, source_target_pairs={{0,5},{1,4},{4,1},{5,0},{2,7},{3,6},{6,3},{7,2},{8,13},{9,12},{12,... | collective-permute-start | bytes 786440 | tf_op jit(solution)/shard_map/ppermute | solution.py:49
  164.1 22.7 %collective-permute-start.39 = (bf16[2,256,768]{2,1,0:T(8,128)(2,1)S(1)}, bf16[2,256,768]{2,1,0:T(8,128)(2,1)S(1)}, u32[]{:S(2)}, u32[]{:S(2)}) collective-permute-start(bf16[2,256,768]{2,1,0:T(8,128)(2,1)S(1)} %get-tuple-element.246), channel_id=1, source_target_pairs={{0,8},{8,0},{16,24},{24,16},{1,9},{9,1},{17,25},{25,17},{2,10},{10... | collective-permute-start | bytes 2359304 | tf_op jit(solution)/shard_map/ppermute | solution.py:80
  167.9 11.9 %collective-permute-start.37 = (bf16[128,1024]{1,0:T(8,128)(2,1)S(1)}, bf16[128,1024]{1,0:T(8,128)(2,1)S(1)}, u32[]{:S(2)}, u32[]{:S(2)}) collective-permute-start(bf16[128,1024]{1,0:T(8,128)(2,1)S(1)} %get-tuple-element.244), channel_id=1, source_target_pairs={{0,4},{4,0},{1,5},{5,1},{2,6},{6,2},{3,7},{7,3},{8,12},{12,8},{9,1... | collective-permute-start | bytes 786440 | tf_op jit(solution)/shard_map/ppermute | solution.py:45
  170.2 16.8 %collective-permute-start.40 = (bf16[1,96,1024]{2,1,0:T(8,128)(2,1)S(1)}, bf16[1,96,1024]{2,1,0:T(8,128)(2,1)S(1)}, u32[]{:S(2)}, u32[]{:S(2)}) collective-permute-start(bf16[1,96,1024]{2,1,0:T(8,128)(2,1)S(1)} %get-tuple-element.252), channel_id=1, source_target_pairs={{0,16},{8,24},{16,0},{24,8},{1,17},{9,25},{17,1},{25,9},{2,18},{10... | collective-permute-start | bytes 589832 | tf_op jit(solution)/shard_map/ppermute | solution.py:80
  187.0 22.4 %collective-permute-start.43 = (bf16[1,256,768]{2,1,0:T(8,128)(2,1)S(1)}, bf16[1,256,768]{2,1,0:T(8,128)(2,1)S(1)}, u32[]{:S(2)}, u32[]{:S(2)}) collective-permute-start(bf16[1,256,768]{2,1,0:T(8,128)(2,1)S(1)} %get-tuple-element.266), channel_id=1, source_target_pairs={{0,16},{8,24},{16,0},{24,8},{1,17},{9,25},{17,1},{25,9},{2,18},{10... | collective-permute-start | bytes 1179656 | tf_op jit(solution)/shard_map/ppermute | solution.py:80
  189.1 20.3 %collective-permute-start.42 = (bf16[96,1024]{1,0:T(8,128)(2,1)S(1)}, bf16[96,1024]{1,0:T(8,128)(2,1)S(1)}, u32[]{:S(2)}, u32[]{:S(2)}) collective-permute-start(bf16[96,1024]{1,0:T(8,128)(2,1)S(1)} %shard_map.287), channel_id=1, source_target_pairs={{0,0},{1,4},{2,8},{3,12},{4,16},{5,20},{6,24},{7,28},{8,1},{9,5},{... | collective-permute-start | bytes 589832 | tf_op jit(solution)/shard_map/ppermute | solution.py:109
  210.1 25.9 %collective-permute-start.48 = (bf16[4,128,1024]{2,1,0:T(8,128)(2,1)}, bf16[4,128,1024]{2,1,0:T(8,128)(2,1)}, u32[]{:S(2)}, u32[]{:S(2)}) collective-permute-start(bf16[4,128,1024]{2,1,0:T(8,128)(2,1)} %shard_map.285), channel_id=1, source_target_pairs={{0,2},{2,0},{1,3},{3,1},{4,6},{6,4},{5,7},{7,5},{8,10},{10,8},{9,1... | collective-permute-start | bytes 3145736 | tf_op jit(solution)/shard_map/ppermute | solution.py:45
  217.7 15.8 %collective-permute-start.44 = (bf16[2,272,512]{2,1,0:T(8,128)(2,1)}, bf16[2,272,512]{2,1,0:T(8,128)(2,1)}, u32[]{:S(2)}, u32[]{:S(2)}) collective-permute-start(bf16[2,272,512]{2,1,0:T(8,128)(2,1)} %get-tuple-element.268), channel_id=1, source_target_pairs={{0,8},{8,0},{16,24},{24,16},{1,9},{9,1},{17,25},{25,17},{2,10},{10... | collective-permute-start | bytes 1671176 | tf_op jit(solution)/shard_map/ppermute | solution.py:80
  217.8 38.4 %all-to-all-start.3 = ((bf16[4,128,1024]{2,1,0:T(8,128)(2,1)}), bf16[4,128,1024]{2,1,0:T(8,128)(2,1)}, u32[]{:S(2)}, u32[]{:S(2)}) async-start(bf16[4,128,1024]{2,1,0:T(8,128)(2,1)} %copy-done.28), calls=%async_computation.3 | async-start | bytes 2097152 | tf_op jit(solution)/shard_map/all_to_all | solution.py:827
  224.5 16.8 %collective-permute-start.46 = (bf16[2,64,1024]{2,1,0:T(8,128)(2,1)S(1)}, bf16[2,64,1024]{2,1,0:T(8,128)(2,1)S(1)}, u32[]{:S(2)}, u32[]{:S(2)}) collective-permute-start(bf16[2,64,1024]{2,1,0:T(8,128)(2,1)S(1)} %get-tuple-element.275), channel_id=1, source_target_pairs={{0,8},{8,0},{16,24},{24,16},{1,9},{9,1},{17,25},{25,17},{2,10},{10... | collective-permute-start | bytes 786440 | tf_op jit(solution)/shard_map/ppermute | solution.py:80
  235.9 19.2 %collective-permute-start.45 = (bf16[1,272,512]{2,1,0:T(8,128)(2,1)S(1)}, bf16[1,272,512]{2,1,0:T(8,128)(2,1)S(1)}, u32[]{:S(2)}, u32[]{:S(2)}) collective-permute-start(bf16[1,272,512]{2,1,0:T(8,128)(2,1)S(1)} %get-tuple-element.272), channel_id=1, source_target_pairs={{0,16},{8,24},{16,0},{24,8},{1,17},{9,25},{17,1},{25,9},{2,18},{10... | collective-permute-start | bytes 835592 | tf_op jit(solution)/shard_map/ppermute | solution.py:80
  241.4 13.7 %collective-permute-start.47 = (bf16[1,64,1024]{2,1,0:T(8,128)(2,1)S(1)}, bf16[1,64,1024]{2,1,0:T(8,128)(2,1)S(1)}, u32[]{:S(2)}, u32[]{:S(2)}) collective-permute-start(bf16[1,64,1024]{2,1,0:T(8,128)(2,1)S(1)} %get-tuple-element.279), channel_id=1, source_target_pairs={{0,16},{8,24},{16,0},{24,8},{1,17},{9,25},{17,1},{25,9},{2,18},{10... | collective-permute-start | bytes 393224 | tf_op jit(solution)/shard_map/ppermute | solution.py:80
  256.2 21.5 %all-to-all-start.4 = ((bf16[8,40,1280]{2,1,0:T(8,128)(2,1)}), bf16[8,40,1280]{2,1,0:T(8,128)(2,1)S(1)}, u32[]{:S(2)}, u32[]{:S(2)}) async-start(bf16[8,40,1280]{2,1,0:T(8,128)(2,1)} %shard_map.293), calls=%async_computation.4 | async-start | bytes 1638400 | tf_op jit(solution)/shard_map/all_to_all | solution.py:63
  260.1 16.9 %collective-permute-start.52 = (bf16[64,1024]{1,0:T(8,128)(2,1)S(1)}, bf16[64,1024]{1,0:T(8,128)(2,1)S(1)}, u32[]{:S(2)}, u32[]{:S(2)}) collective-permute-start(bf16[64,1024]{1,0:T(8,128)(2,1)S(1)} %shard_map.295), channel_id=1, source_target_pairs={{0,0},{1,4},{2,8},{3,12},{4,16},{5,20},{6,24},{7,28},{8,1},{9,5},{... | collective-permute-start | bytes 393224 | tf_op jit(solution)/shard_map/ppermute | solution.py:109
  (91 other events, 909.3 us)
